TPU v7x, 256 devices: a whole 4x4x8 slice. The times are simulated.
256 devices in a mesh: row: 32 (over x, y, core), col: 8 (over z).
Axes of the slice: x: 4, y: 4, z: 8, core: 2. Of those that a mesh axis runs over, the one named last changes fastest.
Arguments:
- data_slab: float32 [24576, 32768], P('row', 'col'), may hold values from -4.8 to 4.8
- sketch: float32 [32768, 64], P('col'), may hold values from -0.03125 to 0.03125
Outputs:
- range_basis: float32 [24576, 64], P('row')
- projected: float32 [64, 32768], P(None, 'col')
All inputs are finite; a program needn't handle non-finite values.
Results may differ from a plain program's by a relative error of at most 0.0003.
Values sent between devices are 32-bit elements; how exact they have to be, the bound alone decides.
No kernel may reach another device: no remote copies, remote signals or barrier semaphores. Data moves between devices by JAX's collectives and lax.ppermute only.
A program may use at most 64 MiB of HBM per device.

v0:
```python
import math

import jax
import jax.numpy as jnp
from jax import lax
from jax.sharding import PartitionSpec as P


def from_partner(block, axis, stride):
    count = lax.axis_size(axis)
    route = []
    for low in range(count):
        high = low | 1 << stride
        if high != low and high < count:
            route += [(low, high), (high, low)]
    return lax.ppermute(block, axis, route)


def lower_of(gram_matrix):
    return jnp.linalg.cholesky(gram_matrix)


def gram_of(sample_rows):
    return jnp.dot(
        sample_rows.T,
        sample_rows,
        precision=lax.Precision.HIGHEST,
        preferred_element_type=jnp.float32,
    )


def solve_lower(lower_factor, right_side):
    return lax.linalg.triangular_solve(lower_factor, right_side, left_side=True, lower=True)


def body(data_slab, sketch):
    rows_dev = data_slab.shape[0]
    partial_value = jnp.dot(
        data_slab, sketch, precision=lax.Precision.HIGHEST, preferred_element_type=jnp.float32
    )
    sample_t = None
    whole_sample = lax.psum(partial_value, "col")
    sample_t = whole_sample.T
    upper_factor = lower_of(gram_of(whole_sample)).T
    for level in range(lax.axis_size("row").bit_length() - 1):
        partner = from_partner(upper_factor, "row", level)
        merged = gram_of(upper_factor) + gram_of(partner)
        upper_factor = lower_of(merged).T
    lower_factor = upper_factor.T
    local_t = solve_lower(lower_factor, sample_t)
    term = jnp.dot(
        local_t, data_slab, precision=lax.Precision.HIGHEST, preferred_element_type=jnp.float32
    )
    projected = lax.psum(term, "row")
    range_basis = local_t.T * math.sqrt(rows_dev * lax.axis_size("row"))
    return (range_basis, projected)


def solution(mesh):
    placed = (P("row", "col"), P("col", None))
    return jax.shard_map(
        body,
        mesh=mesh,
        in_specs=placed,
        out_specs=(P("row", None), P(None, "col")),
        check_vma=False,
    )
```

profile of v0, /device:TPU:1, one launch (start us, length us, event | category | flops | bytes accessed | tf_op | source)
XLA Modules:
  0.0 306.5 jit_solution(1041535637465293263)
XLA Ops:
  7.2 0.0 copy-start
  7.2 0.0 all-reduce.3.cloned.1.call-start
  7.2 1.2 copy-done
  8.4 15.5 %fusion.54 = f32[768,64]{0,1:T(8,128)} fusion(f32[768,4096]{1,0:T(8,128)} %param.3, f32[4096,64]{0,1:T(8,128)S(1)} %copy-done), kind=kOutput, calls=%fused_computation.81 | convolution fusion | flops 2415919104 | bytes 13828096 | tf_op jit(solution)/shard_map/dot_general | solution.py:38
  23.9 0.0 all-reduce.3.cloned.1.call-update
  24.0 0.0 all-reduce.5.cloned.1.call-start
  24.0 71.6 %all-reduce.3.cloned.1.call-done = f32[768,64]{0,1:T(8,128)} async-done(((f32[768,64]{0,1:T(8,128)}), f32[768,64]{0,1:T(8,128)}) %all-reduce.3.cloned.1.call-update) | async-done | bytes 196624 | tf_op jit(solution)/shard_map/psum | solution.py:42
  95.6 1.3 fusion.55
  96.9 0.1 copy.4
  97.0 5.8 %cholesky.104 = f32[64,64]{1,0:T(8,128)S(1)} custom-call(f32[64,64]{1,0:T(8,128)S(1)} %fusion.8), custom_call_target="Cholesky" | custom-call | tf_op jit(solution)/shard_map/jit(cholesky)/cholesky | solution.py:20
  102.9 0.6 compare_reduce_fusion.5
  103.5 0.7 fusion.19
  104.2 5.3 %collective-permute-start = (f32[64,64]{0,1:T(8,128)S(1)}, f32[64,64]{0,1:T(8,128)S(1)}, u32[]{:S(2)}, u32[]{:S(2)}) collective-permute-start(f32[64,64]{0,1:T(8,128)S(1)} %fusion.19), channel_id=1, source_target_pairs={{0,8},{8,0},{16,24},{24,16},{32,40},{40,32},{48,56},{56,48},{64,72... | collective-permute-start | bytes 49160 | tf_op jit(solution)/shard_map/ppermute | solution.py:16
  109.5 0.8 fusion.20
  110.3 0.0 collective-permute-done
  110.3 0.2 convolution_add_fusion.4
  110.5 0.1 copy.7
  110.6 5.8 %cholesky.115 = f32[64,64]{1,0:T(8,128)S(1)} custom-call(f32[64,64]{1,0:T(8,128)S(1)} %fusion.7), custom_call_target="Cholesky" | custom-call | tf_op jit(solution)/shard_map/jit(cholesky)/cholesky | solution.py:20
  116.5 0.6 compare_reduce_fusion.4
  117.1 0.7 fusion.21
  117.8 1.3 collective-permute-start.1
  119.1 0.8 fusion.22
  119.9 0.7 collective-permute-done.1
  120.7 0.2 convolution_add_fusion.3
  120.8 0.1 copy.10
  120.9 5.8 %cholesky.126 = f32[64,64]{1,0:T(8,128)S(1)} custom-call(f32[64,64]{1,0:T(8,128)S(1)} %fusion.6), custom_call_target="Cholesky" | custom-call | tf_op jit(solution)/shard_map/jit(cholesky)/cholesky | solution.py:20
  126.8 0.6 compare_reduce_fusion.3
  127.5 0.7 fusion.23
  128.1 3.0 collective-permute-start.2
  131.1 0.8 fusion.24
  132.0 0.7 collective-permute-done.2
  132.7 0.2 convolution_add_fusion.2
  132.9 0.1 copy.13
  133.0 5.8 %cholesky.137 = f32[64,64]{1,0:T(8,128)S(1)} custom-call(f32[64,64]{1,0:T(8,128)S(1)} %fusion.5), custom_call_target="Cholesky" | custom-call | tf_op jit(solution)/shard_map/jit(cholesky)/cholesky | solution.py:20
  138.8 0.6 compare_reduce_fusion.2
  139.5 0.7 fusion.25
  140.1 1.3 collective-permute-start.3
  141.4 0.8 fusion.26
  142.2 0.7 collective-permute-done.3
  143.0 0.2 convolution_add_fusion.1
  143.2 0.1 copy.16
  143.3 5.8 %cholesky.148 = f32[64,64]{1,0:T(8,128)S(1)} custom-call(f32[64,64]{1,0:T(8,128)S(1)} %fusion.4), custom_call_target="Cholesky" | custom-call | tf_op jit(solution)/shard_map/jit(cholesky)/cholesky | solution.py:20
  149.2 0.6 compare_reduce_fusion.1
  149.8 0.7 fusion.27
  150.5 2.8 collective-permute-start.4
  153.3 0.8 fusion.28
  154.1 0.7 collective-permute-done.4
  154.8 0.2 convolution_add_fusion
  155.0 0.1 copy.19
  155.1 5.8 %cholesky.159 = f32[64,64]{1,0:T(8,128)S(1)} custom-call(f32[64,64]{1,0:T(8,128)S(1)} %fusion.3), custom_call_target="Cholesky" | custom-call | tf_op jit(solution)/shard_map/jit(cholesky)/cholesky | solution.py:20
  161.0 0.6 compare_reduce_fusion
  161.6 0.7 fusion
  162.3 4.9 %custom-call.5 = f32[1,64,64]{1,2,0:T(8,128)S(1)} custom-call(f32[1,64,64]{2,1,0:T(8,128)S(1)} %fusion), custom_call_target="InvertDiagBlocksLowerTriangular" | custom-call | tf_op jit(solution)/shard_map/triangular_solve | solution.py:33
  167.2 1.3 fusion.1
  168.5 11.1 %fusion.56 = f32[64,4096]{1,0:T(8,128)} fusion(f32[64,768]{1,0:T(8,128)S(1)} %fusion.1, f32[768,4096]{1,0:T(8,128)} %param.3), kind=kOutput, calls=%fused_computation.83 | convolution fusion | flops 2415919104 | bytes 13828096 | tf_op jit(solution)/shard_map/dot_general | solution.py:51
  179.6 0.0 all-reduce.5.cloned.1.call-update
  179.6 0.7 multiply_bitcast_fusion
  180.3 117.1 %all-reduce.5.cloned.1.call-done = f32[64,4096]{1,0:T(8,128)} async-done(((f32[64,4096]{1,0:T(8,128)}), f32[64,4096]{1,0:T(8,128)}) %all-reduce.5.cloned.1.call-update) | async-done | bytes 1048592 | tf_op jit(solution)/shard_map/psum | solution.py:54
  297.4 2.3 copy.32
  (12 shorter events, 0.2 us)
Async XLA Ops:
  7.2 1.2 copy-start
  7.2 88.4 %all-reduce.3.cloned.1.call-start = ((), (), s32[]{:S(2)}) async-start(), calls=%async_computation | async-start | bytes 393216 | tf_op jit(solution)/shard_map/psum | solution.py:42
  24.0 273.5 %all-reduce.5.cloned.1.call-start = ((), (), s32[]{:S(2)}) async-start(), calls=%async_computation.1 | async-start | bytes 2097152 | tf_op jit(solution)/shard_map/psum | solution.py:54
  104.2 6.1 %collective-permute-start = (f32[64,64]{0,1:T(8,128)S(1)}, f32[64,64]{0,1:T(8,128)S(1)}, u32[]{:S(2)}, u32[]{:S(2)}) collective-permute-start(f32[64,64]{0,1:T(8,128)S(1)} %fusion.19), channel_id=1, source_target_pairs={{0,8},{8,0},{16,24},{24,16},{32,40},{40,32},{48,56},{56,48},{64,72... | collective-permute-start | bytes 49160 | tf_op jit(solution)/shard_map/ppermute | solution.py:16
  117.8 2.9 collective-permute-start.1
  128.1 4.5 %collective-permute-start.2 = (f32[64,64]{0,1:T(8,128)S(1)}, f32[64,64]{0,1:T(8,128)S(1)}, u32[]{:S(2)}, u32[]{:S(2)}) collective-permute-start(f32[64,64]{0,1:T(8,128)S(1)} %fusion.23), channel_id=1, source_target_pairs={{0,32},{32,0},{8,40},{40,8},{16,48},{48,16},{24,56},{56,24},{64,96... | collective-permute-start | bytes 49160 | tf_op jit(solution)/shard_map/ppermute | solution.py:16
  140.1 2.9 collective-permute-start.3
  150.5 4.4 %collective-permute-start.4 = (f32[64,64]{0,1:T(8,128)S(1)}, f32[64,64]{0,1:T(8,128)S(1)}, u32[]{:S(2)}, u32[]{:S(2)}) collective-permute-start(f32[64,64]{0,1:T(8,128)S(1)} %fusion.27), channel_id=1, source_target_pairs={{0,128},{128,0},{8,136},{136,8},{16,144},{144,16},{24,152},{152,24... | collective-permute-start | bytes 49160 | tf_op jit(solution)/shard_map/ppermute | solution.py:16
Sparse Core Ops, SparseCore 0:
  24.1 71.4 all-reduce.2
  179.7 117.6 all-reduce.4
where the time goes:
time: 307 us
  waiting for transfers between devices  192 us (63%)
  other arithmetic  48.7 us (16%)
  matrix products  34.3 us (11%)
  between operations  14.3 us (5%)
  starting transfers between devices  13.7 us (4%)
  local copies, waits for them, and re-layouts  3.89 us (1%)
    psum x1, waiting for transfers between devices, body(): projected = lax.psum(term, 'row')  117 us
    psum x1, waiting for transfers between devices, body(): whole_sample = lax.psum(partial_value, 'col')  71.6 us
    another operation x18, other arithmetic, lower_of(): return jnp.linalg.cholesky(gram_matrix)  39.1 us
    dot_general x1, matrix products, body(): jnp.dot(data_slab, sketch, precision=lax.Precision.HIGHEST, preferred_ele...  15.5 us
    ppermute x5, starting transfers between devices, from_partner(): return lax.ppermute(block, axis, route)  13.6 us
    dot_general x1, matrix products, body(): jnp.dot(local_t, data_slab, precision=lax.Precision.HIGHEST, preferred_el...  11.1 us
    dot_general x11, matrix products, gram_of(): jnp.dot(sample_rows.T, sample_rows, precision=lax.Precision.HIGHEST, pref...  6.4 us
  transfers between devices with their start and end apart: 7, of which 6 were waited for; matrix products, arithmetic and copies ran while one was open for 2% of the time, Pallas kernels for 0%

commit v1 on v0

v1 whole, which is shorter than its diff:
```python
import functools
import math

import jax
import jax.numpy as jnp
from jax import lax
from jax.experimental import pallas as pl
from jax.experimental.pallas import tpu as pltpu
from jax.sharding import PartitionSpec as P

F32 = jnp.float32
BF16 = jnp.bfloat16
VMEM = pltpu.VMEM
K = 64
LANES = 128
QUARTERS = 4
BLOCKS = 32
GROUPS = 8
PER_GROUP = 4


def split(value):
    high = value.astype(BF16)
    return high, (value - high.astype(F32)).astype(BF16)


def own_quarter():
    z = lax.axis_index("col")
    return jnp.where(z < QUARTERS, z, 2 * QUARTERS - 1 - z)


def position():
    row = lax.axis_index("row")
    core, y, x = row % 2, (row // 2) % 4, row // 8
    return core, jnp.where(core == 0, x, y), jnp.where(core == 0, y, x)


def group_place(group):
    core, first, second = position()
    if group < PER_GROUP:
        return core * PER_GROUP + (first ^ group), second
    return (1 - core) * PER_GROUP + (second ^ (group - PER_GROUP)), first


def sample_kernel(data_ref, sketch_ref, *refs):
    outs, (data, sketch, weights, sems) = refs[:QUARTERS], refs[QUARTERS:]
    rows = data.shape[1]
    mine = own_quarter()
    load = pltpu.make_async_copy(sketch_ref, sketch, sems.at[QUARTERS])
    load.start()
    order = (3, 2, 1, 0)
    copies = {}
    for j in order:
        start = pl.multiple_of((mine ^ j) * rows, rows)
        copies[j] = pltpu.make_async_copy(data_ref.at[pl.ds(start, rows)], data.at[j], sems.at[j])
        copies[j].start()
    load.wait()
    high, low = split(sketch[...])
    weights[...] = jnp.concatenate([high, low], axis=1)
    lane = lax.broadcasted_iota(jnp.int32, (rows // 2, LANES), 1)
    for j in order:
        copies[j].wait()
        high, low = split(data[j])
        total = jnp.dot(high, weights[...], preferred_element_type=F32)
        total += jnp.dot(low, weights[...], preferred_element_type=F32)
        total += pltpu.roll(total, K, axis=1)
        outs[j][...] = jnp.where(lane < K, total[: rows // 2], total[rows // 2 :])


def partial_sample(data_slab, sketch):
    rows, columns = data_slab.shape
    quarter = rows // QUARTERS
    return pl.pallas_call(
        sample_kernel,
        out_shape=[jax.ShapeDtypeStruct((quarter // 2, LANES), F32)] * QUARTERS,
        in_specs=[pl.BlockSpec(memory_space=pl.ANY)] * 2,
        out_specs=[pl.BlockSpec(memory_space=VMEM)] * QUARTERS,
        scratch_shapes=[
            VMEM((QUARTERS, quarter, columns), F32),
            VMEM((columns, K), F32),
            VMEM((columns, LANES), BF16),
            pltpu.SemaphoreType.DMA((QUARTERS + 1,)),
        ],
        compiler_params=pltpu.CompilerParams(vmem_limit_bytes=40 * 2**20),
        cost_estimate=pl.CostEstimate(flops=8 * rows * columns * K, bytes_accessed=4 * rows * columns, transcendentals=0),
    )(data_slab, sketch)


def term_kernel(s0, s1, s2, s3, data_ref, keep_ref, send_ref, data, sample, sems):
    groups, rows, width = data.shape
    quarter = rows // QUARTERS
    half = quarter // 2
    mine = own_quarter()
    order = (4, 5, 6, 7, 0, 1, 2, 3)
    copies = {}
    for g in order:
        place, _ = group_place(g)
        start = pl.multiple_of(place * width, width)
        copies[g] = pltpu.make_async_copy(data_ref.at[:, pl.ds(start, width)], data.at[g], sems.at[g])
        copies[g].start()
    for j, ref in enumerate((s0, s1, s2, s3)):
        start = pl.multiple_of((mine ^ j) * quarter, quarter)
        sample[pl.ds(start, half), :] = ref[:, :K]
        sample[pl.ds(start + half, half), :] = ref[:, K:]
    high, low = split(sample[...].T)
    left = jnp.concatenate([high, low], axis=0)
    gram = lax.dot_general(left, left, (((1,), (1,)), ((), ())), preferred_element_type=F32)
    gram = gram[:K] + gram[K:]
    gram = gram + pltpu.roll(gram, K, axis=1)
    keep_ref[BLOCKS // 2] = gram
    send_ref[BLOCKS // 2] = gram
    for g in order:
        copies[g].wait()
        _, mask = group_place(g)
        high, low = split(data[g])
        total = jnp.dot(left, high, preferred_element_type=F32)
        total += jnp.dot(left, low, preferred_element_type=F32)
        total = total[:K] + total[K:]
        out_ref, base = (keep_ref, g * PER_GROUP) if g < PER_GROUP else (send_ref, (g - PER_GROUP) * PER_GROUP)
        for t in range(PER_GROUP):
            out_ref[base + (mask ^ t)] = total[:, t * LANES : (t + 1) * LANES]


def partial_terms(quarters, data_slab):
    rows, columns = data_slab.shape
    width = columns // GROUPS
    return pl.pallas_call(
        term_kernel,
        out_shape=[jax.ShapeDtypeStruct((BLOCKS // 2 + 1, K, LANES), F32)] * 2,
        in_specs=[pl.BlockSpec(memory_space=VMEM)] * QUARTERS + [pl.BlockSpec(memory_space=pl.ANY)],
        out_specs=[pl.BlockSpec(memory_space=VMEM)] * 2,
        scratch_shapes=[
            VMEM((GROUPS, rows, width), F32),
            VMEM((rows, K), F32),
            pltpu.SemaphoreType.DMA((GROUPS,)),
        ],
        compiler_params=pltpu.CompilerParams(vmem_limit_bytes=40 * 2**20),
        cost_estimate=pl.CostEstimate(flops=8 * rows * columns * K, bytes_accessed=4 * rows * columns, transcendentals=0),
    )(*quarters, data_slab)


def basis_kernel(scale, gram_ref, s0, s1, s2, s3, inverse_ref, basis_ref):
    lane = lax.broadcasted_iota(jnp.int32, (K, LANES), 1)
    row = lax.broadcasted_iota(jnp.int32, (K, LANES), 0)
    work = jnp.where(lane < K, gram_ref[...], jnp.where(lane == row + K, 1.0, 0.0))
    parts = [work[8 * i : 8 * i + 8] for i in range(K // 8)]
    sub = lax.broadcasted_iota(jnp.int32, (8, 1), 0)
    pivots = []
    for j in range(K):
        block, at = divmod(j, 8)
        line = parts[block][at : at + 1]
        pivot = line[:, j : j + 1]
        pivots.append(pivot)
        scaled = line * (1.0 / pivot)
        for i in range(block, K // 8):
            factor = parts[i][:, j : j + 1]
            if i == block:
                factor = jnp.where(sub > at, factor, 0.0)
            parts[i] = parts[i] - factor * scaled
    for i in range(K // 8):
        diagonal = jnp.concatenate(pivots[8 * i : 8 * i + 8], axis=0)
        parts[i] = parts[i] * (1.0 / jnp.sqrt(diagonal))
    inverse = jnp.concatenate(parts, axis=0)[:, K:]
    inverse_ref[...] = inverse
    mine = own_quarter()
    half = s0.shape[0]
    for j, ref in enumerate((s0, s1, s2, s3)):
        start = pl.multiple_of((mine ^ j) * 2 * half, 2 * half)
        for side in range(2):
            product = lax.dot_general(
                ref[:, side * K : (side + 1) * K],
                inverse * scale,
                (((1,), (1,)), ((), ())),
                precision=lax.Precision.HIGHEST,
                preferred_element_type=F32,
            )
            basis_ref[pl.ds(start + side * half, half), :] = product


def basis_of(gram, quarters, rows, scale):
    return pl.pallas_call(
        functools.partial(basis_kernel, scale),
        out_shape=[jax.ShapeDtypeStruct((K, K), F32), jax.ShapeDtypeStruct((rows, K), F32)],
        in_specs=[pl.BlockSpec(memory_space=VMEM)] * (1 + QUARTERS),
        out_specs=[pl.BlockSpec(memory_space=VMEM)] * 2,
        cost_estimate=pl.CostEstimate(flops=12 * rows * K * K, bytes_accessed=8 * rows * K, transcendentals=K),
    )(gram, *quarters)


def apply_kernel(inverse_ref, own_ref, other_ref, out_ref):
    high, low = split(inverse_ref[...])
    left = jnp.concatenate([high, low, high], axis=1)
    width = PER_GROUP * LANES
    for g in range(GROUPS):
        ref = own_ref if g < PER_GROUP else other_ref
        base = (g % PER_GROUP) * PER_GROUP
        place, mask = group_place(g)
        value = jnp.concatenate([ref[base + t] for t in range(PER_GROUP)], axis=1)
        high, low = split(value)
        right = jnp.concatenate([high, high, low], axis=0)
        total = jnp.dot(left, right, preferred_element_type=F32)
        for t in range(PER_GROUP):
            start = pl.multiple_of(place * width + (mask ^ t) * LANES, LANES)
            out_ref[:, pl.ds(start, LANES)] = total[:, t * LANES : (t + 1) * LANES]


def applied(inverse, own, other):
    columns = BLOCKS * LANES
    return pl.pallas_call(
        apply_kernel,
        out_shape=jax.ShapeDtypeStruct((K, columns), F32),
        in_specs=[pl.BlockSpec(memory_space=VMEM)] * 3,
        out_specs=pl.BlockSpec(memory_space=VMEM),
        cost_estimate=pl.CostEstimate(flops=6 * columns * K * K, bytes_accessed=8 * columns * K, transcendentals=0),
    )(inverse, own, other)


def along_col(value, mask):
    return lax.ppermute(value, "col", [(i, i ^ mask) for i in range(8)])


def along_row(value, masks):
    return lax.ppermute(value, "row", [(i, i ^ masks[i % 2]) for i in range(32)])


CORE = (1, 1)
FIRST = [(t << 3, t << 1) for t in range(4)]
SECOND = [(t << 1, t << 3) for t in range(4)]


def body(data_slab, sketch):
    rows = data_slab.shape[0]
    parts = partial_sample(data_slab, sketch)
    owned = parts[0] + along_col(parts[1], 1) + along_col(parts[2], 2) + along_col(parts[3], 3)
    owned = owned + along_col(owned, 7)
    quarters = [owned] + [along_col(owned, t) for t in (1, 2, 3)]

    keep, send = partial_terms(quarters, data_slab)
    total = keep + along_row(send, CORE)
    gram = total[16:]
    got = [along_row(jnp.concatenate([total[4 * t : 4 * t + 4], gram]), FIRST[t]) for t in (1, 2, 3)]
    total = jnp.concatenate([total[:4], gram]) + got[0] + got[1] + got[2]
    gram = total[4:]
    got = [along_row(jnp.concatenate([total[t : t + 1], gram]), SECOND[t]) for t in (1, 2, 3)]
    total = jnp.concatenate([total[:1], gram]) + got[0] + got[1] + got[2]

    inverse, range_basis = basis_of(total[1], quarters, rows, math.sqrt(rows * lax.axis_size("row")))

    block = total[:1]
    row_of = jnp.concatenate([block] + [along_row(block, SECOND[t]) for t in (1, 2, 3)])
    own = jnp.concatenate([row_of] + [along_row(row_of, FIRST[t]) for t in (1, 2, 3)])
    other = along_row(own, CORE)
    return range_basis, applied(inverse, own, other)


def solution(mesh):
    placed = (P("row", "col"), P("col", None))
    return jax.shard_map(
        body,
        mesh=mesh,
        in_specs=placed,
        out_specs=(P("row", None), P(None, "col")),
        check_vma=False,
    )
```

time: 307 us -> 99.1 us (0.32)
  waiting for transfers between devices: 192 us -> 26 us
  other arithmetic: 48.7 us -> 0.18 us
  matrix products: 34.3 us -> 0 us
  starting transfers between devices: 13.7 us -> 38.7 us
  Pallas kernels: 0 us -> 23.3 us
  between operations: 14.3 us -> 0.82 us
  local copies, waits for them, and re-layouts: 3.89 us -> 9.79 us
    psum x2 -> x0, waiting for transfers between devices: 189 us -> none  [the longest x1 117 us: body(): projected = lax.psum(term, 'row')]
    another operation x20 -> x0, other arithmetic: 44.7 us -> none  [the longest x18 39.1 us: lower_of(): return jnp.linalg.cholesky(gram_matrix)]
    dot_general x13 -> x0, matrix products: 33 us -> none  [the longest x1 15.5 us: body(): jnp.dot(data_slab, sketch, precision=lax.Precision.HIGHEST, preferred_ele...]
    ppermute x5 -> x21, starting transfers between devices: 13.6 us -> 38.7 us  [the longest x14 26.3 us: along_row(): lax.ppermute(value, 'row', [(i, i ^ masks[i % 2]) for i in range(32)])]
    pallas_call x0 -> x4, Pallas kernels: none -> 23.3 us  [the longest x1 7.63 us: basis_of(): pl.pallas_call(functools.partial(basis_kernel, scale), out_shape=[jax.Sha...]
    ppermute x5 -> x21, waiting for transfers between devices: 2.92 us -> 26 us  [the longest x14 17.1 us: along_row(): lax.ppermute(value, 'row', [(i, i ^ masks[i % 2]) for i in range(32)])]
    unnamed x3 -> x21, local copies, waits for them, and re-layouts: 3.45 us -> 9.09 us
    transpose x5 -> x0, other arithmetic: 3.26 us -> none  [the longest x4 2.61 us: body(): upper_factor = lower_of(merged).T]
  transfers between devices with their start and end apart: 7 -> 21, of which waited for: 6 -> 17; matrix products, arithmetic and copies ran while one was open for 2% -> 2% of each run, Pallas kernels for 0% -> 8%
where the time goes in v1:
time: 99.1 us; the launch traced here: 98.8 us
  starting transfers between devices  38.7 us (39%)
  waiting for transfers between devices  26 us (26%)
  Pallas kernels  23.3 us (24%)
  local copies, waits for them, and re-layouts  9.79 us (10%)
    ppermute x14, starting transfers between devices, along_row(): lax.ppermute(value, 'row', [(i, i ^ masks[i % 2]) for i in range(32)])  26.3 us
    ppermute x14, waiting for transfers between devices, along_row(): lax.ppermute(value, 'row', [(i, i ^ masks[i % 2]) for i in range(32)])  17.1 us
    ppermute x7, starting transfers between devices, along_col(): return lax.ppermute(value, 'col', [(i, i ^ mask) for i in range(8)])  12.4 us
    unnamed x21, local copies, waits for them, and re-layouts  9.09 us
    ppermute x7, waiting for transfers between devices, along_col(): return lax.ppermute(value, 'col', [(i, i ^ mask) for i in range(8)])  8.91 us
    pallas_call x1, Pallas kernels, basis_of(): pl.pallas_call(functools.partial(basis_kernel, scale), out_shape=[jax.Sha...  7.63 us
    pallas_call x1, Pallas kernels, partial_terms(): pl.pallas_call(term_kernel, out_shape=[jax.ShapeDtypeStruct((BLOCKS // 2...  6.7 us
    pallas_call x1, Pallas kernels, partial_sample(): pl.pallas_call(sample_kernel, out_shape=[jax.ShapeDtypeStruct((quarter //...  6.31 us
  transfers between devices with their start and end apart: 21, of which 17 were waited for; matrix products, arithmetic and copies ran while one was open for 2% of the time, Pallas kernels for 8%

profile of v1, /device:TPU:1, one launch (start us, length us, event | category | flops | bytes accessed | tf_op | source)
XLA Modules:
  0.0 98.8 jit_solution(16383088755884573284)
XLA Ops:
  0.6 1.8 %copy.4.sketch_ref = f32[4096,64]{1,0:T(8,128)S(1)} copy(f32[4096,64]{0,1:T(8,128)} %param.3) | data formatting | bytes 2097152 | tf_op args[1]
  2.5 6.3 %shard_map.41 = (f32[96,128]{1,0:T(8,128)S(1)}, f32[96,128]{1,0:T(8,128)S(1)}, f32[96,128]{1,0:T(8,128)S(1)}, f32[96,128]{1,0:T(8,128)S(1)}) custom-call(f32[768,4096]{1,0:T(8,128)} %data_ref.3, f32[4096,64]{1,0:T(8,128)S(1)} %copy.4.sketch_ref), custom_call_target="tpu_custom_call" | custom-call | flops 1610612736 | bytes 12582912 | tf_op jit(solution)/shard_map/pallas_call | solution.py:73
  8.8 2.6 %collective-permute-start = (f32[96,128]{1,0:T(8,128)S(1)}, f32[96,128]{1,0:T(8,128)S(1)}, u32[]{:S(2)}, u32[]{:S(2)}) collective-permute-start(f32[96,128]{1,0:T(8,128)S(1)} %get-tuple-element.11), channel_id=1, source_target_pairs={{0,1},{1,0},{2,3},{3,2},{4,5},{5,4},{6,7},{7,6},{8,9},{9,8},{10,11... | collective-permute-start | bytes 147464 | tf_op jit(solution)/shard_map/ppermute | solution.py:219
  11.3 3.0 %collective-permute-start.1 = (f32[96,128]{1,0:T(8,128)S(1)}, f32[96,128]{1,0:T(8,128)S(1)}, u32[]{:S(2)}, u32[]{:S(2)}) collective-permute-start(f32[96,128]{1,0:T(8,128)S(1)} %get-tuple-element.12), channel_id=1, source_target_pairs={{0,2},{1,3},{2,0},{3,1},{4,6},{5,7},{6,4},{7,5},{8,10},{9,11},{10,... | collective-permute-start | bytes 147464 | tf_op jit(solution)/shard_map/ppermute | solution.py:219
  14.3 0.0 collective-permute-start.2
  14.3 0.0 collective-permute-done
  14.3 2.0 %collective-permute-done.1 = f32[96,128]{1,0:T(8,128)S(1)} collective-permute-done((f32[96,128]{1,0:T(8,128)S(1)}, f32[96,128]{1,0:T(8,128)S(1)}, u32[]{:S(2)}, u32[]{:S(2)}) %collective-permute-start.1) | collective-permute-done | bytes 49184 | tf_op jit(solution)/shard_map/ppermute | solution.py:219
  16.3 2.7 %collective-permute-done.2 = f32[96,128]{1,0:T(8,128)S(1)} collective-permute-done((f32[96,128]{1,0:T(8,128)S(1)}, f32[96,128]{1,0:T(8,128)S(1)}, u32[]{:S(2)}, u32[]{:S(2)}) %collective-permute-start.2) | collective-permute-done | bytes 49184 | tf_op jit(solution)/shard_map/ppermute | solution.py:219
  19.1 3.3 %collective-permute-start.3 = (f32[96,128]{1,0:T(8,128)S(1)}, f32[96,128]{1,0:T(8,128)S(1)}, u32[]{:S(2)}, u32[]{:S(2)}) collective-permute-start(f32[96,128]{1,0:T(8,128)S(1)} %add_add_fusion), channel_id=1, source_target_pairs={{0,7},{1,6},{2,5},{3,4},{4,3},{5,2},{6,1},{7,0},{8,15},{9,14},{10,... | collective-permute-start | bytes 147464 | tf_op jit(solution)/shard_map/ppermute | solution.py:219
  22.3 1.9 %collective-permute-done.3 = f32[96,128]{1,0:T(8,128)S(1)} collective-permute-done((f32[96,128]{1,0:T(8,128)S(1)}, f32[96,128]{1,0:T(8,128)S(1)}, u32[]{:S(2)}, u32[]{:S(2)}) %collective-permute-start.3) | collective-permute-done | bytes 49184 | tf_op jit(solution)/shard_map/ppermute | solution.py:219
  24.3 0.0 copy-start.1
  24.3 1.3 %collective-permute-start.6 = (f32[96,128]{1,0:T(8,128)S(1)}, f32[96,128]{1,0:T(8,128)S(1)}, u32[]{:S(2)}, u32[]{:S(2)}) collective-permute-start(f32[96,128]{1,0:T(8,128)S(1)} %add.36.s0), channel_id=1, source_target_pairs={{0,3},{1,2},{2,1},{3,0},{4,7},{5,6},{6,5},{7,4},{8,11},{9,10},{10,... | collective-permute-start | bytes 147464 | tf_op jit(solution)/shard_map/ppermute | solution.py:219
  25.5 0.9 collective-permute-start.5
  26.4 1.5 %collective-permute-start.4 = (f32[96,128]{1,0:T(8,128)S(1)}, f32[96,128]{1,0:T(8,128)S(1)}, u32[]{:S(2)}, u32[]{:S(2)}) collective-permute-start(f32[96,128]{1,0:T(8,128)S(1)} %add.36.s0), channel_id=1, source_target_pairs={{0,1},{1,0},{2,3},{3,2},{4,5},{5,4},{6,7},{7,6},{8,9},{9,8},{10,11... | collective-permute-start | bytes 147464 | tf_op jit(solution)/shard_map/ppermute | solution.py:219
  27.9 1.2 %collective-permute-done.6.s3 = f32[96,128]{1,0:T(8,128)S(1)} collective-permute-done((f32[96,128]{1,0:T(8,128)S(1)}, f32[96,128]{1,0:T(8,128)S(1)}, u32[]{:S(2)}, u32[]{:S(2)}) %collective-permute-start.6) | collective-permute-done | bytes 49184 | tf_op jit(solution)/shard_map/ppermute | solution.py:219
  29.1 0.0 copy-start.2
  29.1 1.0 %collective-permute-done.5.s2 = f32[96,128]{1,0:T(8,128)S(1)} collective-permute-done((f32[96,128]{1,0:T(8,128)S(1)}, f32[96,128]{1,0:T(8,128)S(1)}, u32[]{:S(2)}, u32[]{:S(2)}) %collective-permute-start.5) | collective-permute-done | bytes 49184 | tf_op jit(solution)/shard_map/ppermute | solution.py:219
  30.2 0.0 copy-start.3
  30.2 0.0 collective-permute-done.4.s1
  30.2 0.0 copy-start
  30.2 4.6 %copy-done = f32[768,4096]{1,0:T(8,128)S(1)} copy-done((f32[768,4096]{1,0:T(8,128)S(1)}, f32[768,4096]{1,0:T(8,128)}, u32[]{:S(2)}) %copy-start) | copy-done | bytes 12582936
  34.8 0.0 copy-start.4
  34.8 6.7 %shard_map.42 = (f32[17,64,128]{2,1,0:T(8,128)S(1)}, f32[17,64,128]{2,1,0:T(8,128)S(1)}) custom-call(f32[96,128]{1,0:T(8,128)S(1)} %add.36.s0, f32[96,128]{1,0:T(8,128)S(1)} %collective-permute-done.4.s1, f32[96,128]{1,0:T(8,128)S(1)} %collective-permute-done.5.s2, f32[96,128]{1,0:T(8,128)S(1)} %collective-permute-done.6.s3, f32[768,4096]{1,0:T(8,128)S(1)} %copy-done), custom_call_target="tpu_custom_call" | custom-call | flops 1610612736 | bytes 12582912 | tf_op jit(solution)/shard_map/pallas_call | solution.py:127
  41.5 4.8 %collective-permute-start.7 = (f32[17,64,128]{2,1,0:T(8,128)S(1)}, f32[17,64,128]{2,1,0:T(8,128)S(1)}, u32[]{:S(2)}, u32[]{:S(2)}) collective-permute-start(f32[17,64,128]{2,1,0:T(8,128)S(1)} %get-tuple-element.15), channel_id=1, source_target_pairs={{0,8},{8,0},{16,24},{24,16},{32,40},{40,32},{48,56},{56,48},{64,72... | collective-permute-start | bytes 1671176 | tf_op jit(solution)/shard_map/ppermute | solution.py:223
  46.3 1.6 %collective-permute-done.7 = f32[17,64,128]{2,1,0:T(8,128)S(1)} collective-permute-done((f32[17,64,128]{2,1,0:T(8,128)S(1)}, f32[17,64,128]{2,1,0:T(8,128)S(1)}, u32[]{:S(2)}, u32[]{:S(2)}) %collective-permute-start.7) | collective-permute-done | bytes 557088 | tf_op jit(solution)/shard_map/ppermute | solution.py:223
  47.8 0.1 add.37
  48.0 2.8 %collective-permute-start.10 = (f32[5,64,128]{2,1,0:T(8,128)S(1)}, f32[5,64,128]{2,1,0:T(8,128)S(1)}, u32[]{:S(2)}, u32[]{:S(2)}) collective-permute-start(f32[5,64,128]{2,1,0:T(8,128)S(1)} %concatenate.41), channel_id=1, source_target_pairs={{0,192},{8,56},{16,208},{24,40},{32,224},{40,24},{48,240},{56,8},{... | collective-permute-start | bytes 491528 | tf_op jit(solution)/shard_map/ppermute | solution.py:223
  50.9 0.1 collective-permute-start.8
  51.0 1.2 %collective-permute-start.9 = (f32[5,64,128]{2,1,0:T(8,128)S(1)}, f32[5,64,128]{2,1,0:T(8,128)S(1)}, u32[]{:S(2)}, u32[]{:S(2)}) collective-permute-start(f32[5,64,128]{2,1,0:T(8,128)S(1)} %get-tuple-element.33), channel_id=1, source_target_pairs={{0,128},{8,40},{16,144},{24,56},{32,160},{40,8},{48,176},{56,24},{... | collective-permute-start | bytes 491528 | tf_op jit(solution)/shard_map/ppermute | solution.py:223
  52.1 1.7 %collective-permute-done.10 = f32[5,64,128]{2,1,0:T(8,128)S(1)} collective-permute-done((f32[5,64,128]{2,1,0:T(8,128)S(1)}, f32[5,64,128]{2,1,0:T(8,128)S(1)}, u32[]{:S(2)}, u32[]{:S(2)}) %collective-permute-start.10) | collective-permute-done | bytes 163872 | tf_op jit(solution)/shard_map/ppermute | solution.py:223
  53.8 1.6 %collective-permute-done.8 = f32[5,64,128]{2,1,0:T(8,128)S(1)} collective-permute-done((f32[5,64,128]{2,1,0:T(8,128)S(1)}, f32[5,64,128]{2,1,0:T(8,128)S(1)}, u32[]{:S(2)}, u32[]{:S(2)}) %collective-permute-start.8) | collective-permute-done | bytes 163872 | tf_op jit(solution)/shard_map/ppermute | solution.py:223
  55.4 1.6 %collective-permute-done.9 = f32[5,64,128]{2,1,0:T(8,128)S(1)} collective-permute-done((f32[5,64,128]{2,1,0:T(8,128)S(1)}, f32[5,64,128]{2,1,0:T(8,128)S(1)}, u32[]{:S(2)}, u32[]{:S(2)}) %collective-permute-start.9) | collective-permute-done | bytes 163872 | tf_op jit(solution)/shard_map/ppermute | solution.py:223
  57.1 2.6 %collective-permute-start.13 = (f32[2,64,128]{2,1,0:T(8,128)S(1)}, f32[2,64,128]{2,1,0:T(8,128)S(1)}, u32[]{:S(2)}, u32[]{:S(2)}) collective-permute-start(f32[2,64,128]{2,1,0:T(8,128)S(1)} %concatenate.42), channel_id=1, source_target_pairs={{0,48},{8,200},{16,32},{24,216},{32,16},{40,232},{48,0},{56,248},{... | collective-permute-start | bytes 196616 | tf_op jit(solution)/shard_map/ppermute | solution.py:223
  59.7 0.1 collective-permute-start.11
  59.8 1.4 %collective-permute-start.12 = (f32[2,64,128]{2,1,0:T(8,128)S(1)}, f32[2,64,128]{2,1,0:T(8,128)S(1)}, u32[]{:S(2)}, u32[]{:S(2)}) collective-permute-start(f32[2,64,128]{2,1,0:T(8,128)S(1)} %get-tuple-element.31), channel_id=1, source_target_pairs={{0,32},{8,136},{16,48},{24,152},{32,0},{40,168},{48,16},{56,184},{... | collective-permute-start | bytes 196616 | tf_op jit(solution)/shard_map/ppermute | solution.py:223
  61.1 0.4 collective-permute-done.13
  61.5 1.7 %collective-permute-done.11 = f32[2,64,128]{2,1,0:T(8,128)S(1)} collective-permute-done((f32[2,64,128]{2,1,0:T(8,128)S(1)}, f32[2,64,128]{2,1,0:T(8,128)S(1)}, u32[]{:S(2)}, u32[]{:S(2)}) %collective-permute-start.11) | collective-permute-done | bytes 65568 | tf_op jit(solution)/shard_map/ppermute | solution.py:223
  63.2 1.3 %collective-permute-done.12 = f32[2,64,128]{2,1,0:T(8,128)S(1)} collective-permute-done((f32[2,64,128]{2,1,0:T(8,128)S(1)}, f32[2,64,128]{2,1,0:T(8,128)S(1)}, u32[]{:S(2)}, u32[]{:S(2)}) %collective-permute-start.12) | collective-permute-done | bytes 65568 | tf_op jit(solution)/shard_map/ppermute | solution.py:223
  64.5 0.6 fusion.8
  65.1 1.5 %collective-permute-start.16 = (f32[1,64,128]{2,1,0:T(8,128)S(1)}, f32[1,64,128]{2,1,0:T(8,128)S(1)}, u32[]{:S(2)}, u32[]{:S(2)}) collective-permute-start(f32[1,64,128]{2,1,0:T(8,128)S(1)} %get-tuple-element.27), channel_id=1, source_target_pairs={{0,48},{8,200},{16,32},{24,216},{32,16},{40,232},{48,0},{56,248},{... | collective-permute-start | bytes 98312 | tf_op jit(solution)/shard_map/ppermute | solution.py:223
  66.6 1.7 %collective-permute-start.15 = (f32[1,64,128]{2,1,0:T(8,128)S(1)}, f32[1,64,128]{2,1,0:T(8,128)S(1)}, u32[]{:S(2)}, u32[]{:S(2)}) collective-permute-start(f32[1,64,128]{2,1,0:T(8,128)S(1)} %get-tuple-element.27), channel_id=1, source_target_pairs={{0,32},{8,136},{16,48},{24,152},{32,0},{40,168},{48,16},{56,184},{... | collective-permute-start | bytes 98312 | tf_op jit(solution)/shard_map/ppermute | solution.py:223
  68.3 0.1 collective-permute-start.14
  68.4 0.7 collective-permute-done.16
  69.1 1.8 %collective-permute-done.15 = f32[1,64,128]{2,1,0:T(8,128)S(1)} collective-permute-done((f32[1,64,128]{2,1,0:T(8,128)S(1)}, f32[1,64,128]{2,1,0:T(8,128)S(1)}, u32[]{:S(2)}, u32[]{:S(2)}) %collective-permute-start.15) | collective-permute-done | bytes 32800 | tf_op jit(solution)/shard_map/ppermute | solution.py:223
  70.9 0.2 collective-permute-done.14
  71.0 2.9 %collective-permute-start.19 = (f32[4,64,128]{2,1,0:T(8,128)S(1)}, f32[4,64,128]{2,1,0:T(8,128)S(1)}, u32[]{:S(2)}, u32[]{:S(2)}) collective-permute-start(f32[4,64,128]{2,1,0:T(8,128)S(1)} %pad_maximum_fusion.3), channel_id=1, source_target_pairs={{0,192},{8,56},{16,208},{24,40},{32,224},{40,24},{48,240},{56,8},{... | collective-permute-start | bytes 393224 | tf_op jit(solution)/shard_map/ppermute | solution.py:223
  74.0 0.3 collective-permute-start.18
  74.3 0.4 collective-permute-start.17
  74.7 3.8 %collective-permute-done.17 = f32[4,64,128]{2,1,0:T(8,128)S(1)} collective-permute-done((f32[4,64,128]{2,1,0:T(8,128)S(1)}, f32[4,64,128]{2,1,0:T(8,128)S(1)}, u32[]{:S(2)}, u32[]{:S(2)}) %collective-permute-start.17) | collective-permute-done | bytes 131104 | tf_op jit(solution)/shard_map/ppermute | solution.py:223
  78.5 0.8 collective-permute-done.18
  79.3 0.0 collective-permute-done.19
  79.3 0.0 copy-start.5
  79.3 6.5 %collective-permute-start.20 = (f32[16,64,128]{2,1,0:T(8,128)S(1)}, f32[16,64,128]{2,1,0:T(8,128)S(1)}, u32[]{:S(2)}, u32[]{:S(2)}) collective-permute-start(f32[16,64,128]{2,1,0:T(8,128)S(1)} %constant_dynamic-update-slice_fusion.own_ref), channel_id=1, source_target_pairs={{0,8},{8,0},{16,24},{24,16},{32,40},{40,32},{48,56},{56,48},{64,72... | collective-permute-start | bytes 1572872 | tf_op jit(solution)/shard_map/ppermute | solution.py:223
  85.8 0.0 copy-done.1
  85.9 0.0 copy-done.2
  85.9 0.0 copy-done.3
  85.9 0.0 copy-done.4
  85.9 7.6 %shard_map.43 = (f32[64,64]{1,0:T(8,128)}, f32[768,64]{1,0:T(8,128)}) custom-call(f32[64,128]{1,0:T(8,128)} %get-tuple-element.29.gram_ref, f32[96,128]{1,0:T(8,128)} %copy-done.1, f32[96,128]{1,0:T(8,128)} %copy-done.4, f32[96,128]{1,0:T(8,128)} %copy-done.3, f32[96,128]{1,0:T(8,128)} %copy-done.2), custom_call_target="tpu_custom_call" | custom-call | flops 37748736 | bytes 393216 | tf_op jit(solution)/shard_map/pallas_call | solution.py:181
  93.5 1.8 %copy.5 = f32[768,64]{0,1:T(8,128)} copy(f32[768,64]{1,0:T(8,128)} %get-tuple-element.18) | data formatting | bytes 393216
  95.3 0.0 collective-permute-done.20.other_ref
  95.3 0.0 copy-start.6
  95.3 0.0 copy-done.5
  95.3 0.8 copy-done.6
  96.1 2.6 %shard_map.44 = f32[64,4096]{1,0:T(8,128)} custom-call(f32[64,64]{1,0:T(8,128)} %get-tuple-element.17.inverse_ref, f32[16,64,128]{2,1,0:T(8,128)} %copy-done.5, f32[16,64,128]{2,1,0:T(8,128)} %copy-done.6), custom_call_target="tpu_custom_call" | custom-call | flops 100663296 | bytes 2097152 | tf_op jit(solution)/shard_map/pallas_call | solution.py:209
  (18 shorter events, 0.2 us)
Async XLA Ops:
  8.8 5.5 %collective-permute-start = (f32[96,128]{1,0:T(8,128)S(1)}, f32[96,128]{1,0:T(8,128)S(1)}, u32[]{:S(2)}, u32[]{:S(2)}) collective-permute-start(f32[96,128]{1,0:T(8,128)S(1)} %get-tuple-element.11), channel_id=1, source_target_pairs={{0,1},{1,0},{2,3},{3,2},{4,5},{5,4},{6,7},{7,6},{8,9},{9,8},{10,11... | collective-permute-start | bytes 147464 | tf_op jit(solution)/shard_map/ppermute | solution.py:219
  11.3 5.0 %collective-permute-start.1 = (f32[96,128]{1,0:T(8,128)S(1)}, f32[96,128]{1,0:T(8,128)S(1)}, u32[]{:S(2)}, u32[]{:S(2)}) collective-permute-start(f32[96,128]{1,0:T(8,128)S(1)} %get-tuple-element.12), channel_id=1, source_target_pairs={{0,2},{1,3},{2,0},{3,1},{4,6},{5,7},{6,4},{7,5},{8,10},{9,11},{10,... | collective-permute-start | bytes 147464 | tf_op jit(solution)/shard_map/ppermute | solution.py:219
  14.3 4.7 %collective-permute-start.2 = (f32[96,128]{1,0:T(8,128)S(1)}, f32[96,128]{1,0:T(8,128)S(1)}, u32[]{:S(2)}, u32[]{:S(2)}) collective-permute-start(f32[96,128]{1,0:T(8,128)S(1)} %get-tuple-element.13), channel_id=1, source_target_pairs={{0,3},{1,2},{2,1},{3,0},{4,7},{5,6},{6,5},{7,4},{8,11},{9,10},{10,... | collective-permute-start | bytes 147464 | tf_op jit(solution)/shard_map/ppermute | solution.py:219
  19.1 5.2 %collective-permute-start.3 = (f32[96,128]{1,0:T(8,128)S(1)}, f32[96,128]{1,0:T(8,128)S(1)}, u32[]{:S(2)}, u32[]{:S(2)}) collective-permute-start(f32[96,128]{1,0:T(8,128)S(1)} %add_add_fusion), channel_id=1, source_target_pairs={{0,7},{1,6},{2,5},{3,4},{4,3},{5,2},{6,1},{7,0},{8,15},{9,14},{10,... | collective-permute-start | bytes 147464 | tf_op jit(solution)/shard_map/ppermute | solution.py:219
  24.3 61.6 %copy-start.1 = (f32[96,128]{1,0:T(8,128)}, f32[96,128]{1,0:T(8,128)S(1)}, u32[]{:S(2)}) copy-start(f32[96,128]{1,0:T(8,128)S(1)} %add.36.s0) | copy-start | bytes 147460
  24.3 4.9 %collective-permute-start.6 = (f32[96,128]{1,0:T(8,128)S(1)}, f32[96,128]{1,0:T(8,128)S(1)}, u32[]{:S(2)}, u32[]{:S(2)}) collective-permute-start(f32[96,128]{1,0:T(8,128)S(1)} %add.36.s0), channel_id=1, source_target_pairs={{0,3},{1,2},{2,1},{3,0},{4,7},{5,6},{6,5},{7,4},{8,11},{9,10},{10,... | collective-permute-start | bytes 147464 | tf_op jit(solution)/shard_map/ppermute | solution.py:219
  25.5 4.6 %collective-permute-start.5 = (f32[96,128]{1,0:T(8,128)S(1)}, f32[96,128]{1,0:T(8,128)S(1)}, u32[]{:S(2)}, u32[]{:S(2)}) collective-permute-start(f32[96,128]{1,0:T(8,128)S(1)} %add.36.s0), channel_id=1, source_target_pairs={{0,2},{1,3},{2,0},{3,1},{4,6},{5,7},{6,4},{7,5},{8,10},{9,11},{10,... | collective-permute-start | bytes 147464 | tf_op jit(solution)/shard_map/ppermute | solution.py:219
  26.4 3.8 %collective-permute-start.4 = (f32[96,128]{1,0:T(8,128)S(1)}, f32[96,128]{1,0:T(8,128)S(1)}, u32[]{:S(2)}, u32[]{:S(2)}) collective-permute-start(f32[96,128]{1,0:T(8,128)S(1)} %add.36.s0), channel_id=1, source_target_pairs={{0,1},{1,0},{2,3},{3,2},{4,5},{5,4},{6,7},{7,6},{8,9},{9,8},{10,11... | collective-permute-start | bytes 147464 | tf_op jit(solution)/shard_map/ppermute | solution.py:219
  29.1 56.7 %copy-start.2 = (f32[96,128]{1,0:T(8,128)}, f32[96,128]{1,0:T(8,128)S(1)}, u32[]{:S(2)}) copy-start(f32[96,128]{1,0:T(8,128)S(1)} %collective-permute-done.6.s3) | copy-start | bytes 147460
  30.2 55.7 %copy-start.3 = (f32[96,128]{1,0:T(8,128)}, f32[96,128]{1,0:T(8,128)S(1)}, u32[]{:S(2)}) copy-start(f32[96,128]{1,0:T(8,128)S(1)} %collective-permute-done.5.s2) | copy-start | bytes 147460
  30.2 4.6 %copy-start = (f32[768,4096]{1,0:T(8,128)S(1)}, f32[768,4096]{1,0:T(8,128)}, u32[]{:S(2)}) copy-start(f32[768,4096]{1,0:T(8,128)} %data_ref.3) | copy-start | bytes 37748740
  34.8 51.1 %copy-start.4 = (f32[96,128]{1,0:T(8,128)}, f32[96,128]{1,0:T(8,128)S(1)}, u32[]{:S(2)}) copy-start(f32[96,128]{1,0:T(8,128)S(1)} %collective-permute-done.4.s1) | copy-start | bytes 147460
  41.5 6.4 %collective-permute-start.7 = (f32[17,64,128]{2,1,0:T(8,128)S(1)}, f32[17,64,128]{2,1,0:T(8,128)S(1)}, u32[]{:S(2)}, u32[]{:S(2)}) collective-permute-start(f32[17,64,128]{2,1,0:T(8,128)S(1)} %get-tuple-element.15), channel_id=1, source_target_pairs={{0,8},{8,0},{16,24},{24,16},{32,40},{40,32},{48,56},{56,48},{64,72... | collective-permute-start | bytes 1671176 | tf_op jit(solution)/shard_map/ppermute | solution.py:223
  48.0 5.8 %collective-permute-start.10 = (f32[5,64,128]{2,1,0:T(8,128)S(1)}, f32[5,64,128]{2,1,0:T(8,128)S(1)}, u32[]{:S(2)}, u32[]{:S(2)}) collective-permute-start(f32[5,64,128]{2,1,0:T(8,128)S(1)} %concatenate.41), channel_id=1, source_target_pairs={{0,192},{8,56},{16,208},{24,40},{32,224},{40,24},{48,240},{56,8},{... | collective-permute-start | bytes 491528 | tf_op jit(solution)/shard_map/ppermute | solution.py:223
  50.9 4.6 %collective-permute-start.8 = (f32[5,64,128]{2,1,0:T(8,128)S(1)}, f32[5,64,128]{2,1,0:T(8,128)S(1)}, u32[]{:S(2)}, u32[]{:S(2)}) collective-permute-start(f32[5,64,128]{2,1,0:T(8,128)S(1)} %get-tuple-element.32), channel_id=1, source_target_pairs={{0,64},{8,24},{16,80},{24,8},{32,96},{40,56},{48,112},{56,40},{64,... | collective-permute-start | bytes 491528 | tf_op jit(solution)/shard_map/ppermute | solution.py:223
  51.0 6.1 %collective-permute-start.9 = (f32[5,64,128]{2,1,0:T(8,128)S(1)}, f32[5,64,128]{2,1,0:T(8,128)S(1)}, u32[]{:S(2)}, u32[]{:S(2)}) collective-permute-start(f32[5,64,128]{2,1,0:T(8,128)S(1)} %get-tuple-element.33), channel_id=1, source_target_pairs={{0,128},{8,40},{16,144},{24,56},{32,160},{40,8},{48,176},{56,24},{... | collective-permute-start | bytes 491528 | tf_op jit(solution)/shard_map/ppermute | solution.py:223
  57.1 4.4 %collective-permute-start.13 = (f32[2,64,128]{2,1,0:T(8,128)S(1)}, f32[2,64,128]{2,1,0:T(8,128)S(1)}, u32[]{:S(2)}, u32[]{:S(2)}) collective-permute-start(f32[2,64,128]{2,1,0:T(8,128)S(1)} %concatenate.42), channel_id=1, source_target_pairs={{0,48},{8,200},{16,32},{24,216},{32,16},{40,232},{48,0},{56,248},{... | collective-permute-start | bytes 196616 | tf_op jit(solution)/shard_map/ppermute | solution.py:223
  59.7 3.5 %collective-permute-start.11 = (f32[2,64,128]{2,1,0:T(8,128)S(1)}, f32[2,64,128]{2,1,0:T(8,128)S(1)}, u32[]{:S(2)}, u32[]{:S(2)}) collective-permute-start(f32[2,64,128]{2,1,0:T(8,128)S(1)} %get-tuple-element.30), channel_id=1, source_target_pairs={{0,16},{8,72},{16,0},{24,88},{32,48},{40,104},{48,32},{56,120},{64... | collective-permute-start | bytes 196616 | tf_op jit(solution)/shard_map/ppermute | solution.py:223
  59.8 4.7 %collective-permute-start.12 = (f32[2,64,128]{2,1,0:T(8,128)S(1)}, f32[2,64,128]{2,1,0:T(8,128)S(1)}, u32[]{:S(2)}, u32[]{:S(2)}) collective-permute-start(f32[2,64,128]{2,1,0:T(8,128)S(1)} %get-tuple-element.31), channel_id=1, source_target_pairs={{0,32},{8,136},{16,48},{24,152},{32,0},{40,168},{48,16},{56,184},{... | collective-permute-start | bytes 196616 | tf_op jit(solution)/shard_map/ppermute | solution.py:223
  65.1 4.0 %collective-permute-start.16 = (f32[1,64,128]{2,1,0:T(8,128)S(1)}, f32[1,64,128]{2,1,0:T(8,128)S(1)}, u32[]{:S(2)}, u32[]{:S(2)}) collective-permute-start(f32[1,64,128]{2,1,0:T(8,128)S(1)} %get-tuple-element.27), channel_id=1, source_target_pairs={{0,48},{8,200},{16,32},{24,216},{32,16},{40,232},{48,0},{56,248},{... | collective-permute-start | bytes 98312 | tf_op jit(solution)/shard_map/ppermute | solution.py:223
  66.6 4.3 %collective-permute-start.15 = (f32[1,64,128]{2,1,0:T(8,128)S(1)}, f32[1,64,128]{2,1,0:T(8,128)S(1)}, u32[]{:S(2)}, u32[]{:S(2)}) collective-permute-start(f32[1,64,128]{2,1,0:T(8,128)S(1)} %get-tuple-element.27), channel_id=1, source_target_pairs={{0,32},{8,136},{16,48},{24,152},{32,0},{40,168},{48,16},{56,184},{... | collective-permute-start | bytes 98312 | tf_op jit(solution)/shard_map/ppermute | solution.py:223
  68.3 2.8 %collective-permute-start.14 = (f32[1,64,128]{2,1,0:T(8,128)S(1)}, f32[1,64,128]{2,1,0:T(8,128)S(1)}, u32[]{:S(2)}, u32[]{:S(2)}) collective-permute-start(f32[1,64,128]{2,1,0:T(8,128)S(1)} %get-tuple-element.27), channel_id=1, source_target_pairs={{0,16},{8,72},{16,0},{24,88},{32,48},{40,104},{48,32},{56,120},{64... | collective-permute-start | bytes 98312 | tf_op jit(solution)/shard_map/ppermute | solution.py:223
  71.0 8.3 %collective-permute-start.19 = (f32[4,64,128]{2,1,0:T(8,128)S(1)}, f32[4,64,128]{2,1,0:T(8,128)S(1)}, u32[]{:S(2)}, u32[]{:S(2)}) collective-permute-start(f32[4,64,128]{2,1,0:T(8,128)S(1)} %pad_maximum_fusion.3), channel_id=1, source_target_pairs={{0,192},{8,56},{16,208},{24,40},{32,224},{40,24},{48,240},{56,8},{... | collective-permute-start | bytes 393224 | tf_op jit(solution)/shard_map/ppermute | solution.py:223
  74.0 5.3 %collective-permute-start.18 = (f32[4,64,128]{2,1,0:T(8,128)S(1)}, f32[4,64,128]{2,1,0:T(8,128)S(1)}, u32[]{:S(2)}, u32[]{:S(2)}) collective-permute-start(f32[4,64,128]{2,1,0:T(8,128)S(1)} %pad_maximum_fusion.3), channel_id=1, source_target_pairs={{0,128},{8,40},{16,144},{24,56},{32,160},{40,8},{48,176},{56,24},{... | collective-permute-start | bytes 393224 | tf_op jit(solution)/shard_map/ppermute | solution.py:223
  74.3 4.2 %collective-permute-start.17 = (f32[4,64,128]{2,1,0:T(8,128)S(1)}, f32[4,64,128]{2,1,0:T(8,128)S(1)}, u32[]{:S(2)}, u32[]{:S(2)}) collective-permute-start(f32[4,64,128]{2,1,0:T(8,128)S(1)} %pad_maximum_fusion.3), channel_id=1, source_target_pairs={{0,64},{8,24},{16,80},{24,8},{32,96},{40,56},{48,112},{56,40},{64,... | collective-permute-start | bytes 393224 | tf_op jit(solution)/shard_map/ppermute | solution.py:223
  79.3 16.0 %copy-start.5 = (f32[16,64,128]{2,1,0:T(8,128)}, f32[16,64,128]{2,1,0:T(8,128)S(1)}, u32[]{:S(2)}) copy-start(f32[16,64,128]{2,1,0:T(8,128)S(1)} %constant_dynamic-update-slice_fusion.own_ref) | copy-start | bytes 1572868
  79.3 16.0 %collective-permute-start.20 = (f32[16,64,128]{2,1,0:T(8,128)S(1)}, f32[16,64,128]{2,1,0:T(8,128)S(1)}, u32[]{:S(2)}, u32[]{:S(2)}) collective-permute-start(f32[16,64,128]{2,1,0:T(8,128)S(1)} %constant_dynamic-update-slice_fusion.own_ref), channel_id=1, source_target_pairs={{0,8},{8,0},{16,24},{24,16},{32,40},{40,32},{48,56},{56,48},{64,72... | collective-permute-start | bytes 1572872 | tf_op jit(solution)/shard_map/ppermute | solution.py:223
  95.3 0.8 copy-start.6

commit v2 on v0

v2 whole, which is shorter than its diff:
```python
import functools
import math

import jax
import jax.numpy as jnp
from jax import lax
from jax.experimental import pallas as pl
from jax.experimental.pallas import tpu as pltpu
from jax.sharding import PartitionSpec as P

F32 = jnp.float32
BF16 = jnp.bfloat16
VMEM = pltpu.VMEM
MIB = 2**20
K = 64
LANES = 128
HALVES = 2
CHUNKS = 4
BLOCKS = 32
GROUPS = 8
PER_GROUP = 4


def split(value):
    high = value.astype(BF16)
    return high, (value - high.astype(F32)).astype(BF16)


def own_half():
    z = lax.axis_index("col")
    return jnp.where(z < 4, z, 7 - z) % HALVES


def position():
    row = lax.axis_index("row")
    core, y, x = row % 2, (row // 2) % 4, row // 8
    return core, jnp.where(core == 0, x, y), jnp.where(core == 0, y, x)


def group_place(group):
    core, first, second = position()
    if group < PER_GROUP:
        return core * PER_GROUP + (first ^ group)
    return (1 - core) * PER_GROUP + (second ^ (group - PER_GROUP))


def vmem(count):
    return [pl.BlockSpec(memory_space=VMEM)] * count


def packed(value):
    half = value.shape[0] // 2
    return jnp.concatenate([value[:half], value[half:]], axis=1)


def unpacked(value):
    return jnp.concatenate([value[:, :K], value[:, K:]], axis=0)


def sample_half(data_ref, half, weights, out_ref, terms_ref, data, sems, prepare):
    count, chunk = data.shape[:2]
    rows = count * chunk
    copies = []
    for i in range(count):
        start = pl.multiple_of(half * rows + i * chunk, chunk)
        copies.append(pltpu.make_async_copy(data_ref.at[pl.ds(start, chunk)], data.at[i], sems.at[i]))
        copies[i].start()
    prepare()
    lane = lax.broadcasted_iota(jnp.int32, (chunk, LANES), 1)
    totals = []
    for i in range(count):
        copies[i].wait()
        high, low = split(data[i])
        terms_ref[pl.ds(i * chunk, chunk), :] = high
        terms_ref[pl.ds(rows + i * chunk, chunk), :] = low
        total = jnp.dot(high, weights[...], preferred_element_type=F32)
        total += jnp.dot(low, weights[...], preferred_element_type=F32)
        totals.append(total + pltpu.roll(total, K, axis=1))
    for i in range(count // 2):
        out_ref[pl.ds(i * chunk, chunk), :] = jnp.where(lane < K, totals[i], totals[i + count // 2])


def send_kernel(data_ref, sketch_ref, out_ref, terms_ref, weights_ref, data, sketch, sems):
    load = pltpu.make_async_copy(sketch_ref, sketch, sems.at[CHUNKS])
    load.start()

    def prepare():
        load.wait()
        high, low = split(sketch[...].T)
        weights_ref[...] = jnp.concatenate([high, low], axis=1)

    sample_half(data_ref, 1 - own_half(), weights_ref, out_ref, terms_ref, data, sems, prepare)


def keep_kernel(data_ref, weights_ref, out_ref, terms_ref, data, sems):
    sample_half(data_ref, own_half(), weights_ref, out_ref, terms_ref, data, sems, lambda: None)


def partial_samples(data_slab, sketch_t):
    rows, columns = data_slab.shape
    half = rows // HALVES
    chunk = half // CHUNKS
    cost = pl.CostEstimate(flops=4 * rows * columns * K, bytes_accessed=4 * half * columns, transcendentals=0)
    outs = [jax.ShapeDtypeStruct((half // 2, LANES), F32), jax.ShapeDtypeStruct((2 * half, columns), BF16)]
    sent, sent_terms, weights = pl.pallas_call(
        send_kernel,
        out_shape=outs + [jax.ShapeDtypeStruct((columns, LANES), BF16)],
        in_specs=[pl.BlockSpec(memory_space=pl.ANY)] * 2,
        out_specs=vmem(3),
        scratch_shapes=[
            VMEM((CHUNKS, chunk, columns), F32),
            VMEM((K, columns), F32),
            pltpu.SemaphoreType.DMA((CHUNKS + 1,)),
        ],
        compiler_params=pltpu.CompilerParams(vmem_limit_bytes=44 * MIB),
        cost_estimate=cost,
    )(data_slab, sketch_t)
    kept, kept_terms = pl.pallas_call(
        keep_kernel,
        out_shape=outs,
        in_specs=[pl.BlockSpec(memory_space=pl.ANY)] + vmem(1),
        out_specs=vmem(2),
        scratch_shapes=[VMEM((CHUNKS, chunk, columns), F32), pltpu.SemaphoreType.DMA((CHUNKS,))],
        compiler_params=pltpu.CompilerParams(vmem_limit_bytes=40 * MIB),
        cost_estimate=cost,
    )(data_slab, weights)
    return sent, sent_terms, kept, kept_terms


def left_of(sample):
    high, low = split(unpacked(sample).T)
    left = jnp.concatenate([high, low], axis=0)
    return left, jnp.concatenate([left, left], axis=1)


def first_term_kernel(sample_ref, terms_ref, out_ref):
    _, left = left_of(sample_ref[...])
    width = out_ref.shape[1] // GROUPS
    for g in range(GROUPS):
        at = pl.ds(g * width, width)
        total = jnp.dot(left, terms_ref[:, at], preferred_element_type=F32)
        out_ref[:, at] = total[:K] + total[K:]


def second_term_kernel(other_ref, sample_ref, terms_ref, begun_ref, keep_ref, send_ref):
    single, left = left_of(sample_ref[...])
    other, _ = left_of(other_ref[...])
    both = jnp.concatenate([single, other], axis=1)
    gram = lax.dot_general(both, both, (((1,), (1,)), ((), ())), preferred_element_type=F32)
    gram = gram[:K] + gram[K:]
    gram = gram + pltpu.roll(gram, K, axis=1)
    keep_ref[BLOCKS // 2] = gram
    send_ref[BLOCKS // 2] = gram
    width = PER_GROUP * LANES
    for g in (4, 5, 6, 7, 0, 1, 2, 3):
        at = pl.ds(pl.multiple_of(group_place(g) * width, width), width)
        total = jnp.dot(left, terms_ref[:, at], preferred_element_type=F32)
        total = total[:K] + total[K:] + begun_ref[:, at]
        out_ref, base = (keep_ref, g) if g < PER_GROUP else (send_ref, g - PER_GROUP)
        for t in range(PER_GROUP):
            out_ref[base * PER_GROUP + t] = total[:, t * LANES : (t + 1) * LANES]


def term_cost(terms):
    return pl.CostEstimate(flops=4 * K * terms.size, bytes_accessed=2 * terms.size, transcendentals=0)


def first_terms(sample, terms):
    return pl.pallas_call(
        first_term_kernel,
        out_shape=jax.ShapeDtypeStruct((K, terms.shape[1]), F32),
        in_specs=vmem(2),
        out_specs=vmem(1)[0],
        compiler_params=pltpu.CompilerParams(vmem_limit_bytes=16 * MIB),
        cost_estimate=term_cost(terms),
    )(sample, terms)


def second_terms(other, sample, terms, begun):
    return pl.pallas_call(
        second_term_kernel,
        out_shape=[jax.ShapeDtypeStruct((BLOCKS // 2 + 1, K, LANES), F32)] * 2,
        in_specs=vmem(4),
        out_specs=vmem(2),
        compiler_params=pltpu.CompilerParams(vmem_limit_bytes=16 * MIB),
        cost_estimate=term_cost(terms),
    )(other, sample, terms, begun)


def inverse_kernel(gram_ref, inverse_ref):
    lane = lax.broadcasted_iota(jnp.int32, (K, LANES), 1)
    row = lax.broadcasted_iota(jnp.int32, (K, LANES), 0)
    work = jnp.where(lane < K, gram_ref[...], jnp.where(lane == row + K, 1.0, 0.0))
    parts = [work[8 * i : 8 * i + 8] for i in range(K // 8)]
    sub = lax.broadcasted_iota(jnp.int32, (8, 1), 0)
    pivots = []
    for j in range(K):
        block, at = divmod(j, 8)
        line = parts[block][at : at + 1]
        pivot = line[:, j : j + 1]
        pivots.append(pivot)
        scaled = line * (1.0 / pivot)
        for i in range(block, K // 8):
            factor = parts[i][:, j : j + 1]
            if i == block:
                factor = jnp.where(sub > at, factor, 0.0)
            parts[i] = parts[i] - factor * scaled
    for i in range(K // 8):
        diagonal = jnp.concatenate(pivots[8 * i : 8 * i + 8], axis=0)
        parts[i] = parts[i] * (1.0 / jnp.sqrt(diagonal))
    inverse_ref[...] = jnp.concatenate(parts, axis=0)[:, K:]


def inverse_of(gram):
    return pl.pallas_call(
        inverse_kernel,
        out_shape=jax.ShapeDtypeStruct((K, K), F32),
        in_specs=vmem(1),
        out_specs=vmem(1)[0],
        compiler_params=pltpu.CompilerParams(vmem_limit_bytes=8 * MIB),
        cost_estimate=pl.CostEstimate(flops=K**3 * 100, bytes_accessed=8 * K * K, transcendentals=K),
    )(gram)


def basis_kernel(scale, inverse_ref, own_ref, other_ref, basis_ref):
    half = basis_ref.shape[1] // HALVES
    left = inverse_ref[...] * scale
    own, other = [
        lax.dot_general(
            left,
            unpacked(ref[...]),
            (((1,), (1,)), ((), ())),
            precision=lax.Precision.HIGHEST,
            preferred_element_type=F32,
        )
        for ref in (own_ref, other_ref)
    ]
    is_first = own_half() == 0
    basis_ref[:, :half] = jnp.where(is_first, own, other)
    basis_ref[:, half:] = jnp.where(is_first, other, own)


def basis_of(inverse, own, other, rows, scale):
    return pl.pallas_call(
        functools.partial(basis_kernel, scale),
        out_shape=jax.ShapeDtypeStruct((K, rows), F32),
        in_specs=vmem(3),
        out_specs=vmem(1)[0],
        compiler_params=pltpu.CompilerParams(vmem_limit_bytes=8 * MIB),
        cost_estimate=pl.CostEstimate(flops=12 * rows * K * K, bytes_accessed=8 * rows * K, transcendentals=0),
    )(inverse, own, other)


def apply_kernel(inverse_ref, own_ref, other_ref, out_ref):
    high, low = split(inverse_ref[...])
    left = jnp.concatenate([high, low, high], axis=1)
    width = PER_GROUP * LANES
    for g in range(GROUPS):
        ref, base = (own_ref, g) if g < PER_GROUP else (other_ref, g - PER_GROUP)
        value = jnp.concatenate([ref[base * PER_GROUP + t] for t in range(PER_GROUP)], axis=1)
        high, low = split(value)
        right = jnp.concatenate([high, high, low], axis=0)
        at = pl.ds(pl.multiple_of(group_place(g) * width, width), width)
        out_ref[:, at] = jnp.dot(left, right, preferred_element_type=F32)


def applied(inverse, own, other):
    columns = BLOCKS * LANES
    return pl.pallas_call(
        apply_kernel,
        out_shape=jax.ShapeDtypeStruct((K, columns), F32),
        in_specs=vmem(3),
        out_specs=vmem(1)[0],
        compiler_params=pltpu.CompilerParams(vmem_limit_bytes=8 * MIB),
        cost_estimate=pl.CostEstimate(flops=6 * columns * K * K, bytes_accessed=8 * columns * K, transcendentals=0),
    )(inverse, own, other)


def along_col(value, mask):
    return lax.ppermute(value, "col", [(i, i ^ mask) for i in range(8)])


def along_row(value, masks):
    return lax.ppermute(value, "row", [(i, i ^ masks[i % 2]) for i in range(32)])


CORE = (1, 1)
FIRST = [(t << 3, t << 1) for t in range(4)]
SECOND = [(t << 1, t << 3) for t in range(4)]


def body(data_slab, sketch):
    rows = data_slab.shape[0]
    sent, sent_terms, kept, kept_terms = partial_samples(data_slab, sketch.T)
    own = kept + along_col(sent, 1)
    own = own + along_col(own, 2)
    own = own + along_col(own, 7)
    other = along_col(own, 1)

    begun = first_terms(own, kept_terms)
    keep, send = second_terms(own, other, sent_terms, begun)
    total = keep + along_row(send, CORE)
    gram = total[16:]
    got = [along_row(jnp.concatenate([total[4 * t : 4 * t + 4], gram]), FIRST[t]) for t in (1, 2, 3)]
    total = jnp.concatenate([total[:4], gram]) + got[0] + got[1] + got[2]
    got = [along_row(total, SECOND[t]) for t in (1, 2, 3)]
    total = total + got[0] + got[1] + got[2]

    inverse = inverse_of(total[4])
    block = total[:4]
    mine = jnp.concatenate([block] + [along_row(block, FIRST[t]) for t in (1, 2, 3)])
    mine, inverse = lax.optimization_barrier((mine, inverse))
    theirs = along_row(mine, CORE)
    range_basis = basis_of(inverse, own, other, rows, math.sqrt(rows * lax.axis_size("row")))
    return range_basis.T, applied(inverse, mine, theirs)


def solution(mesh):
    placed = (P("row", "col"), P("col", None))
    return jax.shard_map(
        body,
        mesh=mesh,
        in_specs=placed,
        out_specs=(P("row", None), P(None, "col")),
        check_vma=False,
    )
```

time: 307 us -> 70.9 us (0.23)
  waiting for transfers between devices: 192 us -> 23.6 us
  other arithmetic: 48.7 us -> 0.24 us
  matrix products: 34.3 us -> 0 us
  Pallas kernels: 0 us -> 18.8 us
  between operations: 14.3 us -> 0.79 us
  starting transfers between devices: 13.7 us -> 26 us
    psum x2 -> x0, waiting for transfers between devices: 189 us -> none  [the longest x1 117 us: body(): projected = lax.psum(term, 'row')]
    another operation x20 -> x0, other arithmetic: 44.7 us -> none  [the longest x18 39.1 us: lower_of(): return jnp.linalg.cholesky(gram_matrix)]
    dot_general x13 -> x0, matrix products: 33 us -> none  [the longest x1 15.5 us: body(): jnp.dot(data_slab, sketch, precision=lax.Precision.HIGHEST, preferred_ele...]
    ppermute x5 -> x15, waiting for transfers between devices: 2.92 us -> 23.6 us  [the longest x4 11.8 us: along_col(): return lax.ppermute(value, 'col', [(i, i ^ mask) for i in range(8)])]
    pallas_call x0 -> x7, Pallas kernels: none -> 18.8 us  [the longest x1 5.45 us: inverse_of(): pl.pallas_call(inverse_kernel, out_shape=jax.ShapeDtypeStruct((K, K), F32...]
    ppermute x5 -> x15, starting transfers between devices: 13.6 us -> 26 us  [the longest x11 16.2 us: along_row(): lax.ppermute(value, 'row', [(i, i ^ masks[i % 2]) for i in range(32)])]
    transpose x5 -> x0, other arithmetic: 3.26 us -> none  [the longest x4 2.61 us: body(): upper_factor = lower_of(merged).T]
  transfers between devices with their start and end apart: 7 -> 15, of which waited for: 6 -> 10; matrix products, arithmetic and copies ran while one was open for 2% -> 0% of each run, Pallas kernels for 0% -> 17%
where the time goes in v2:
time: 70.9 us; the launch traced here: 70.8 us
  starting transfers between devices  26 us (37%)
  waiting for transfers between devices  23.6 us (33%)
  Pallas kernels  18.8 us (27%)
  local copies, waits for them, and re-layouts  1.28 us (2%)
  between operations  0.79 us (1%)
    ppermute x11, starting transfers between devices, along_row(): lax.ppermute(value, 'row', [(i, i ^ masks[i % 2]) for i in range(32)])  16.2 us
    ppermute x4, waiting for transfers between devices, along_col(): return lax.ppermute(value, 'col', [(i, i ^ mask) for i in range(8)])  11.8 us
    ppermute x11, waiting for transfers between devices, along_row(): lax.ppermute(value, 'row', [(i, i ^ masks[i % 2]) for i in range(32)])  11.8 us
    ppermute x4, starting transfers between devices, along_col(): return lax.ppermute(value, 'col', [(i, i ^ mask) for i in range(8)])  9.82 us
    pallas_call x1, Pallas kernels, inverse_of(): pl.pallas_call(inverse_kernel, out_shape=jax.ShapeDtypeStruct((K, K), F32...  5.45 us
    pallas_call x1, Pallas kernels, partial_samples(): pl.pallas_call(send_kernel, out_shape=outs + [jax.ShapeDtypeStruct((colum...  4.24 us
    pallas_call x1, Pallas kernels, partial_samples(): pl.pallas_call(keep_kernel, out_shape=outs, in_specs=[pl.BlockSpec(memory...  4.15 us
    pallas_call x1, Pallas kernels, applied(): pl.pallas_call(apply_kernel, out_shape=jax.ShapeDtypeStruct((K, columns),...  1.43 us
  transfers between devices with their start and end apart: 15, of which 10 were waited for; matrix products, arithmetic and copies ran while one was open for 0% of the time, Pallas kernels for 17%

profile of v2, /device:TPU:1, one launch (start us, length us, event | category | flops | bytes accessed | tf_op | source)
XLA Modules:
  0.0 70.8 jit_solution(15158391074896285803)
XLA Ops:
  0.6 0.0 copy-start
  0.6 1.2 %copy-done = f32[4096,64]{0,1:T(8,128)S(1)} copy-done((f32[4096,64]{0,1:T(8,128)S(1)}, f32[4096,64]{0,1:T(8,128)}, u32[]{:S(2)}) %copy-start) | copy-done | bytes 1048600
  1.9 4.2 %shard_map.41 = (f32[192,128]{1,0:T(8,128)S(1)}, bf16[768,4096]{1,0:T(8,128)(2,1)S(1)}, bf16[4096,128]{1,0:T(8,128)(2,1)S(1)}) custom-call(f32[768,4096]{1,0:T(8,128)} %data_ref.3, f32[64,4096]{1,0:T(8,128)S(1)} %bitcast.4), custom_call_target="tpu_custom_call" | custom-call | flops 805306368 | bytes 6291456 | tf_op jit(solution)/shard_map/pallas_call | solution.py:105
  6.1 2.6 %collective-permute-start = (f32[192,128]{1,0:T(8,128)S(1)}, f32[192,128]{1,0:T(8,128)S(1)}, u32[]{:S(2)}, u32[]{:S(2)}) collective-permute-start(f32[192,128]{1,0:T(8,128)S(1)} %get-tuple-element.13), channel_id=1, source_target_pairs={{0,1},{1,0},{2,3},{3,2},{4,5},{5,4},{6,7},{7,6},{8,9},{9,8},{10,11... | collective-permute-start | bytes 294920 | tf_op jit(solution)/shard_map/ppermute | solution.py:280
  8.7 4.2 %shard_map.42 = (f32[192,128]{1,0:T(8,128)S(1)}, bf16[768,4096]{1,0:T(8,128)(2,1)S(1)}) custom-call(f32[768,4096]{1,0:T(8,128)} %data_ref.3, bf16[4096,128]{1,0:T(8,128)(2,1)S(1)} %get-tuple-element.11.weights_ref), custom_call_target="tpu_custom_call" | custom-call | flops 805306368 | bytes 6291456 | tf_op jit(solution)/shard_map/pallas_call | solution.py:118
  12.8 0.0 collective-permute-done
  12.9 3.1 %collective-permute-start.1 = (f32[192,128]{1,0:T(8,128)S(1)}, f32[192,128]{1,0:T(8,128)S(1)}, u32[]{:S(2)}, u32[]{:S(2)}) collective-permute-start(f32[192,128]{1,0:T(8,128)S(1)} %add.30), channel_id=1, source_target_pairs={{0,2},{1,3},{2,0},{3,1},{4,6},{5,7},{6,4},{7,5},{8,10},{9,11},{10,... | collective-permute-start | bytes 294920 | tf_op jit(solution)/shard_map/ppermute | solution.py:280
  15.9 4.9 %collective-permute-done.1 = f32[192,128]{1,0:T(8,128)S(1)} collective-permute-done((f32[192,128]{1,0:T(8,128)S(1)}, f32[192,128]{1,0:T(8,128)S(1)}, u32[]{:S(2)}, u32[]{:S(2)}) %collective-permute-start.1) | collective-permute-done | bytes 98336 | tf_op jit(solution)/shard_map/ppermute | solution.py:280
  20.8 4.1 %collective-permute-start.2 = (f32[192,128]{1,0:T(8,128)S(1)}, f32[192,128]{1,0:T(8,128)S(1)}, u32[]{:S(2)}, u32[]{:S(2)}) collective-permute-start(f32[192,128]{1,0:T(8,128)S(1)} %add.31), channel_id=1, source_target_pairs={{0,7},{1,6},{2,5},{3,4},{4,3},{5,2},{6,1},{7,0},{8,15},{9,14},{10,... | collective-permute-start | bytes 294920 | tf_op jit(solution)/shard_map/ppermute | solution.py:280
  24.9 4.3 %collective-permute-done.2 = f32[192,128]{1,0:T(8,128)S(1)} collective-permute-done((f32[192,128]{1,0:T(8,128)S(1)}, f32[192,128]{1,0:T(8,128)S(1)}, u32[]{:S(2)}, u32[]{:S(2)}) %collective-permute-start.2) | collective-permute-done | bytes 98336 | tf_op jit(solution)/shard_map/ppermute | solution.py:280
  29.2 0.1 collective-permute-start.3
  29.3 1.1 %shard_map.43.begun_ref = f32[64,4096]{1,0:T(8,128)S(1)} custom-call(f32[192,128]{1,0:T(8,128)S(1)} %add.32.sample_ref.other_ref.own_ref, bf16[768,4096]{1,0:T(8,128)(2,1)S(1)} %get-tuple-element.15.terms_ref), custom_call_target="tpu_custom_call" | custom-call | flops 805306368 | bytes 6291456 | tf_op jit(solution)/shard_map/pallas_call | solution.py:169
  30.4 2.7 %collective-permute-done.3.sample_ref.other_ref = f32[192,128]{1,0:T(8,128)S(1)} collective-permute-done((f32[192,128]{1,0:T(8,128)S(1)}, f32[192,128]{1,0:T(8,128)S(1)}, u32[]{:S(2)}, u32[]{:S(2)}) %collective-permute-start.3) | collective-permute-done | bytes 98336 | tf_op jit(solution)/shard_map/ppermute | solution.py:280
  33.1 1.2 %shard_map.44 = (f32[17,64,128]{2,1,0:T(8,128)S(1)}, f32[17,64,128]{2,1,0:T(8,128)S(1)}) custom-call(f32[192,128]{1,0:T(8,128)S(1)} %add.32.sample_ref.other_ref.own_ref, f32[192,128]{1,0:T(8,128)S(1)} %collective-permute-done.3.sample_ref.other_ref, bf16[768,4096]{1,0:T(8,128)(2,1)S(1)} %get-tuple-element.14.terms_ref, f32[64,4096]{1,0:T(8,128)S(1)} %shard_map.43.begun_ref), custom_call_target="tpu_custom_call" | custom-call | flops 805306368 | bytes 6291456 | tf_op jit(solution)/shard_map/pallas_call | solution.py:180
  34.3 1.5 %collective-permute-start.4 = (f32[17,64,128]{2,1,0:T(8,128)S(1)}, f32[17,64,128]{2,1,0:T(8,128)S(1)}, u32[]{:S(2)}, u32[]{:S(2)}) collective-permute-start(f32[17,64,128]{2,1,0:T(8,128)S(1)} %get-tuple-element.17), channel_id=1, source_target_pairs={{0,8},{8,0},{16,24},{24,16},{32,40},{40,32},{48,56},{56,48},{64,72... | collective-permute-start | bytes 1671176 | tf_op jit(solution)/shard_map/ppermute | solution.py:284
  35.8 1.6 %collective-permute-done.4 = f32[17,64,128]{2,1,0:T(8,128)S(1)} collective-permute-done((f32[17,64,128]{2,1,0:T(8,128)S(1)}, f32[17,64,128]{2,1,0:T(8,128)S(1)}, u32[]{:S(2)}, u32[]{:S(2)}) %collective-permute-start.4) | collective-permute-done | bytes 557088 | tf_op jit(solution)/shard_map/ppermute | solution.py:284
  37.4 0.1 add.33
  37.5 2.8 %collective-permute-start.7 = (f32[5,64,128]{2,1,0:T(8,128)S(1)}, f32[5,64,128]{2,1,0:T(8,128)S(1)}, u32[]{:S(2)}, u32[]{:S(2)}) collective-permute-start(f32[5,64,128]{2,1,0:T(8,128)S(1)} %concatenate.20), channel_id=1, source_target_pairs={{0,192},{8,56},{16,208},{24,40},{32,224},{40,24},{48,240},{56,8},{... | collective-permute-start | bytes 491528 | tf_op jit(solution)/shard_map/ppermute | solution.py:284
  40.4 0.1 collective-permute-start.5
  40.5 1.2 %collective-permute-start.6 = (f32[5,64,128]{2,1,0:T(8,128)S(1)}, f32[5,64,128]{2,1,0:T(8,128)S(1)}, u32[]{:S(2)}, u32[]{:S(2)}) collective-permute-start(f32[5,64,128]{2,1,0:T(8,128)S(1)} %get-tuple-element.24), channel_id=1, source_target_pairs={{0,128},{8,40},{16,144},{24,56},{32,160},{40,8},{48,176},{56,24},{... | collective-permute-start | bytes 491528 | tf_op jit(solution)/shard_map/ppermute | solution.py:284
  41.7 1.7 %collective-permute-done.7 = f32[5,64,128]{2,1,0:T(8,128)S(1)} collective-permute-done((f32[5,64,128]{2,1,0:T(8,128)S(1)}, f32[5,64,128]{2,1,0:T(8,128)S(1)}, u32[]{:S(2)}, u32[]{:S(2)}) %collective-permute-start.7) | collective-permute-done | bytes 163872 | tf_op jit(solution)/shard_map/ppermute | solution.py:284
  43.4 1.6 %collective-permute-done.5 = f32[5,64,128]{2,1,0:T(8,128)S(1)} collective-permute-done((f32[5,64,128]{2,1,0:T(8,128)S(1)}, f32[5,64,128]{2,1,0:T(8,128)S(1)}, u32[]{:S(2)}, u32[]{:S(2)}) %collective-permute-start.5) | collective-permute-done | bytes 163872 | tf_op jit(solution)/shard_map/ppermute | solution.py:284
  44.9 1.8 %collective-permute-done.6 = f32[5,64,128]{2,1,0:T(8,128)S(1)} collective-permute-done((f32[5,64,128]{2,1,0:T(8,128)S(1)}, f32[5,64,128]{2,1,0:T(8,128)S(1)}, u32[]{:S(2)}, u32[]{:S(2)}) %collective-permute-start.6) | collective-permute-done | bytes 163872 | tf_op jit(solution)/shard_map/ppermute | solution.py:284
  46.8 2.6 %collective-permute-start.10 = (f32[5,64,128]{2,1,0:T(8,128)S(1)}, f32[5,64,128]{2,1,0:T(8,128)S(1)}, u32[]{:S(2)}, u32[]{:S(2)}) collective-permute-start(f32[5,64,128]{2,1,0:T(8,128)S(1)} %fusion.2), channel_id=1, source_target_pairs={{0,48},{8,200},{16,32},{24,216},{32,16},{40,232},{48,0},{56,248},{... | collective-permute-start | bytes 491528 | tf_op jit(solution)/shard_map/ppermute | solution.py:284
  49.3 0.2 collective-permute-start.9
  49.6 0.6 collective-permute-start.8
  50.1 3.2 %collective-permute-done.10 = f32[5,64,128]{2,1,0:T(8,128)S(1)} collective-permute-done((f32[5,64,128]{2,1,0:T(8,128)S(1)}, f32[5,64,128]{2,1,0:T(8,128)S(1)}, u32[]{:S(2)}, u32[]{:S(2)}) %collective-permute-start.10) | collective-permute-done | bytes 163872 | tf_op jit(solution)/shard_map/ppermute | solution.py:284
  53.4 1.7 %collective-permute-done.9 = f32[5,64,128]{2,1,0:T(8,128)S(1)} collective-permute-done((f32[5,64,128]{2,1,0:T(8,128)S(1)}, f32[5,64,128]{2,1,0:T(8,128)S(1)}, u32[]{:S(2)}, u32[]{:S(2)}) %collective-permute-start.9) | collective-permute-done | bytes 163872 | tf_op jit(solution)/shard_map/ppermute | solution.py:284
  55.0 0.0 collective-permute-done.8
  55.1 2.6 %collective-permute-start.13 = (f32[4,64,128]{2,1,0:T(8,128)S(1)}, f32[4,64,128]{2,1,0:T(8,128)S(1)}, u32[]{:S(2)}, u32[]{:S(2)}) collective-permute-start(f32[4,64,128]{2,1,0:T(8,128)S(1)} %slice.30), channel_id=1, source_target_pairs={{0,192},{8,56},{16,208},{24,40},{32,224},{40,24},{48,240},{56,8},{... | collective-permute-start | bytes 393224 | tf_op jit(solution)/shard_map/ppermute | solution.py:284
  57.7 0.4 collective-permute-start.12
  58.1 0.3 collective-permute-start.11
  58.4 5.5 %shard_map.45.inverse_ref = f32[64,64]{1,0:T(8,128)S(1)} custom-call(f32[64,128]{1,0:T(8,128)S(1)} %slice_bitcast_fusion.gram_ref), custom_call_target="tpu_custom_call" | custom-call | flops 26214400 | bytes 32768 | tf_op jit(solution)/shard_map/pallas_call | solution.py:215
  63.9 0.0 collective-permute-done.13
  63.9 0.0 collective-permute-done.12
  63.9 0.0 collective-permute-done.11
  63.9 3.9 %collective-permute-start.14 = (f32[16,64,128]{2,1,0:T(8,128)S(1)}, f32[16,64,128]{2,1,0:T(8,128)S(1)}, u32[]{:S(2)}, u32[]{:S(2)}) collective-permute-start(f32[16,64,128]{2,1,0:T(8,128)S(1)} %pad_maximum_fusion.own_ref), channel_id=1, source_target_pairs={{0,8},{8,0},{16,24},{24,16},{32,40},{40,32},{48,56},{56,48},{64,72... | collective-permute-start | bytes 1572872 | tf_op jit(solution)/shard_map/ppermute | solution.py:284
  67.8 1.3 %shard_map.46 = f32[64,768]{1,0:T(8,128)} custom-call(f32[64,64]{1,0:T(8,128)S(1)} %shard_map.45.inverse_ref, f32[192,128]{1,0:T(8,128)S(1)} %add.32.sample_ref.other_ref.own_ref, f32[192,128]{1,0:T(8,128)S(1)} %collective-permute-done.3.sample_ref.other_ref), custom_call_target="tpu_custom_call" | custom-call | flops 37748736 | bytes 393216 | tf_op jit(solution)/shard_map/pallas_call | solution.py:244
  69.1 0.3 collective-permute-done.14.other_ref
  69.3 1.4 %shard_map.47 = f32[64,4096]{1,0:T(8,128)} custom-call(f32[64,64]{1,0:T(8,128)S(1)} %shard_map.45.inverse_ref, f32[16,64,128]{2,1,0:T(8,128)S(1)} %pad_maximum_fusion.own_ref, f32[16,64,128]{2,1,0:T(8,128)S(1)} %collective-permute-done.14.other_ref), custom_call_target="tpu_custom_call" | custom-call | flops 100663296 | bytes 2097152 | tf_op jit(solution)/shard_map/pallas_call | solution.py:269
  (12 shorter events, 0.2 us)
Async XLA Ops:
  0.6 1.2 %copy-start = (f32[4096,64]{0,1:T(8,128)S(1)}, f32[4096,64]{0,1:T(8,128)}, u32[]{:S(2)}) copy-start(f32[4096,64]{0,1:T(8,128)} %param.3) | copy-start | bytes 3145732
  6.1 6.7 %collective-permute-start = (f32[192,128]{1,0:T(8,128)S(1)}, f32[192,128]{1,0:T(8,128)S(1)}, u32[]{:S(2)}, u32[]{:S(2)}) collective-permute-start(f32[192,128]{1,0:T(8,128)S(1)} %get-tuple-element.13), channel_id=1, source_target_pairs={{0,1},{1,0},{2,3},{3,2},{4,5},{5,4},{6,7},{7,6},{8,9},{9,8},{10,11... | collective-permute-start | bytes 294920 | tf_op jit(solution)/shard_map/ppermute | solution.py:280
  12.9 7.9 %collective-permute-start.1 = (f32[192,128]{1,0:T(8,128)S(1)}, f32[192,128]{1,0:T(8,128)S(1)}, u32[]{:S(2)}, u32[]{:S(2)}) collective-permute-start(f32[192,128]{1,0:T(8,128)S(1)} %add.30), channel_id=1, source_target_pairs={{0,2},{1,3},{2,0},{3,1},{4,6},{5,7},{6,4},{7,5},{8,10},{9,11},{10,... | collective-permute-start | bytes 294920 | tf_op jit(solution)/shard_map/ppermute | solution.py:280
  20.8 8.4 %collective-permute-start.2 = (f32[192,128]{1,0:T(8,128)S(1)}, f32[192,128]{1,0:T(8,128)S(1)}, u32[]{:S(2)}, u32[]{:S(2)}) collective-permute-start(f32[192,128]{1,0:T(8,128)S(1)} %add.31), channel_id=1, source_target_pairs={{0,7},{1,6},{2,5},{3,4},{4,3},{5,2},{6,1},{7,0},{8,15},{9,14},{10,... | collective-permute-start | bytes 294920 | tf_op jit(solution)/shard_map/ppermute | solution.py:280
  29.2 3.9 %collective-permute-start.3 = (f32[192,128]{1,0:T(8,128)S(1)}, f32[192,128]{1,0:T(8,128)S(1)}, u32[]{:S(2)}, u32[]{:S(2)}) collective-permute-start(f32[192,128]{1,0:T(8,128)S(1)} %add.32.sample_ref.other_ref.own_ref), channel_id=1, source_target_pairs={{0,1},{1,0},{2,3},{3,2},{4,5},{5,4},{6,7},{7,6},{8,9},{9,8},{10,11... | collective-permute-start | bytes 294920 | tf_op jit(solution)/shard_map/ppermute | solution.py:280
  34.3 3.1 %collective-permute-start.4 = (f32[17,64,128]{2,1,0:T(8,128)S(1)}, f32[17,64,128]{2,1,0:T(8,128)S(1)}, u32[]{:S(2)}, u32[]{:S(2)}) collective-permute-start(f32[17,64,128]{2,1,0:T(8,128)S(1)} %get-tuple-element.17), channel_id=1, source_target_pairs={{0,8},{8,0},{16,24},{24,16},{32,40},{40,32},{48,56},{56,48},{64,72... | collective-permute-start | bytes 1671176 | tf_op jit(solution)/shard_map/ppermute | solution.py:284
  37.5 5.8 %collective-permute-start.7 = (f32[5,64,128]{2,1,0:T(8,128)S(1)}, f32[5,64,128]{2,1,0:T(8,128)S(1)}, u32[]{:S(2)}, u32[]{:S(2)}) collective-permute-start(f32[5,64,128]{2,1,0:T(8,128)S(1)} %concatenate.20), channel_id=1, source_target_pairs={{0,192},{8,56},{16,208},{24,40},{32,224},{40,24},{48,240},{56,8},{... | collective-permute-start | bytes 491528 | tf_op jit(solution)/shard_map/ppermute | solution.py:284
  40.4 4.6 %collective-permute-start.5 = (f32[5,64,128]{2,1,0:T(8,128)S(1)}, f32[5,64,128]{2,1,0:T(8,128)S(1)}, u32[]{:S(2)}, u32[]{:S(2)}) collective-permute-start(f32[5,64,128]{2,1,0:T(8,128)S(1)} %get-tuple-element.23), channel_id=1, source_target_pairs={{0,64},{8,24},{16,80},{24,8},{32,96},{40,56},{48,112},{56,40},{64,... | collective-permute-start | bytes 491528 | tf_op jit(solution)/shard_map/ppermute | solution.py:284
  40.5 6.2 %collective-permute-start.6 = (f32[5,64,128]{2,1,0:T(8,128)S(1)}, f32[5,64,128]{2,1,0:T(8,128)S(1)}, u32[]{:S(2)}, u32[]{:S(2)}) collective-permute-start(f32[5,64,128]{2,1,0:T(8,128)S(1)} %get-tuple-element.24), channel_id=1, source_target_pairs={{0,128},{8,40},{16,144},{24,56},{32,160},{40,8},{48,176},{56,24},{... | collective-permute-start | bytes 491528 | tf_op jit(solution)/shard_map/ppermute | solution.py:284
  46.8 6.6 %collective-permute-start.10 = (f32[5,64,128]{2,1,0:T(8,128)S(1)}, f32[5,64,128]{2,1,0:T(8,128)S(1)}, u32[]{:S(2)}, u32[]{:S(2)}) collective-permute-start(f32[5,64,128]{2,1,0:T(8,128)S(1)} %fusion.2), channel_id=1, source_target_pairs={{0,48},{8,200},{16,32},{24,216},{32,16},{40,232},{48,0},{56,248},{... | collective-permute-start | bytes 491528 | tf_op jit(solution)/shard_map/ppermute | solution.py:284
  49.3 5.7 %collective-permute-start.9 = (f32[5,64,128]{2,1,0:T(8,128)S(1)}, f32[5,64,128]{2,1,0:T(8,128)S(1)}, u32[]{:S(2)}, u32[]{:S(2)}) collective-permute-start(f32[5,64,128]{2,1,0:T(8,128)S(1)} %fusion.2), channel_id=1, source_target_pairs={{0,32},{8,136},{16,48},{24,152},{32,0},{40,168},{48,16},{56,184},{... | collective-permute-start | bytes 491528 | tf_op jit(solution)/shard_map/ppermute | solution.py:284
  49.6 5.5 %collective-permute-start.8 = (f32[5,64,128]{2,1,0:T(8,128)S(1)}, f32[5,64,128]{2,1,0:T(8,128)S(1)}, u32[]{:S(2)}, u32[]{:S(2)}) collective-permute-start(f32[5,64,128]{2,1,0:T(8,128)S(1)} %fusion.2), channel_id=1, source_target_pairs={{0,16},{8,72},{16,0},{24,88},{32,48},{40,104},{48,32},{56,120},{64... | collective-permute-start | bytes 491528 | tf_op jit(solution)/shard_map/ppermute | solution.py:284
  55.1 8.8 %collective-permute-start.13 = (f32[4,64,128]{2,1,0:T(8,128)S(1)}, f32[4,64,128]{2,1,0:T(8,128)S(1)}, u32[]{:S(2)}, u32[]{:S(2)}) collective-permute-start(f32[4,64,128]{2,1,0:T(8,128)S(1)} %slice.30), channel_id=1, source_target_pairs={{0,192},{8,56},{16,208},{24,40},{32,224},{40,24},{48,240},{56,8},{... | collective-permute-start | bytes 393224 | tf_op jit(solution)/shard_map/ppermute | solution.py:284
  57.7 6.2 %collective-permute-start.12 = (f32[4,64,128]{2,1,0:T(8,128)S(1)}, f32[4,64,128]{2,1,0:T(8,128)S(1)}, u32[]{:S(2)}, u32[]{:S(2)}) collective-permute-start(f32[4,64,128]{2,1,0:T(8,128)S(1)} %slice.30), channel_id=1, source_target_pairs={{0,128},{8,40},{16,144},{24,56},{32,160},{40,8},{48,176},{56,24},{... | collective-permute-start | bytes 393224 | tf_op jit(solution)/shard_map/ppermute | solution.py:284
  58.1 5.8 %collective-permute-start.11 = (f32[4,64,128]{2,1,0:T(8,128)S(1)}, f32[4,64,128]{2,1,0:T(8,128)S(1)}, u32[]{:S(2)}, u32[]{:S(2)}) collective-permute-start(f32[4,64,128]{2,1,0:T(8,128)S(1)} %slice.30), channel_id=1, source_target_pairs={{0,64},{8,24},{16,80},{24,8},{32,96},{40,56},{48,112},{56,40},{64,... | collective-permute-start | bytes 393224 | tf_op jit(solution)/shard_map/ppermute | solution.py:284
  63.9 5.4 %collective-permute-start.14 = (f32[16,64,128]{2,1,0:T(8,128)S(1)}, f32[16,64,128]{2,1,0:T(8,128)S(1)}, u32[]{:S(2)}, u32[]{:S(2)}) collective-permute-start(f32[16,64,128]{2,1,0:T(8,128)S(1)} %pad_maximum_fusion.own_ref), channel_id=1, source_target_pairs={{0,8},{8,0},{16,24},{24,16},{32,40},{40,32},{48,56},{56,48},{64,72... | collective-permute-start | bytes 1572872 | tf_op jit(solution)/shard_map/ppermute | solution.py:284

commit v3 on v2

v3 whole, which is shorter than its diff:
```python
import functools
import math

import jax
import jax.numpy as jnp
from jax import lax
from jax.experimental import pallas as pl
from jax.experimental.pallas import tpu as pltpu
from jax.sharding import PartitionSpec as P

F32 = jnp.float32
BF16 = jnp.bfloat16
VMEM = pltpu.VMEM
MIB = 2**20
K = 64
LANES = 128
QUARTERS = 4
CHUNKS = 2
BLOCKS = 32
GROUPS = 8
PER_GROUP = 4


def split(value):
    high = value.astype(BF16)
    return high, (value - high.astype(F32)).astype(BF16)


def own_quarter():
    z = lax.axis_index("col")
    return jnp.where(z < QUARTERS, z, 2 * QUARTERS - 1 - z)


def position():
    row = lax.axis_index("row")
    core, y, x = row % 2, (row // 2) % 4, row // 8
    return core, jnp.where(core == 0, x, y), jnp.where(core == 0, y, x)


def group_place(group):
    core, first, second = position()
    if group < PER_GROUP:
        return core * PER_GROUP + (first ^ group)
    return (1 - core) * PER_GROUP + (second ^ (group - PER_GROUP))


def vmem(count):
    return [pl.BlockSpec(memory_space=VMEM)] * count


def unpacked(value):
    return jnp.concatenate([value[:, :K], value[:, K:]], axis=0)


def sample_quarters(data_ref, masks, weights, outs, terms_ref, data, sems, prepare):
    chunk = data.shape[1]
    rows = CHUNKS * chunk
    mine = own_quarter()
    copies = []
    for i in range(len(masks) * CHUNKS):
        start = pl.multiple_of((mine ^ masks[i // CHUNKS]) * rows + i % CHUNKS * chunk, chunk)
        copies.append(pltpu.make_async_copy(data_ref.at[pl.ds(start, chunk)], data.at[i], sems.at[i]))
        copies[i].start()
    prepare()
    lane = lax.broadcasted_iota(jnp.int32, (chunk, LANES), 1)
    for q in range(len(masks)):
        totals = []
        for i in range(CHUNKS):
            at = q * CHUNKS + i
            copies[at].wait()
            high, low = split(data[at])
            terms_ref[pl.ds(2 * q * rows + i * chunk, chunk), :] = high
            terms_ref[pl.ds((2 * q + 1) * rows + i * chunk, chunk), :] = low
            total = jnp.dot(high, weights[...], preferred_element_type=F32)
            total += jnp.dot(low, weights[...], preferred_element_type=F32)
            totals.append(total + pltpu.roll(total, K, axis=1))
        outs[q][...] = jnp.where(lane < K, totals[0], totals[1])


SENT = (3, 2, 1)


def send_kernel(data_ref, sketch_ref, out3, out2, out1, terms_ref, weights_ref, data, sketch, sems):
    load = pltpu.make_async_copy(sketch_ref, sketch, sems.at[len(SENT) * CHUNKS])
    load.start()

    def prepare():
        load.wait()
        high, low = split(sketch[...].T)
        weights_ref[...] = jnp.concatenate([high, low], axis=1)

    sample_quarters(data_ref, SENT, weights_ref, (out3, out2, out1), terms_ref, data, sems, prepare)


def keep_kernel(data_ref, weights_ref, out_ref, terms_ref, data, sems):
    sample_quarters(data_ref, (0,), weights_ref, (out_ref,), terms_ref, data, sems, lambda: None)


def partial_samples(data_slab, sketch_t):
    rows, columns = data_slab.shape
    quarter = rows // QUARTERS
    chunk = quarter // CHUNKS
    sample = jax.ShapeDtypeStruct((chunk, LANES), F32)

    def cost(count):
        return pl.CostEstimate(
            flops=8 * count * quarter * columns * K, bytes_accessed=4 * count * quarter * columns, transcendentals=0
        )

    def scratch(count):
        return [VMEM((count * CHUNKS, chunk, columns), F32)]

    *sent, sent_terms, weights = pl.pallas_call(
        send_kernel,
        out_shape=[sample] * len(SENT)
        + [
            jax.ShapeDtypeStruct((2 * len(SENT) * quarter, columns), BF16),
            jax.ShapeDtypeStruct((columns, LANES), BF16),
        ],
        in_specs=[pl.BlockSpec(memory_space=pl.ANY)] * 2,
        out_specs=vmem(len(SENT) + 2),
        scratch_shapes=scratch(len(SENT))
        + [VMEM((K, columns), F32), pltpu.SemaphoreType.DMA((len(SENT) * CHUNKS + 1,))],
        compiler_params=pltpu.CompilerParams(vmem_limit_bytes=42 * MIB),
        cost_estimate=cost(len(SENT)),
    )(data_slab, sketch_t)
    kept, kept_terms = pl.pallas_call(
        keep_kernel,
        out_shape=[sample, jax.ShapeDtypeStruct((2 * quarter, columns), BF16)],
        in_specs=[pl.BlockSpec(memory_space=pl.ANY)] + vmem(1),
        out_specs=vmem(2),
        scratch_shapes=scratch(1) + [pltpu.SemaphoreType.DMA((CHUNKS,))],
        compiler_params=pltpu.CompilerParams(vmem_limit_bytes=40 * MIB),
        cost_estimate=cost(1),
    )(data_slab, weights)
    return sent, sent_terms, kept, kept_terms


def left_of(sample):
    high, low = split(unpacked(sample).T)
    left = jnp.concatenate([high, low], axis=0)
    return left, jnp.concatenate([left, left], axis=1)


def first_term_kernel(own_ref, sample_ref, kept_ref, sent_ref, out_ref):
    _, left = left_of(own_ref[...])
    _, other = left_of(sample_ref[...])
    size = kept_ref.shape[0]
    width = out_ref.shape[1] // GROUPS
    for g in range(GROUPS):
        at = pl.ds(g * width, width)
        total = jnp.dot(left, kept_ref[:, at], preferred_element_type=F32)
        total += jnp.dot(other, sent_ref[:size, at], preferred_element_type=F32)
        out_ref[:, at] = total[:K] + total[K:]


def second_term_kernel(s0, s3, s2, s1, sent_ref, begun_ref, keep_ref, send_ref):
    singles, lefts = zip(*[left_of(ref[...]) for ref in (s2, s1, s0, s3)])
    left = jnp.concatenate(lefts[:2], axis=1)
    every = jnp.concatenate(singles, axis=1)
    gram = lax.dot_general(every, every, (((1,), (1,)), ((), ())), preferred_element_type=F32)
    gram = gram[:K] + gram[K:]
    gram = gram + pltpu.roll(gram, K, axis=1)
    lane = lax.broadcasted_iota(jnp.int32, (K // 2, LANES), 1)
    gram = jnp.where(lane < K, gram[: K // 2], gram[K // 2 :])
    keep_ref[BLOCKS // 2 * K :, :] = gram
    send_ref[BLOCKS // 2 * K :, :] = gram
    size = left.shape[1]
    width = PER_GROUP * LANES
    for g in (4, 5, 6, 7, 0, 1, 2, 3):
        at = pl.ds(pl.multiple_of(group_place(g) * width, width), width)
        total = jnp.dot(left, sent_ref[size // 2 :, at], preferred_element_type=F32)
        total = total[:K] + total[K:] + begun_ref[:, at]
        out_ref, base = (keep_ref, g) if g < PER_GROUP else (send_ref, g - PER_GROUP)
        for t in range(PER_GROUP):
            out_ref[pl.ds((base * PER_GROUP + t) * K, K), :] = total[:, t * LANES : (t + 1) * LANES]


def term_cost(rows, columns):
    return pl.CostEstimate(flops=8 * K * rows * columns, bytes_accessed=4 * rows * columns, transcendentals=0)


def first_terms(own, third, kept_terms, sent_terms):
    size, columns = kept_terms.shape
    return pl.pallas_call(
        first_term_kernel,
        out_shape=jax.ShapeDtypeStruct((K, columns), F32),
        in_specs=vmem(4),
        out_specs=vmem(1)[0],
        compiler_params=pltpu.CompilerParams(vmem_limit_bytes=16 * MIB),
        cost_estimate=term_cost(size, columns),
    )(own, third, kept_terms, sent_terms)


def second_terms(quarters, sent_terms, begun):
    size, columns = sent_terms.shape
    return pl.pallas_call(
        second_term_kernel,
        out_shape=[jax.ShapeDtypeStruct((BLOCKS // 2 * K + K // 2, LANES), F32)] * 2,
        in_specs=vmem(len(quarters) + 2),
        out_specs=vmem(2),
        compiler_params=pltpu.CompilerParams(vmem_limit_bytes=16 * MIB),
        cost_estimate=term_cost(size // 3, columns),
    )(*quarters, sent_terms, begun)


def inverse_kernel(gram_ref, inverse_ref):
    lane = lax.broadcasted_iota(jnp.int32, (K // 2, LANES), 1)
    row = lax.broadcasted_iota(jnp.int32, (K // 2, LANES), 0)
    upper = gram_ref[...]
    lower = pltpu.roll(upper, K, axis=1)
    work = jnp.concatenate(
        [
            jnp.where(lane < K, upper, jnp.where(lane == row + K, 1.0, 0.0)),
            jnp.where(lane < K, lower, jnp.where(lane == row + K + K // 2, 1.0, 0.0)),
        ],
        axis=0,
    )
    count = K // 8
    parts = [work[8 * i : 8 * i + 8] for i in range(count)]
    sub = lax.broadcasted_iota(jnp.int32, (8, LANES), 0)
    diagonal = [jnp.ones((8, LANES), F32)] * count

    def full(value):
        return jnp.broadcast_to(value, (8, LANES))

    for j in range(0, K, 4):
        block, at = divmod(j, 8)
        own = parts[block]
        c1, c2, c3, c4 = [[full(parts[i][:, j + c : j + c + 1]) for i in range(block, count)] for c in range(4)]
        r1, r2, r3, r4 = [full(own[at + r : at + r + 1]) for r in range(4)]
        a11, a12, a13, a14 = [full(c[0][at : at + 1]) for c in (c1, c2, c3, c4)]
        a22, a23, a24 = [full(c[0][at + 1 : at + 2]) for c in (c2, c3, c4)]
        a33, a34 = [full(c[0][at + 2 : at + 3]) for c in (c3, c4)]
        a44 = full(c4[0][at + 3 : at + 4])
        first = a11 * a22 - a12 * a12
        scale = 1.0 / first
        l31, l32 = (a22 * a13 - a12 * a23) * scale, (a11 * a23 - a12 * a13) * scale
        l41, l42 = (a22 * a14 - a12 * a24) * scale, (a11 * a24 - a12 * a14) * scale
        s33 = a33 - (l31 * a13 + l32 * a23)
        s34 = a34 - (l31 * a14 + l32 * a24)
        s44 = a44 - (l41 * a14 + l42 * a24)
        r3 = r3 - (l31 * r1 + l32 * r2)
        r4 = r4 - (l41 * r1 + l42 * r2)
        second = s33 * s44 - s34 * s34
        again = 1.0 / second
        v1, v2 = (a22 * r1 - a12 * r2) * scale, (a11 * r2 - a12 * r1) * scale
        v3, v4 = (s44 * r3 - s34 * r4) * again, (s33 * r4 - s34 * r3) * again
        p1, p3 = 1.0 / a11, 1.0 / s33
        rows = (r2 - a12 * p1 * r1, r3, r4 - s34 * p3 * r3)
        diag = (a11, first * p1, s33, second * p3)
        for r in range(4):
            diagonal[block] = jnp.where(sub == at + r, diag[r], diagonal[block])
        for i in range(block, count):
            f1, f2, f3, f4 = [c[i - block] for c in (c1, c2, c3, c4)]
            f3 = f3 - (f1 * l31 + f2 * l32)
            f4 = f4 - (f1 * l41 + f2 * l42)
            new = parts[i] - ((f1 * v1 + f2 * v2) + (f3 * v3 + f4 * v4))
            if i == block:
                new = jnp.where(sub > at + 3, new, own)
                for r in range(3):
                    new = jnp.where(sub == at + 1 + r, rows[r], new)
            parts[i] = new
    parts = [part * (1.0 / jnp.sqrt(diag)) for part, diag in zip(parts, diagonal)]
    inverse_ref[...] = jnp.concatenate(parts, axis=0)[:, K:]


def inverse_of(gram):
    return pl.pallas_call(
        inverse_kernel,
        out_shape=jax.ShapeDtypeStruct((K, K), F32),
        in_specs=vmem(1),
        out_specs=vmem(1)[0],
        compiler_params=pltpu.CompilerParams(vmem_limit_bytes=8 * MIB),
        cost_estimate=pl.CostEstimate(flops=K**3 * 100, bytes_accessed=8 * K * K, transcendentals=K),
    )(gram)


def basis_kernel(scale, inverse_ref, s0, s3, s2, s1, basis_ref, sample):
    half = s0.shape[0]
    mine = own_quarter()
    for mask, ref in ((0, s0), (3, s3), (2, s2), (1, s1)):
        start = pl.multiple_of((mine ^ mask) * 2 * half, 2 * half)
        sample[pl.ds(start, half), :] = ref[:, :K]
        sample[pl.ds(start + half, half), :] = ref[:, K:]
    basis_ref[...] = lax.dot_general(
        inverse_ref[...] * scale,
        sample[...],
        (((1,), (1,)), ((), ())),
        precision=lax.Precision.HIGHEST,
        preferred_element_type=F32,
    )


def basis_of(inverse, quarters, rows, scale):
    return pl.pallas_call(
        functools.partial(basis_kernel, scale),
        out_shape=jax.ShapeDtypeStruct((K, rows), F32),
        in_specs=vmem(1 + len(quarters)),
        out_specs=vmem(1)[0],
        scratch_shapes=[VMEM((rows, K), F32)],
        compiler_params=pltpu.CompilerParams(vmem_limit_bytes=8 * MIB),
        cost_estimate=pl.CostEstimate(flops=12 * rows * K * K, bytes_accessed=8 * rows * K, transcendentals=0),
    )(inverse, *quarters)


def apply_kernel(first_group, inverse_ref, value_ref, *refs):
    out_ref, parts, sems = refs[-3:]
    high, low = split(inverse_ref[...])
    left = jnp.concatenate([high, low, high], axis=1)
    width = PER_GROUP * LANES
    copies = []
    for g in range(PER_GROUP):
        rows = [value_ref[pl.ds((g * PER_GROUP + t) * K, K), :] for t in range(PER_GROUP)]
        high, low = split(jnp.concatenate(rows, axis=1))
        right = jnp.concatenate([high, high, low], axis=0)
        parts[g] = jnp.dot(left, right, preferred_element_type=F32)
        at = pl.ds(pl.multiple_of(group_place(first_group + g) * width, width), width)
        copies.append(pltpu.make_async_copy(parts.at[g], out_ref.at[:, at], sems.at[g]))
        copies[g].start()
    for copy in copies:
        copy.wait()


def applied(first_group, inverse, value, begun=None):
    columns = BLOCKS * LANES
    more = [] if begun is None else [begun]
    return pl.pallas_call(
        functools.partial(apply_kernel, first_group),
        out_shape=jax.ShapeDtypeStruct((K, columns), F32),
        in_specs=vmem(2) + [pl.BlockSpec(memory_space=pl.ANY)] * len(more),
        out_specs=pl.BlockSpec(memory_space=pl.ANY),
        input_output_aliases={2: 0} if more else {},
        scratch_shapes=[VMEM((PER_GROUP, K, PER_GROUP * LANES), F32), pltpu.SemaphoreType.DMA((PER_GROUP,))],
        compiler_params=pltpu.CompilerParams(vmem_limit_bytes=8 * MIB),
        cost_estimate=pl.CostEstimate(flops=3 * columns * K * K, bytes_accessed=4 * columns * K, transcendentals=0),
    )(inverse, value, *more)


def along_col(value, mask):
    return lax.ppermute(value, "col", [(i, i ^ mask) for i in range(8)])


def along_row(value, masks):
    return lax.ppermute(value, "row", [(i, i ^ masks[i % 2]) for i in range(32)])


CORE = (1, 1)
FIRST = [(t << 3, t << 1) for t in range(4)]
SECOND = [(t << 1, t << 3) for t in range(4)]


def body(data_slab, sketch):
    rows = data_slab.shape[0]
    sent, sent_terms, kept, kept_terms = partial_samples(data_slab, sketch.T)
    got = [along_col(part, mask) for part, mask in zip(sent, SENT)]
    own = kept + got[0] + got[1] + got[2]
    own = own + along_col(own, 7)
    quarters = [own] + [along_col(own, mask) for mask in SENT]

    begun = first_terms(own, quarters[1], kept_terms, sent_terms)
    keep, send = second_terms(quarters, sent_terms, begun)
    total = keep + along_row(send, CORE)
    size = PER_GROUP * K
    gram = total[4 * size :]
    got = [along_row(jnp.concatenate([total[t * size : (t + 1) * size], gram]), FIRST[t]) for t in (1, 2, 3)]
    total = jnp.concatenate([total[:size], gram]) + got[0] + got[1] + got[2]
    got = [along_row(total, SECOND[t]) for t in (1, 2, 3)]
    total = total + got[0] + got[1] + got[2]

    inverse = inverse_of(total[size:])
    block = total[:size]
    mine = jnp.concatenate([block] + [along_row(block, FIRST[t]) for t in (1, 2, 3)])
    range_basis = basis_of(inverse, quarters, rows, math.sqrt(rows * lax.axis_size("row")))
    mine, inverse, range_basis = lax.optimization_barrier((mine, inverse, range_basis))
    theirs = along_row(mine, CORE)
    projected = applied(PER_GROUP, inverse, theirs, applied(0, inverse, mine))
    return range_basis.T, projected


def solution(mesh):
    placed = (P("row", "col"), P("col", None))
    return jax.shard_map(
        body,
        mesh=mesh,
        in_specs=placed,
        out_specs=(P("row", None), P(None, "col")),
        check_vma=False,
    )
```

time: 70.9 us -> 69.1 us (0.975)
  waiting for transfers between devices: 23.6 us -> 16.2 us
  starting transfers between devices: 26 us -> 32.9 us
  Pallas kernels: 18.8 us -> 17.4 us
    ppermute x4 -> x7, waiting for transfers between devices: 11.8 us -> 4.1 us  [along_col(): return lax.ppermute(value, 'col', [(i, i ^ mask) for i in range(8)])]
    ppermute x4 -> x7, starting transfers between devices: 9.82 us -> 13.9 us  [along_col(): return lax.ppermute(value, 'col', [(i, i ^ mask) for i in range(8)])]
    ppermute x11, starting transfers between devices: 16.2 us -> 19 us  [along_row(): lax.ppermute(value, 'row', [(i, i ^ masks[i % 2]) for i in range(32)])]
    pallas_call x1, Pallas kernels: 5.45 us -> 2.67 us  [inverse_of(): pl.pallas_call(inverse_kernel, out_shape=jax.ShapeDtypeStruct((K, K), F32...]
    pallas_call x4 -> x5, Pallas kernels: 10.9 us -> 12 us  [the longest x1 5.61 us: partial_samples(): pl.pallas_call(send_kernel, out_shape=[sample] * len(SENT) + [jax.ShapeDt...]
  transfers between devices with their start and end apart: 15 -> 18, of which waited for: 10 -> 11; matrix products, arithmetic and copies ran while one was open for 0% -> 0% of each run, Pallas kernels for 17% -> 14%
where the time goes in v3:
time: 69.1 us; the launch traced here: 68.9 us
  starting transfers between devices  32.9 us (48%)
  Pallas kernels  17.4 us (25%)
  waiting for transfers between devices  16.2 us (23%)
  local copies, waits for them, and re-layouts  1.27 us (2%)
  between operations  0.94 us (1%)
    ppermute x11, starting transfers between devices, along_row(): lax.ppermute(value, 'row', [(i, i ^ masks[i % 2]) for i in range(32)])  19 us
    ppermute x7, starting transfers between devices, along_col(): return lax.ppermute(value, 'col', [(i, i ^ mask) for i in range(8)])  13.9 us
    ppermute x11, waiting for transfers between devices, along_row(): lax.ppermute(value, 'row', [(i, i ^ masks[i % 2]) for i in range(32)])  12.1 us
    pallas_call x1, Pallas kernels, partial_samples(): pl.pallas_call(send_kernel, out_shape=[sample] * len(SENT) + [jax.ShapeDt...  5.61 us
    ppermute x7, waiting for transfers between devices, along_col(): return lax.ppermute(value, 'col', [(i, i ^ mask) for i in range(8)])  4.1 us
    pallas_call x1, Pallas kernels, partial_samples(): pl.pallas_call(keep_kernel, out_shape=[sample, jax.ShapeDtypeStruct((2 *...  2.78 us
    pallas_call x1, Pallas kernels, inverse_of(): pl.pallas_call(inverse_kernel, out_shape=jax.ShapeDtypeStruct((K, K), F32...  2.67 us
    pallas_call x2, Pallas kernels, applied(): pl.pallas_call(functools.partial(apply_kernel, first_group), out_shape=ja...  2.06 us
  transfers between devices with their start and end apart: 18, of which 11 were waited for; matrix products, arithmetic and copies ran while one was open for 0% of the time, Pallas kernels for 14%

profile of v3, /device:TPU:1, one launch (start us, length us, event | category | flops | bytes accessed | tf_op | source)
XLA Modules:
  0.0 68.9 jit_solution(3985749123991842936)
XLA Ops:
  0.6 0.0 copy-start
  0.6 1.2 %copy-done = f32[4096,64]{0,1:T(8,128)S(1)} copy-done((f32[4096,64]{0,1:T(8,128)S(1)}, f32[4096,64]{0,1:T(8,128)}, u32[]{:S(2)}) %copy-start) | copy-done | bytes 1048600
  1.9 5.6 %shard_map.41 = (f32[96,128]{1,0:T(8,128)S(1)}, f32[96,128]{1,0:T(8,128)S(1)}, f32[96,128]{1,0:T(8,128)S(1)}, bf16[1152,4096]{1,0:T(8,128)(2,1)S(1)}, bf16[4096,128]{1,0:T(8,128)(2,1)S(1)}) custom-call(f32[768,4096]{1,0:T(8,128)} %data_ref.3, f32[64,4096]{1,0:T(8,128)S(1)} %bitcast.2), custom_call_target="tpu_custom_call" | custom-call | flops 1207959552 | bytes 9437184 | tf_op jit(solution)/shard_map/pallas_call | solution.py:113
  7.5 5.3 %collective-permute-start = (f32[96,128]{1,0:T(8,128)S(1)}, f32[96,128]{1,0:T(8,128)S(1)}, u32[]{:S(2)}, u32[]{:S(2)}) collective-permute-start(f32[96,128]{1,0:T(8,128)S(1)} %get-tuple-element.16), channel_id=1, source_target_pairs={{0,3},{1,2},{2,1},{3,0},{4,7},{5,6},{6,5},{7,4},{8,11},{9,10},{10,... | collective-permute-start | bytes 147464 | tf_op jit(solution)/shard_map/ppermute | solution.py:341
  12.7 0.0 collective-permute-start.1
  12.7 0.4 collective-permute-start.2
  13.1 2.8 %shard_map.42 = (f32[96,128]{1,0:T(8,128)S(1)}, bf16[384,4096]{1,0:T(8,128)(2,1)S(1)}) custom-call(f32[768,4096]{1,0:T(8,128)} %data_ref.3, bf16[4096,128]{1,0:T(8,128)(2,1)S(1)} %get-tuple-element.14.weights_ref), custom_call_target="tpu_custom_call" | custom-call | flops 402653184 | bytes 3145728 | tf_op jit(solution)/shard_map/pallas_call | solution.py:127
  15.9 0.0 collective-permute-done
  15.9 1.3 %collective-permute-done.1 = f32[96,128]{1,0:T(8,128)S(1)} collective-permute-done((f32[96,128]{1,0:T(8,128)S(1)}, f32[96,128]{1,0:T(8,128)S(1)}, u32[]{:S(2)}, u32[]{:S(2)}) %collective-permute-start.1) | collective-permute-done | bytes 49184 | tf_op jit(solution)/shard_map/ppermute | solution.py:341
  17.2 0.0 collective-permute-done.2
  17.2 4.6 %collective-permute-start.3 = (f32[96,128]{1,0:T(8,128)S(1)}, f32[96,128]{1,0:T(8,128)S(1)}, u32[]{:S(2)}, u32[]{:S(2)}) collective-permute-start(f32[96,128]{1,0:T(8,128)S(1)} %add_add_fusion.1), channel_id=1, source_target_pairs={{0,7},{1,6},{2,5},{3,4},{4,3},{5,2},{6,1},{7,0},{8,15},{9,14},{10,... | collective-permute-start | bytes 147464 | tf_op jit(solution)/shard_map/ppermute | solution.py:341
  21.8 1.5 %collective-permute-done.3 = f32[96,128]{1,0:T(8,128)S(1)} collective-permute-done((f32[96,128]{1,0:T(8,128)S(1)}, f32[96,128]{1,0:T(8,128)S(1)}, u32[]{:S(2)}, u32[]{:S(2)}) %collective-permute-start.3) | collective-permute-done | bytes 49184 | tf_op jit(solution)/shard_map/ppermute | solution.py:341
  23.3 1.7 %collective-permute-start.4 = (f32[96,128]{1,0:T(8,128)S(1)}, f32[96,128]{1,0:T(8,128)S(1)}, u32[]{:S(2)}, u32[]{:S(2)}) collective-permute-start(f32[96,128]{1,0:T(8,128)S(1)} %add.36.own_ref.s0), channel_id=1, source_target_pairs={{0,3},{1,2},{2,1},{3,0},{4,7},{5,6},{6,5},{7,4},{8,11},{9,10},{10,... | collective-permute-start | bytes 147464 | tf_op jit(solution)/shard_map/ppermute | solution.py:341
  25.0 0.0 collective-permute-start.6
  25.0 1.9 %collective-permute-start.5 = (f32[96,128]{1,0:T(8,128)S(1)}, f32[96,128]{1,0:T(8,128)S(1)}, u32[]{:S(2)}, u32[]{:S(2)}) collective-permute-start(f32[96,128]{1,0:T(8,128)S(1)} %add.36.own_ref.s0), channel_id=1, source_target_pairs={{0,2},{1,3},{2,0},{3,1},{4,6},{5,7},{6,4},{7,5},{8,10},{9,11},{10,... | collective-permute-start | bytes 147464 | tf_op jit(solution)/shard_map/ppermute | solution.py:341
  27.0 1.3 %collective-permute-done.4.sample_ref.s3 = f32[96,128]{1,0:T(8,128)S(1)} collective-permute-done((f32[96,128]{1,0:T(8,128)S(1)}, f32[96,128]{1,0:T(8,128)S(1)}, u32[]{:S(2)}, u32[]{:S(2)}) %collective-permute-start.4) | collective-permute-done | bytes 49184 | tf_op jit(solution)/shard_map/ppermute | solution.py:341
  28.3 1.6 %shard_map.43.begun_ref = f32[64,4096]{1,0:T(8,128)S(1)} custom-call(f32[96,128]{1,0:T(8,128)S(1)} %add.36.own_ref.s0, f32[96,128]{1,0:T(8,128)S(1)} %collective-permute-done.4.sample_ref.s3, bf16[384,4096]{1,0:T(8,128)(2,1)S(1)} %get-tuple-element.20.kept_ref, bf16[1152,4096]{1,0:T(8,128)(2,1)S(1)} %get-tuple-element.19.sent_ref), custom_call_target="tpu_custom_call" | custom-call | flops 805306368 | bytes 6291456 | tf_op jit(solution)/shard_map/pallas_call | solution.py:185
  29.8 0.0 collective-permute-done.6.s1
  29.8 0.0 collective-permute-done.5.s2
  29.8 1.4 %shard_map.44 = (f32[1056,128]{1,0:T(8,128)S(1)}, f32[1056,128]{1,0:T(8,128)S(1)}) custom-call(f32[96,128]{1,0:T(8,128)S(1)} %add.36.own_ref.s0, f32[96,128]{1,0:T(8,128)S(1)} %collective-permute-done.4.sample_ref.s3, f32[96,128]{1,0:T(8,128)S(1)} %collective-permute-done.5.s2, f32[96,128]{1,0:T(8,128)S(1)} %collective-permute-done.6.s1, ...), custom_call_target="tpu_custom_call" | custom-call | flops 805306368 | bytes 6291456 | tf_op jit(solution)/shard_map/pallas_call | solution.py:197
  31.2 4.0 %collective-permute-start.7 = (f32[1056,128]{1,0:T(8,128)S(1)}, f32[1056,128]{1,0:T(8,128)S(1)}, u32[]{:S(2)}, u32[]{:S(2)}) collective-permute-start(f32[1056,128]{1,0:T(8,128)S(1)} %get-tuple-element.22), channel_id=1, source_target_pairs={{0,8},{8,0},{16,24},{24,16},{32,40},{40,32},{48,56},{56,48},{64,72... | collective-permute-start | bytes 1622024 | tf_op jit(solution)/shard_map/ppermute | solution.py:345
  35.3 1.6 %collective-permute-done.7 = f32[1056,128]{1,0:T(8,128)S(1)} collective-permute-done((f32[1056,128]{1,0:T(8,128)S(1)}, f32[1056,128]{1,0:T(8,128)S(1)}, u32[]{:S(2)}, u32[]{:S(2)}) %collective-permute-start.7) | collective-permute-done | bytes 540704 | tf_op jit(solution)/shard_map/ppermute | solution.py:345
  36.8 0.1 add.37
  36.9 2.8 %collective-permute-start.10 = (f32[288,128]{1,0:T(8,128)S(1)}, f32[288,128]{1,0:T(8,128)S(1)}, u32[]{:S(2)}, u32[]{:S(2)}) collective-permute-start(f32[288,128]{1,0:T(8,128)S(1)} %concatenate.20), channel_id=1, source_target_pairs={{0,192},{8,56},{16,208},{24,40},{32,224},{40,24},{48,240},{56,8},{... | collective-permute-start | bytes 442376 | tf_op jit(solution)/shard_map/ppermute | solution.py:345
  39.8 0.1 collective-permute-start.8
  39.9 1.2 %collective-permute-start.9 = (f32[288,128]{1,0:T(8,128)S(1)}, f32[288,128]{1,0:T(8,128)S(1)}, u32[]{:S(2)}, u32[]{:S(2)}) collective-permute-start(f32[288,128]{1,0:T(8,128)S(1)} %get-tuple-element.30), channel_id=1, source_target_pairs={{0,128},{8,40},{16,144},{24,56},{32,160},{40,8},{48,176},{56,24},{... | collective-permute-start | bytes 442376 | tf_op jit(solution)/shard_map/ppermute | solution.py:345
  41.1 1.5 %collective-permute-done.10 = f32[288,128]{1,0:T(8,128)S(1)} collective-permute-done((f32[288,128]{1,0:T(8,128)S(1)}, f32[288,128]{1,0:T(8,128)S(1)}, u32[]{:S(2)}, u32[]{:S(2)}) %collective-permute-start.10) | collective-permute-done | bytes 147488 | tf_op jit(solution)/shard_map/ppermute | solution.py:345
  42.6 1.6 %collective-permute-done.8 = f32[288,128]{1,0:T(8,128)S(1)} collective-permute-done((f32[288,128]{1,0:T(8,128)S(1)}, f32[288,128]{1,0:T(8,128)S(1)}, u32[]{:S(2)}, u32[]{:S(2)}) %collective-permute-start.8) | collective-permute-done | bytes 147488 | tf_op jit(solution)/shard_map/ppermute | solution.py:345
  44.2 1.6 %collective-permute-done.9 = f32[288,128]{1,0:T(8,128)S(1)} collective-permute-done((f32[288,128]{1,0:T(8,128)S(1)}, f32[288,128]{1,0:T(8,128)S(1)}, u32[]{:S(2)}, u32[]{:S(2)}) %collective-permute-start.9) | collective-permute-done | bytes 147488 | tf_op jit(solution)/shard_map/ppermute | solution.py:345
  45.8 2.6 %collective-permute-start.13 = (f32[288,128]{1,0:T(8,128)S(1)}, f32[288,128]{1,0:T(8,128)S(1)}, u32[]{:S(2)}, u32[]{:S(2)}) collective-permute-start(f32[288,128]{1,0:T(8,128)S(1)} %fusion.2), channel_id=1, source_target_pairs={{0,48},{8,200},{16,32},{24,216},{32,16},{40,232},{48,0},{56,248},{... | collective-permute-start | bytes 442376 | tf_op jit(solution)/shard_map/ppermute | solution.py:345
  48.4 0.2 collective-permute-start.12
  48.6 0.6 collective-permute-start.11
  49.2 2.9 %collective-permute-done.13 = f32[288,128]{1,0:T(8,128)S(1)} collective-permute-done((f32[288,128]{1,0:T(8,128)S(1)}, f32[288,128]{1,0:T(8,128)S(1)}, u32[]{:S(2)}, u32[]{:S(2)}) %collective-permute-start.13) | collective-permute-done | bytes 147488 | tf_op jit(solution)/shard_map/ppermute | solution.py:345
  52.1 1.8 %collective-permute-done.12 = f32[288,128]{1,0:T(8,128)S(1)} collective-permute-done((f32[288,128]{1,0:T(8,128)S(1)}, f32[288,128]{1,0:T(8,128)S(1)}, u32[]{:S(2)}, u32[]{:S(2)}) %collective-permute-start.12) | collective-permute-done | bytes 147488 | tf_op jit(solution)/shard_map/ppermute | solution.py:345
  53.9 0.0 collective-permute-done.11
  53.9 2.7 %collective-permute-start.16 = (f32[256,128]{1,0:T(8,128)S(1)}, f32[256,128]{1,0:T(8,128)S(1)}, u32[]{:S(2)}, u32[]{:S(2)}) collective-permute-start(f32[256,128]{1,0:T(8,128)S(1)} %slice.30), channel_id=1, source_target_pairs={{0,192},{8,56},{16,208},{24,40},{32,224},{40,24},{48,240},{56,8},{... | collective-permute-start | bytes 393224 | tf_op jit(solution)/shard_map/ppermute | solution.py:345
  56.7 0.5 collective-permute-start.15
  57.2 0.2 collective-permute-start.14
  57.4 2.7 %shard_map.45.inverse_ref = f32[64,64]{1,0:T(8,128)S(1)} custom-call(f32[32,128]{1,0:T(8,128)S(1)} %slice.31.gram_ref), custom_call_target="tpu_custom_call" | custom-call | flops 26214400 | bytes 32768 | tf_op jit(solution)/shard_map/pallas_call | solution.py:269
  60.0 1.3 %shard_map.46 = f32[64,768]{1,0:T(8,128)} custom-call(f32[64,64]{1,0:T(8,128)S(1)} %shard_map.45.inverse_ref, f32[96,128]{1,0:T(8,128)S(1)} %add.36.own_ref.s0, f32[96,128]{1,0:T(8,128)S(1)} %collective-permute-done.4.sample_ref.s3, f32[96,128]{1,0:T(8,128)S(1)} %collective-permute-done.5.s2, f32[96,128]{1,0:T(8,128)S(1)} %collective-permute-done.6.s1), custom_call_target="tpu_custom_call" | custom-call | flops 37748736 | bytes 393216 | tf_op jit(solution)/shard_map/pallas_call | solution.py:296
  61.4 0.0 collective-permute-done.16
  61.4 0.6 collective-permute-done.15
  62.0 0.0 collective-permute-done.14
  62.0 4.2 %collective-permute-start.17 = (f32[1024,128]{1,0:T(8,128)S(1)}, f32[1024,128]{1,0:T(8,128)S(1)}, u32[]{:S(2)}, u32[]{:S(2)}) collective-permute-start(f32[1024,128]{1,0:T(8,128)S(1)} %pad_maximum_fusion.value_ref), channel_id=1, source_target_pairs={{0,8},{8,0},{16,24},{24,16},{32,40},{40,32},{48,56},{56,48},{64,72... | collective-permute-start | bytes 1572872 | tf_op jit(solution)/shard_map/ppermute | solution.py:345
  66.2 1.0 %shard_map.47.refs_0_ = f32[64,4096]{1,0:T(8,128)} custom-call(f32[64,64]{1,0:T(8,128)S(1)} %shard_map.45.inverse_ref, f32[1024,128]{1,0:T(8,128)S(1)} %pad_maximum_fusion.value_ref), custom_call_target="tpu_custom_call" | custom-call | flops 50331648 | bytes 1048576 | tf_op jit(solution)/shard_map/pallas_call | solution.py:328
  67.3 0.5 collective-permute-done.17.value_ref
  67.8 1.0 %shard_map.48 = f32[64,4096]{1,0:T(8,128)} custom-call(f32[64,64]{1,0:T(8,128)S(1)} %shard_map.45.inverse_ref, f32[1024,128]{1,0:T(8,128)S(1)} %collective-permute-done.17.value_ref, f32[64,4096]{1,0:T(8,128)} %shard_map.47.refs_0_), custom_call_target="tpu_custom_call", output_to_operand_aliasing={{}: (2, {})} | custom-call | flops 50331648 | bytes 1048576 | tf_op jit(solution)/shard_map/pallas_call | solution.py:328
  (11 shorter events, 0.2 us)
Async XLA Ops:
  0.6 1.2 %copy-start = (f32[4096,64]{0,1:T(8,128)S(1)}, f32[4096,64]{0,1:T(8,128)}, u32[]{:S(2)}) copy-start(f32[4096,64]{0,1:T(8,128)} %param.3) | copy-start | bytes 3145732
  7.5 8.4 %collective-permute-start = (f32[96,128]{1,0:T(8,128)S(1)}, f32[96,128]{1,0:T(8,128)S(1)}, u32[]{:S(2)}, u32[]{:S(2)}) collective-permute-start(f32[96,128]{1,0:T(8,128)S(1)} %get-tuple-element.16), channel_id=1, source_target_pairs={{0,3},{1,2},{2,1},{3,0},{4,7},{5,6},{6,5},{7,4},{8,11},{9,10},{10,... | collective-permute-start | bytes 147464 | tf_op jit(solution)/shard_map/ppermute | solution.py:341
  12.7 4.5 %collective-permute-start.1 = (f32[96,128]{1,0:T(8,128)S(1)}, f32[96,128]{1,0:T(8,128)S(1)}, u32[]{:S(2)}, u32[]{:S(2)}) collective-permute-start(f32[96,128]{1,0:T(8,128)S(1)} %get-tuple-element.17), channel_id=1, source_target_pairs={{0,2},{1,3},{2,0},{3,1},{4,6},{5,7},{6,4},{7,5},{8,10},{9,11},{10,... | collective-permute-start | bytes 147464 | tf_op jit(solution)/shard_map/ppermute | solution.py:341
  12.7 4.5 %collective-permute-start.2 = (f32[96,128]{1,0:T(8,128)S(1)}, f32[96,128]{1,0:T(8,128)S(1)}, u32[]{:S(2)}, u32[]{:S(2)}) collective-permute-start(f32[96,128]{1,0:T(8,128)S(1)} %get-tuple-element.18), channel_id=1, source_target_pairs={{0,1},{1,0},{2,3},{3,2},{4,5},{5,4},{6,7},{7,6},{8,9},{9,8},{10,11... | collective-permute-start | bytes 147464 | tf_op jit(solution)/shard_map/ppermute | solution.py:341
  17.2 6.1 %collective-permute-start.3 = (f32[96,128]{1,0:T(8,128)S(1)}, f32[96,128]{1,0:T(8,128)S(1)}, u32[]{:S(2)}, u32[]{:S(2)}) collective-permute-start(f32[96,128]{1,0:T(8,128)S(1)} %add_add_fusion.1), channel_id=1, source_target_pairs={{0,7},{1,6},{2,5},{3,4},{4,3},{5,2},{6,1},{7,0},{8,15},{9,14},{10,... | collective-permute-start | bytes 147464 | tf_op jit(solution)/shard_map/ppermute | solution.py:341
  23.3 4.9 %collective-permute-start.4 = (f32[96,128]{1,0:T(8,128)S(1)}, f32[96,128]{1,0:T(8,128)S(1)}, u32[]{:S(2)}, u32[]{:S(2)}) collective-permute-start(f32[96,128]{1,0:T(8,128)S(1)} %add.36.own_ref.s0), channel_id=1, source_target_pairs={{0,3},{1,2},{2,1},{3,0},{4,7},{5,6},{6,5},{7,4},{8,11},{9,10},{10,... | collective-permute-start | bytes 147464 | tf_op jit(solution)/shard_map/ppermute | solution.py:341
  25.0 4.8 %collective-permute-start.6 = (f32[96,128]{1,0:T(8,128)S(1)}, f32[96,128]{1,0:T(8,128)S(1)}, u32[]{:S(2)}, u32[]{:S(2)}) collective-permute-start(f32[96,128]{1,0:T(8,128)S(1)} %add.36.own_ref.s0), channel_id=1, source_target_pairs={{0,1},{1,0},{2,3},{3,2},{4,5},{5,4},{6,7},{7,6},{8,9},{9,8},{10,11... | collective-permute-start | bytes 147464 | tf_op jit(solution)/shard_map/ppermute | solution.py:341
  25.0 4.8 %collective-permute-start.5 = (f32[96,128]{1,0:T(8,128)S(1)}, f32[96,128]{1,0:T(8,128)S(1)}, u32[]{:S(2)}, u32[]{:S(2)}) collective-permute-start(f32[96,128]{1,0:T(8,128)S(1)} %add.36.own_ref.s0), channel_id=1, source_target_pairs={{0,2},{1,3},{2,0},{3,1},{4,6},{5,7},{6,4},{7,5},{8,10},{9,11},{10,... | collective-permute-start | bytes 147464 | tf_op jit(solution)/shard_map/ppermute | solution.py:341
  31.2 5.6 %collective-permute-start.7 = (f32[1056,128]{1,0:T(8,128)S(1)}, f32[1056,128]{1,0:T(8,128)S(1)}, u32[]{:S(2)}, u32[]{:S(2)}) collective-permute-start(f32[1056,128]{1,0:T(8,128)S(1)} %get-tuple-element.22), channel_id=1, source_target_pairs={{0,8},{8,0},{16,24},{24,16},{32,40},{40,32},{48,56},{56,48},{64,72... | collective-permute-start | bytes 1622024 | tf_op jit(solution)/shard_map/ppermute | solution.py:345
  36.9 5.7 %collective-permute-start.10 = (f32[288,128]{1,0:T(8,128)S(1)}, f32[288,128]{1,0:T(8,128)S(1)}, u32[]{:S(2)}, u32[]{:S(2)}) collective-permute-start(f32[288,128]{1,0:T(8,128)S(1)} %concatenate.20), channel_id=1, source_target_pairs={{0,192},{8,56},{16,208},{24,40},{32,224},{40,24},{48,240},{56,8},{... | collective-permute-start | bytes 442376 | tf_op jit(solution)/shard_map/ppermute | solution.py:345
  39.8 4.4 %collective-permute-start.8 = (f32[288,128]{1,0:T(8,128)S(1)}, f32[288,128]{1,0:T(8,128)S(1)}, u32[]{:S(2)}, u32[]{:S(2)}) collective-permute-start(f32[288,128]{1,0:T(8,128)S(1)} %get-tuple-element.29), channel_id=1, source_target_pairs={{0,64},{8,24},{16,80},{24,8},{32,96},{40,56},{48,112},{56,40},{64,... | collective-permute-start | bytes 442376 | tf_op jit(solution)/shard_map/ppermute | solution.py:345
  39.9 5.9 %collective-permute-start.9 = (f32[288,128]{1,0:T(8,128)S(1)}, f32[288,128]{1,0:T(8,128)S(1)}, u32[]{:S(2)}, u32[]{:S(2)}) collective-permute-start(f32[288,128]{1,0:T(8,128)S(1)} %get-tuple-element.30), channel_id=1, source_target_pairs={{0,128},{8,40},{16,144},{24,56},{32,160},{40,8},{48,176},{56,24},{... | collective-permute-start | bytes 442376 | tf_op jit(solution)/shard_map/ppermute | solution.py:345
  45.8 6.2 %collective-permute-start.13 = (f32[288,128]{1,0:T(8,128)S(1)}, f32[288,128]{1,0:T(8,128)S(1)}, u32[]{:S(2)}, u32[]{:S(2)}) collective-permute-start(f32[288,128]{1,0:T(8,128)S(1)} %fusion.2), channel_id=1, source_target_pairs={{0,48},{8,200},{16,32},{24,216},{32,16},{40,232},{48,0},{56,248},{... | collective-permute-start | bytes 442376 | tf_op jit(solution)/shard_map/ppermute | solution.py:345
  48.4 5.5 %collective-permute-start.12 = (f32[288,128]{1,0:T(8,128)S(1)}, f32[288,128]{1,0:T(8,128)S(1)}, u32[]{:S(2)}, u32[]{:S(2)}) collective-permute-start(f32[288,128]{1,0:T(8,128)S(1)} %fusion.2), channel_id=1, source_target_pairs={{0,32},{8,136},{16,48},{24,152},{32,0},{40,168},{48,16},{56,184},{... | collective-permute-start | bytes 442376 | tf_op jit(solution)/shard_map/ppermute | solution.py:345
  48.6 5.3 %collective-permute-start.11 = (f32[288,128]{1,0:T(8,128)S(1)}, f32[288,128]{1,0:T(8,128)S(1)}, u32[]{:S(2)}, u32[]{:S(2)}) collective-permute-start(f32[288,128]{1,0:T(8,128)S(1)} %fusion.2), channel_id=1, source_target_pairs={{0,16},{8,72},{16,0},{24,88},{32,48},{40,104},{48,32},{56,120},{64... | collective-permute-start | bytes 442376 | tf_op jit(solution)/shard_map/ppermute | solution.py:345
  53.9 7.4 %collective-permute-start.16 = (f32[256,128]{1,0:T(8,128)S(1)}, f32[256,128]{1,0:T(8,128)S(1)}, u32[]{:S(2)}, u32[]{:S(2)}) collective-permute-start(f32[256,128]{1,0:T(8,128)S(1)} %slice.30), channel_id=1, source_target_pairs={{0,192},{8,56},{16,208},{24,40},{32,224},{40,24},{48,240},{56,8},{... | collective-permute-start | bytes 393224 | tf_op jit(solution)/shard_map/ppermute | solution.py:345
  56.7 5.3 %collective-permute-start.15 = (f32[256,128]{1,0:T(8,128)S(1)}, f32[256,128]{1,0:T(8,128)S(1)}, u32[]{:S(2)}, u32[]{:S(2)}) collective-permute-start(f32[256,128]{1,0:T(8,128)S(1)} %slice.30), channel_id=1, source_target_pairs={{0,128},{8,40},{16,144},{24,56},{32,160},{40,8},{48,176},{56,24},{... | collective-permute-start | bytes 393224 | tf_op jit(solution)/shard_map/ppermute | solution.py:345
  57.2 4.8 %collective-permute-start.14 = (f32[256,128]{1,0:T(8,128)S(1)}, f32[256,128]{1,0:T(8,128)S(1)}, u32[]{:S(2)}, u32[]{:S(2)}) collective-permute-start(f32[256,128]{1,0:T(8,128)S(1)} %slice.30), channel_id=1, source_target_pairs={{0,64},{8,24},{16,80},{24,8},{32,96},{40,56},{48,112},{56,40},{64,... | collective-permute-start | bytes 393224 | tf_op jit(solution)/shard_map/ppermute | solution.py:345
  62.0 5.7 %collective-permute-start.17 = (f32[1024,128]{1,0:T(8,128)S(1)}, f32[1024,128]{1,0:T(8,128)S(1)}, u32[]{:S(2)}, u32[]{:S(2)}) collective-permute-start(f32[1024,128]{1,0:T(8,128)S(1)} %pad_maximum_fusion.value_ref), channel_id=1, source_target_pairs={{0,8},{8,0},{16,24},{24,16},{32,40},{40,32},{48,56},{56,48},{64,72... | collective-permute-start | bytes 1572872 | tf_op jit(solution)/shard_map/ppermute | solution.py:345

commit v4 on v3

--- a/solution.py
+++ b/solution.py
@@ -42,6 +42,10 @@
     if group < PER_GROUP:
         return core * PER_GROUP + (first ^ group)
     return (1 - core) * PER_GROUP + (second ^ (group - PER_GROUP))
+
+
+def in_hbm(value):
+    return pltpu.with_memory_space_constraint(value, pltpu.HBM)
 
 
 def vmem(count):
@@ -71,10 +75,12 @@
             high, low = split(data[at])
             terms_ref[pl.ds(2 * q * rows + i * chunk, chunk), :] = high
             terms_ref[pl.ds((2 * q + 1) * rows + i * chunk, chunk), :] = low
-            total = jnp.dot(high, weights[...], preferred_element_type=F32)
-            total += jnp.dot(low, weights[...], preferred_element_type=F32)
+            total = jnp.dot(jnp.concatenate([high, low], axis=0), weights[...], preferred_element_type=F32)
+            total = total[:chunk] + total[chunk:]
             totals.append(total + pltpu.roll(total, K, axis=1))
-        outs[q][...] = jnp.where(lane < K, totals[0], totals[1])
+        half = CHUNKS // 2
+        for i in range(half):
+            outs[q][pl.ds(i * chunk, chunk), :] = jnp.where(lane < K, totals[i], totals[i + half])
 
 
 SENT = (3, 2, 1)
@@ -86,8 +92,9 @@
 
     def prepare():
         load.wait()
-        high, low = split(sketch[...].T)
-        weights_ref[...] = jnp.concatenate([high, low], axis=1)
+        high, low = split(sketch[...])
+        both = jnp.concatenate([high.astype(F32), low.astype(F32)], axis=0)
+        weights_ref[...] = both.T.astype(BF16)
 
     sample_quarters(data_ref, SENT, weights_ref, (out3, out2, out1), terms_ref, data, sems, prepare)
 
@@ -117,22 +124,22 @@
             jax.ShapeDtypeStruct((2 * len(SENT) * quarter, columns), BF16),
             jax.ShapeDtypeStruct((columns, LANES), BF16),
         ],
-        in_specs=[pl.BlockSpec(memory_space=pl.ANY)] * 2,
+        in_specs=[pl.BlockSpec(memory_space=pltpu.HBM)] * 2,
         out_specs=vmem(len(SENT) + 2),
         scratch_shapes=scratch(len(SENT))
         + [VMEM((K, columns), F32), pltpu.SemaphoreType.DMA((len(SENT) * CHUNKS + 1,))],
         compiler_params=pltpu.CompilerParams(vmem_limit_bytes=42 * MIB),
         cost_estimate=cost(len(SENT)),
-    )(data_slab, sketch_t)
+    )(in_hbm(data_slab), in_hbm(sketch_t))
     kept, kept_terms = pl.pallas_call(
         keep_kernel,
         out_shape=[sample, jax.ShapeDtypeStruct((2 * quarter, columns), BF16)],
-        in_specs=[pl.BlockSpec(memory_space=pl.ANY)] + vmem(1),
+        in_specs=[pl.BlockSpec(memory_space=pltpu.HBM)] + vmem(1),
         out_specs=vmem(2),
         scratch_shapes=scratch(1) + [pltpu.SemaphoreType.DMA((CHUNKS,))],
         compiler_params=pltpu.CompilerParams(vmem_limit_bytes=40 * MIB),
         cost_estimate=cost(1),
-    )(data_slab, weights)
+    )(in_hbm(data_slab), weights)
     return sent, sent_terms, kept, kept_terms
 
 
@@ -142,66 +149,79 @@
     return left, jnp.concatenate([left, left], axis=1)
 
 
-def first_term_kernel(own_ref, sample_ref, kept_ref, sent_ref, out_ref):
-    _, left = left_of(own_ref[...])
-    _, other = left_of(sample_ref[...])
-    size = kept_ref.shape[0]
+def term_kernel(sample_ref, terms_ref, *refs):
+    out_ref = refs[-1]
+    _, left = left_of(sample_ref[...])
     width = out_ref.shape[1] // GROUPS
     for g in range(GROUPS):
         at = pl.ds(g * width, width)
-        total = jnp.dot(left, kept_ref[:, at], preferred_element_type=F32)
-        total += jnp.dot(other, sent_ref[:size, at], preferred_element_type=F32)
-        out_ref[:, at] = total[:K] + total[K:]
-
-
-def second_term_kernel(s0, s3, s2, s1, sent_ref, begun_ref, keep_ref, send_ref):
-    singles, lefts = zip(*[left_of(ref[...]) for ref in (s2, s1, s0, s3)])
-    left = jnp.concatenate(lefts[:2], axis=1)
-    every = jnp.concatenate(singles, axis=1)
+        total = jnp.dot(left, terms_ref[:, at], preferred_element_type=F32)
+        total = total[:K] + total[K:]
+        for ref in refs[:-1]:
+            total += ref[:, at]
+        out_ref[:, at] = total
+
+
+def next_term_kernel(index, sample_ref, terms_ref, begun_ref, out_ref):
+    size = terms_ref.shape[0] // len(SENT)
+    term_kernel(sample_ref, terms_ref.at[pl.ds(index * size, size)], begun_ref, out_ref)
+
+
+def half_blocks(first_group, index, sample_ref, terms_ref, begun_ref, out_ref):
+    size = terms_ref.shape[0] // len(SENT)
+    _, left = left_of(sample_ref[...])
+    width = PER_GROUP * LANES
+    for g in range(PER_GROUP):
+        at = pl.ds(pl.multiple_of(group_place(first_group + g) * width, width), width)
+        total = jnp.dot(left, terms_ref[pl.ds(index * size, size), at], preferred_element_type=F32)
+        total = total[:K] + total[K:] + begun_ref[:, at]
+        for t in range(PER_GROUP):
+            out_ref[pl.ds((g * PER_GROUP + t) * K, K), :] = total[:, t * LANES : (t + 1) * LANES]
+
+
+def sent_half_kernel(index, s0, s3, s2, s1, terms_ref, begun_ref, out_ref):
+    every = jnp.concatenate([left_of(ref[...])[0] for ref in (s0, s3, s2, s1)], axis=1)
     gram = lax.dot_general(every, every, (((1,), (1,)), ((), ())), preferred_element_type=F32)
     gram = gram[:K] + gram[K:]
     gram = gram + pltpu.roll(gram, K, axis=1)
     lane = lax.broadcasted_iota(jnp.int32, (K // 2, LANES), 1)
-    gram = jnp.where(lane < K, gram[: K // 2], gram[K // 2 :])
-    keep_ref[BLOCKS // 2 * K :, :] = gram
-    send_ref[BLOCKS // 2 * K :, :] = gram
-    size = left.shape[1]
-    width = PER_GROUP * LANES
-    for g in (4, 5, 6, 7, 0, 1, 2, 3):
-        at = pl.ds(pl.multiple_of(group_place(g) * width, width), width)
-        total = jnp.dot(left, sent_ref[size // 2 :, at], preferred_element_type=F32)
-        total = total[:K] + total[K:] + begun_ref[:, at]
-        out_ref, base = (keep_ref, g) if g < PER_GROUP else (send_ref, g - PER_GROUP)
-        for t in range(PER_GROUP):
-            out_ref[pl.ds((base * PER_GROUP + t) * K, K), :] = total[:, t * LANES : (t + 1) * LANES]
+    out_ref[BLOCKS // 2 * K :, :] = jnp.where(lane < K, gram[: K // 2], gram[K // 2 :])
+    half_blocks(PER_GROUP, index, (s3, s2, s1)[index], terms_ref, begun_ref, out_ref)
+
+
+def kept_half_kernel(index, sample_ref, terms_ref, begun_ref, sent_ref, out_ref):
+    out_ref[BLOCKS // 2 * K :, :] = sent_ref[BLOCKS // 2 * K :, :]
+    half_blocks(0, index, sample_ref, terms_ref, begun_ref, out_ref)
 
 
 def term_cost(rows, columns):
     return pl.CostEstimate(flops=8 * K * rows * columns, bytes_accessed=4 * rows * columns, transcendentals=0)
 
 
-def first_terms(own, third, kept_terms, sent_terms):
-    size, columns = kept_terms.shape
+def term_call(kernel, shape, operands, cost):
     return pl.pallas_call(
-        first_term_kernel,
-        out_shape=jax.ShapeDtypeStruct((K, columns), F32),
-        in_specs=vmem(4),
+        kernel,
+        out_shape=jax.ShapeDtypeStruct(shape, F32),
+        in_specs=vmem(len(operands)),
         out_specs=vmem(1)[0],
         compiler_params=pltpu.CompilerParams(vmem_limit_bytes=16 * MIB),
-        cost_estimate=term_cost(size, columns),
-    )(own, third, kept_terms, sent_terms)
-
-
-def second_terms(quarters, sent_terms, begun):
-    size, columns = sent_terms.shape
-    return pl.pallas_call(
-        second_term_kernel,
-        out_shape=[jax.ShapeDtypeStruct((BLOCKS // 2 * K + K // 2, LANES), F32)] * 2,
-        in_specs=vmem(len(quarters) + 2),
-        out_specs=vmem(2),
-        compiler_params=pltpu.CompilerParams(vmem_limit_bytes=16 * MIB),
-        cost_estimate=term_cost(size // 3, columns),
-    )(*quarters, sent_terms, begun)
+        cost_estimate=cost,
+    )(*operands)
+
+
+def terms_of(quarters, kept_terms, sent_terms):
+    size, columns = kept_terms.shape
+    cost, less = term_cost(size // 2, columns), term_cost(size // 4, columns)
+    whole = (K, columns)
+    blocks = (BLOCKS // 2 * K + K // 2, LANES)
+    begun = term_call(term_kernel, whole, (quarters[0], kept_terms), cost)
+    for index in (0, 2):
+        kernel = functools.partial(next_term_kernel, index)
+        begun = term_call(kernel, whole, (quarters[1 + index], sent_terms, begun), cost)
+    sent = term_call(functools.partial(sent_half_kernel, 1), blocks, (*quarters, sent_terms, begun), less)
+    kernel = functools.partial(kept_half_kernel, 1)
+    kept = term_call(kernel, blocks, (quarters[2], sent_terms, begun, sent), less)
+    return kept, sent
 
 
 def inverse_kernel(gram_ref, inverse_ref):
@@ -358,8 +378,7 @@
     own = own + along_col(own, 7)
     quarters = [own] + [along_col(own, mask) for mask in SENT]
 
-    begun = first_terms(own, quarters[1], kept_terms, sent_terms)
-    keep, send = second_terms(quarters, sent_terms, begun)
+    keep, send = terms_of(quarters, kept_terms, sent_terms)
     total = keep + along_row(send, CORE)
     size = PER_GROUP * K
     gram = total[4 * size :]

time: 69.1 us -> 67.5 us (0.977)
  waiting for transfers between devices: 16.2 us -> 14.6 us
  Pallas kernels: 17.4 us -> 18.8 us
  local copies, waits for them, and re-layouts: 1.27 us -> 0.06 us
    pallas_call x2 -> x5, Pallas kernels: 2.95 us -> 4.33 us  [term_call(): pl.pallas_call(kernel, out_shape=jax.ShapeDtypeStruct(shape, F32), in_spe...]
    unnamed x2 -> x0, local copies, waits for them, and re-layouts: 1.22 us -> none
    ppermute x7, waiting for transfers between devices: 4.1 us -> 3.22 us  [along_col(): return lax.ppermute(value, 'col', [(i, i ^ mask) for i in range(8)])]
  transfers between devices with their start and end apart: 18 -> 18, of which waited for: 11 -> 11; matrix products, arithmetic and copies ran while one was open for 0% -> 0% of each run, Pallas kernels for 14% -> 17%
where the time goes in v4:
time: 67.5 us
  starting transfers between devices  32.8 us (49%)
  Pallas kernels  18.8 us (28%)
  waiting for transfers between devices  14.6 us (22%)
  between operations  0.95 us (1%)
    ppermute x11, starting transfers between devices, along_row(): lax.ppermute(value, 'row', [(i, i ^ masks[i % 2]) for i in range(32)])  18.9 us
    ppermute x7, starting transfers between devices, along_col(): return lax.ppermute(value, 'col', [(i, i ^ mask) for i in range(8)])  13.9 us
    ppermute x11, waiting for transfers between devices, along_row(): lax.ppermute(value, 'row', [(i, i ^ masks[i % 2]) for i in range(32)])  11.4 us
    pallas_call x1, Pallas kernels, partial_samples(): pl.pallas_call(send_kernel, out_shape=[sample] * len(SENT) + [jax.ShapeDt...  5.71 us
    pallas_call x5, Pallas kernels, term_call(): pl.pallas_call(kernel, out_shape=jax.ShapeDtypeStruct(shape, F32), in_spe...  4.33 us
    ppermute x7, waiting for transfers between devices, along_col(): return lax.ppermute(value, 'col', [(i, i ^ mask) for i in range(8)])  3.22 us
    pallas_call x1, Pallas kernels, partial_samples(): pl.pallas_call(keep_kernel, out_shape=[sample, jax.ShapeDtypeStruct((2 *...  2.72 us
    pallas_call x1, Pallas kernels, inverse_of(): pl.pallas_call(inverse_kernel, out_shape=jax.ShapeDtypeStruct((K, K), F32...  2.67 us
  transfers between devices with their start and end apart: 18, of which 11 were waited for; matrix products, arithmetic and copies ran while one was open for 0% of the time, Pallas kernels for 17%

profile of v4, /device:TPU:1, one launch (start us, length us, event | category | flops | bytes accessed | tf_op | source)
XLA Modules:
  0.0 67.5 jit_solution(8321390214952476349)
XLA Ops:
  0.6 5.7 %shard_map.41 = (f32[96,128]{1,0:T(8,128)S(1)}, f32[96,128]{1,0:T(8,128)S(1)}, f32[96,128]{1,0:T(8,128)S(1)}, bf16[1152,4096]{1,0:T(8,128)(2,1)S(1)}, bf16[4096,128]{1,0:T(8,128)(2,1)S(1)}) custom-call(f32[768,4096]{1,0:T(8,128)} %data_ref.3, f32[64,4096]{1,0:T(8,128)} %bitcast.2), custom_call_target="tpu_custom_call" | custom-call | flops 1207959552 | bytes 9437184 | tf_op jit(solution)/shard_map/pallas_call | solution.py:120
  6.3 5.3 %collective-permute-start = (f32[96,128]{1,0:T(8,128)S(1)}, f32[96,128]{1,0:T(8,128)S(1)}, u32[]{:S(2)}, u32[]{:S(2)}) collective-permute-start(f32[96,128]{1,0:T(8,128)S(1)} %get-tuple-element.14), channel_id=1, source_target_pairs={{0,3},{1,2},{2,1},{3,0},{4,7},{5,6},{6,5},{7,4},{8,11},{9,10},{10,... | collective-permute-start | bytes 147464 | tf_op jit(solution)/shard_map/ppermute | solution.py:361
  11.6 0.0 collective-permute-start.1
  11.6 0.4 collective-permute-start.2
  12.0 2.7 %shard_map.42 = (f32[96,128]{1,0:T(8,128)S(1)}, bf16[384,4096]{1,0:T(8,128)(2,1)S(1)}) custom-call(f32[768,4096]{1,0:T(8,128)} %data_ref.3, bf16[4096,128]{1,0:T(8,128)(2,1)S(1)} %get-tuple-element.12.weights_ref), custom_call_target="tpu_custom_call" | custom-call | flops 402653184 | bytes 3145728 | tf_op jit(solution)/shard_map/pallas_call | solution.py:134
  14.7 0.0 collective-permute-done
  14.7 1.3 %collective-permute-done.1 = f32[96,128]{1,0:T(8,128)S(1)} collective-permute-done((f32[96,128]{1,0:T(8,128)S(1)}, f32[96,128]{1,0:T(8,128)S(1)}, u32[]{:S(2)}, u32[]{:S(2)}) %collective-permute-start.1) | collective-permute-done | bytes 49184 | tf_op jit(solution)/shard_map/ppermute | solution.py:361
  16.1 0.0 collective-permute-done.2
  16.1 4.6 %collective-permute-start.3 = (f32[96,128]{1,0:T(8,128)S(1)}, f32[96,128]{1,0:T(8,128)S(1)}, u32[]{:S(2)}, u32[]{:S(2)}) collective-permute-start(f32[96,128]{1,0:T(8,128)S(1)} %add_add_fusion.1), channel_id=1, source_target_pairs={{0,7},{1,6},{2,5},{3,4},{4,3},{5,2},{6,1},{7,0},{8,15},{9,14},{10,... | collective-permute-start | bytes 147464 | tf_op jit(solution)/shard_map/ppermute | solution.py:361
  20.7 1.5 %collective-permute-done.3 = f32[96,128]{1,0:T(8,128)S(1)} collective-permute-done((f32[96,128]{1,0:T(8,128)S(1)}, f32[96,128]{1,0:T(8,128)S(1)}, u32[]{:S(2)}, u32[]{:S(2)}) %collective-permute-start.3) | collective-permute-done | bytes 49184 | tf_op jit(solution)/shard_map/ppermute | solution.py:361
  22.2 1.7 %collective-permute-start.6 = (f32[96,128]{1,0:T(8,128)S(1)}, f32[96,128]{1,0:T(8,128)S(1)}, u32[]{:S(2)}, u32[]{:S(2)}) collective-permute-start(f32[96,128]{1,0:T(8,128)S(1)} %add.36.sample_ref.s0), channel_id=1, source_target_pairs={{0,3},{1,2},{2,1},{3,0},{4,7},{5,6},{6,5},{7,4},{8,11},{9,10},{10,... | collective-permute-start | bytes 147464 | tf_op jit(solution)/shard_map/ppermute | solution.py:361
  23.9 0.0 collective-permute-start.5
  23.9 1.9 %collective-permute-start.4 = (f32[96,128]{1,0:T(8,128)S(1)}, f32[96,128]{1,0:T(8,128)S(1)}, u32[]{:S(2)}, u32[]{:S(2)}) collective-permute-start(f32[96,128]{1,0:T(8,128)S(1)} %add.36.sample_ref.s0), channel_id=1, source_target_pairs={{0,2},{1,3},{2,0},{3,1},{4,6},{5,7},{6,4},{7,5},{8,10},{9,11},{10,... | collective-permute-start | bytes 147464 | tf_op jit(solution)/shard_map/ppermute | solution.py:361
  25.8 0.9 %shard_map.43.begun_ref = f32[64,4096]{1,0:T(8,128)S(1)} custom-call(f32[96,128]{1,0:T(8,128)S(1)} %add.36.sample_ref.s0, bf16[384,4096]{1,0:T(8,128)(2,1)S(1)} %get-tuple-element.18.terms_ref), custom_call_target="tpu_custom_call" | custom-call | flops 402653184 | bytes 3145728 | tf_op jit(solution)/shard_map/pallas_call | solution.py:202
  26.8 0.4 collective-permute-done.6.sample_ref.s3
  27.1 0.9 %shard_map.44.begun_ref = f32[64,4096]{1,0:T(8,128)S(1)} custom-call(f32[96,128]{1,0:T(8,128)S(1)} %collective-permute-done.6.sample_ref.s3, bf16[1152,4096]{1,0:T(8,128)(2,1)S(1)} %get-tuple-element.17.terms_ref, f32[64,4096]{1,0:T(8,128)S(1)} %shard_map.43.begun_ref), custom_call_target="tpu_custom_call" | custom-call | flops 402653184 | bytes 3145728 | tf_op jit(solution)/shard_map/pallas_call | solution.py:202
  28.1 0.0 collective-permute-done.5.sample_ref.s1
  28.1 0.9 %shard_map.45.begun_ref = f32[64,4096]{1,0:T(8,128)S(1)} custom-call(f32[96,128]{1,0:T(8,128)S(1)} %collective-permute-done.5.sample_ref.s1, bf16[1152,4096]{1,0:T(8,128)(2,1)S(1)} %get-tuple-element.17.terms_ref, f32[64,4096]{1,0:T(8,128)S(1)} %shard_map.44.begun_ref), custom_call_target="tpu_custom_call" | custom-call | flops 402653184 | bytes 3145728 | tf_op jit(solution)/shard_map/pallas_call | solution.py:202
  29.0 0.0 collective-permute-done.4.s2.sample_ref
  29.0 0.9 %shard_map.46.sent_ref = f32[1056,128]{1,0:T(8,128)S(1)} custom-call(f32[96,128]{1,0:T(8,128)S(1)} %add.36.sample_ref.s0, f32[96,128]{1,0:T(8,128)S(1)} %collective-permute-done.6.sample_ref.s3, f32[96,128]{1,0:T(8,128)S(1)} %collective-permute-done.4.s2.sample_ref, f32[96,128]{1,0:T(8,128)S(1)} %collective-permute-done.5.sample_ref.s1, ...), custom_call_target="tpu_custom_call" | custom-call | flops 201326592 | bytes 1572864 | tf_op jit(solution)/shard_map/pallas_call | solution.py:202
  29.9 3.9 %collective-permute-start.7 = (f32[1056,128]{1,0:T(8,128)S(1)}, f32[1056,128]{1,0:T(8,128)S(1)}, u32[]{:S(2)}, u32[]{:S(2)}) collective-permute-start(f32[1056,128]{1,0:T(8,128)S(1)} %shard_map.46.sent_ref), channel_id=1, source_target_pairs={{0,8},{8,0},{16,24},{24,16},{32,40},{40,32},{48,56},{56,48},{64,72... | collective-permute-start | bytes 1622024 | tf_op jit(solution)/shard_map/ppermute | solution.py:365
  33.8 0.7 shard_map.47
  34.5 0.9 %collective-permute-done.7 = f32[1056,128]{1,0:T(8,128)S(1)} collective-permute-done((f32[1056,128]{1,0:T(8,128)S(1)}, f32[1056,128]{1,0:T(8,128)S(1)}, u32[]{:S(2)}, u32[]{:S(2)}) %collective-permute-start.7) | collective-permute-done | bytes 540704 | tf_op jit(solution)/shard_map/ppermute | solution.py:365
  35.3 0.1 add.37
  35.5 2.8 %collective-permute-start.10 = (f32[288,128]{1,0:T(8,128)S(1)}, f32[288,128]{1,0:T(8,128)S(1)}, u32[]{:S(2)}, u32[]{:S(2)}) collective-permute-start(f32[288,128]{1,0:T(8,128)S(1)} %concatenate.20), channel_id=1, source_target_pairs={{0,192},{8,56},{16,208},{24,40},{32,224},{40,24},{48,240},{56,8},{... | collective-permute-start | bytes 442376 | tf_op jit(solution)/shard_map/ppermute | solution.py:365
  38.3 0.1 collective-permute-start.8
  38.4 1.2 %collective-permute-start.9 = (f32[288,128]{1,0:T(8,128)S(1)}, f32[288,128]{1,0:T(8,128)S(1)}, u32[]{:S(2)}, u32[]{:S(2)}) collective-permute-start(f32[288,128]{1,0:T(8,128)S(1)} %get-tuple-element.26), channel_id=1, source_target_pairs={{0,128},{8,40},{16,144},{24,56},{32,160},{40,8},{48,176},{56,24},{... | collective-permute-start | bytes 442376 | tf_op jit(solution)/shard_map/ppermute | solution.py:365
  39.6 1.5 %collective-permute-done.10 = f32[288,128]{1,0:T(8,128)S(1)} collective-permute-done((f32[288,128]{1,0:T(8,128)S(1)}, f32[288,128]{1,0:T(8,128)S(1)}, u32[]{:S(2)}, u32[]{:S(2)}) %collective-permute-start.10) | collective-permute-done | bytes 147488 | tf_op jit(solution)/shard_map/ppermute | solution.py:365
  41.1 1.6 %collective-permute-done.8 = f32[288,128]{1,0:T(8,128)S(1)} collective-permute-done((f32[288,128]{1,0:T(8,128)S(1)}, f32[288,128]{1,0:T(8,128)S(1)}, u32[]{:S(2)}, u32[]{:S(2)}) %collective-permute-start.8) | collective-permute-done | bytes 147488 | tf_op jit(solution)/shard_map/ppermute | solution.py:365
  42.7 1.6 %collective-permute-done.9 = f32[288,128]{1,0:T(8,128)S(1)} collective-permute-done((f32[288,128]{1,0:T(8,128)S(1)}, f32[288,128]{1,0:T(8,128)S(1)}, u32[]{:S(2)}, u32[]{:S(2)}) %collective-permute-start.9) | collective-permute-done | bytes 147488 | tf_op jit(solution)/shard_map/ppermute | solution.py:365
  44.3 2.6 %collective-permute-start.13 = (f32[288,128]{1,0:T(8,128)S(1)}, f32[288,128]{1,0:T(8,128)S(1)}, u32[]{:S(2)}, u32[]{:S(2)}) collective-permute-start(f32[288,128]{1,0:T(8,128)S(1)} %fusion.2), channel_id=1, source_target_pairs={{0,48},{8,200},{16,32},{24,216},{32,16},{40,232},{48,0},{56,248},{... | collective-permute-start | bytes 442376 | tf_op jit(solution)/shard_map/ppermute | solution.py:365
  46.9 0.2 collective-permute-start.12
  47.1 0.5 collective-permute-start.11
  47.7 2.9 %collective-permute-done.13 = f32[288,128]{1,0:T(8,128)S(1)} collective-permute-done((f32[288,128]{1,0:T(8,128)S(1)}, f32[288,128]{1,0:T(8,128)S(1)}, u32[]{:S(2)}, u32[]{:S(2)}) %collective-permute-start.13) | collective-permute-done | bytes 147488 | tf_op jit(solution)/shard_map/ppermute | solution.py:365
  50.6 1.8 %collective-permute-done.12 = f32[288,128]{1,0:T(8,128)S(1)} collective-permute-done((f32[288,128]{1,0:T(8,128)S(1)}, f32[288,128]{1,0:T(8,128)S(1)}, u32[]{:S(2)}, u32[]{:S(2)}) %collective-permute-start.12) | collective-permute-done | bytes 147488 | tf_op jit(solution)/shard_map/ppermute | solution.py:365
  52.4 0.0 collective-permute-done.11
  52.5 2.7 %collective-permute-start.16 = (f32[256,128]{1,0:T(8,128)S(1)}, f32[256,128]{1,0:T(8,128)S(1)}, u32[]{:S(2)}, u32[]{:S(2)}) collective-permute-start(f32[256,128]{1,0:T(8,128)S(1)} %slice.30), channel_id=1, source_target_pairs={{0,192},{8,56},{16,208},{24,40},{32,224},{40,24},{48,240},{56,8},{... | collective-permute-start | bytes 393224 | tf_op jit(solution)/shard_map/ppermute | solution.py:365
  55.2 0.5 collective-permute-start.15
  55.7 0.2 collective-permute-start.14
  55.9 2.7 %shard_map.48.inverse_ref = f32[64,64]{1,0:T(8,128)S(1)} custom-call(f32[32,128]{1,0:T(8,128)S(1)} %slice.31.gram_ref), custom_call_target="tpu_custom_call" | custom-call | flops 26214400 | bytes 32768 | tf_op jit(solution)/shard_map/pallas_call | solution.py:289
  58.6 1.3 %shard_map.49 = f32[64,768]{1,0:T(8,128)} custom-call(f32[64,64]{1,0:T(8,128)S(1)} %shard_map.48.inverse_ref, f32[96,128]{1,0:T(8,128)S(1)} %add.36.sample_ref.s0, f32[96,128]{1,0:T(8,128)S(1)} %collective-permute-done.6.sample_ref.s3, f32[96,128]{1,0:T(8,128)S(1)} %collective-permute-done.4.s2.sample_ref, f32[96,128]{1,0:T(8,128)S(1)} %collective-permute-done.5.sample_ref.s1), custom_call_target="tpu_custom_call" | custom-call | flops 37748736 | bytes 393216 | tf_op jit(solution)/shard_map/pallas_call | solution.py:316
  59.9 0.0 collective-permute-done.16
  59.9 0.6 collective-permute-done.15
  60.5 0.0 collective-permute-done.14
  60.6 4.2 %collective-permute-start.17 = (f32[1024,128]{1,0:T(8,128)S(1)}, f32[1024,128]{1,0:T(8,128)S(1)}, u32[]{:S(2)}, u32[]{:S(2)}) collective-permute-start(f32[1024,128]{1,0:T(8,128)S(1)} %pad_maximum_fusion.value_ref), channel_id=1, source_target_pairs={{0,8},{8,0},{16,24},{24,16},{32,40},{40,32},{48,56},{56,48},{64,72... | collective-permute-start | bytes 1572872 | tf_op jit(solution)/shard_map/ppermute | solution.py:365
  64.7 1.0 %shard_map.50.refs_0_ = f32[64,4096]{1,0:T(8,128)} custom-call(f32[64,64]{1,0:T(8,128)S(1)} %shard_map.48.inverse_ref, f32[1024,128]{1,0:T(8,128)S(1)} %pad_maximum_fusion.value_ref), custom_call_target="tpu_custom_call" | custom-call | flops 50331648 | bytes 1048576 | tf_op jit(solution)/shard_map/pallas_call | solution.py:348
  65.8 0.5 collective-permute-done.17.value_ref
  66.3 1.0 %shard_map.51 = f32[64,4096]{1,0:T(8,128)} custom-call(f32[64,64]{1,0:T(8,128)S(1)} %shard_map.48.inverse_ref, f32[1024,128]{1,0:T(8,128)S(1)} %collective-permute-done.17.value_ref, f32[64,4096]{1,0:T(8,128)} %shard_map.50.refs_0_), custom_call_target="tpu_custom_call", output_to_operand_aliasing={{}: (2, {})} | custom-call | flops 50331648 | bytes 1048576 | tf_op jit(solution)/shard_map/pallas_call | solution.py:348
  (11 shorter events, 0.2 us)
Async XLA Ops:
  6.3 8.4 %collective-permute-start = (f32[96,128]{1,0:T(8,128)S(1)}, f32[96,128]{1,0:T(8,128)S(1)}, u32[]{:S(2)}, u32[]{:S(2)}) collective-permute-start(f32[96,128]{1,0:T(8,128)S(1)} %get-tuple-element.14), channel_id=1, source_target_pairs={{0,3},{1,2},{2,1},{3,0},{4,7},{5,6},{6,5},{7,4},{8,11},{9,10},{10,... | collective-permute-start | bytes 147464 | tf_op jit(solution)/shard_map/ppermute | solution.py:361
  11.6 4.5 %collective-permute-start.1 = (f32[96,128]{1,0:T(8,128)S(1)}, f32[96,128]{1,0:T(8,128)S(1)}, u32[]{:S(2)}, u32[]{:S(2)}) collective-permute-start(f32[96,128]{1,0:T(8,128)S(1)} %get-tuple-element.15), channel_id=1, source_target_pairs={{0,2},{1,3},{2,0},{3,1},{4,6},{5,7},{6,4},{7,5},{8,10},{9,11},{10,... | collective-permute-start | bytes 147464 | tf_op jit(solution)/shard_map/ppermute | solution.py:361
  11.6 4.5 %collective-permute-start.2 = (f32[96,128]{1,0:T(8,128)S(1)}, f32[96,128]{1,0:T(8,128)S(1)}, u32[]{:S(2)}, u32[]{:S(2)}) collective-permute-start(f32[96,128]{1,0:T(8,128)S(1)} %get-tuple-element.16), channel_id=1, source_target_pairs={{0,1},{1,0},{2,3},{3,2},{4,5},{5,4},{6,7},{7,6},{8,9},{9,8},{10,11... | collective-permute-start | bytes 147464 | tf_op jit(solution)/shard_map/ppermute | solution.py:361
  16.1 6.1 %collective-permute-start.3 = (f32[96,128]{1,0:T(8,128)S(1)}, f32[96,128]{1,0:T(8,128)S(1)}, u32[]{:S(2)}, u32[]{:S(2)}) collective-permute-start(f32[96,128]{1,0:T(8,128)S(1)} %add_add_fusion.1), channel_id=1, source_target_pairs={{0,7},{1,6},{2,5},{3,4},{4,3},{5,2},{6,1},{7,0},{8,15},{9,14},{10,... | collective-permute-start | bytes 147464 | tf_op jit(solution)/shard_map/ppermute | solution.py:361
  22.2 4.9 %collective-permute-start.6 = (f32[96,128]{1,0:T(8,128)S(1)}, f32[96,128]{1,0:T(8,128)S(1)}, u32[]{:S(2)}, u32[]{:S(2)}) collective-permute-start(f32[96,128]{1,0:T(8,128)S(1)} %add.36.sample_ref.s0), channel_id=1, source_target_pairs={{0,3},{1,2},{2,1},{3,0},{4,7},{5,6},{6,5},{7,4},{8,11},{9,10},{10,... | collective-permute-start | bytes 147464 | tf_op jit(solution)/shard_map/ppermute | solution.py:361
  23.9 4.2 %collective-permute-start.5 = (f32[96,128]{1,0:T(8,128)S(1)}, f32[96,128]{1,0:T(8,128)S(1)}, u32[]{:S(2)}, u32[]{:S(2)}) collective-permute-start(f32[96,128]{1,0:T(8,128)S(1)} %add.36.sample_ref.s0), channel_id=1, source_target_pairs={{0,1},{1,0},{2,3},{3,2},{4,5},{5,4},{6,7},{7,6},{8,9},{9,8},{10,11... | collective-permute-start | bytes 147464 | tf_op jit(solution)/shard_map/ppermute | solution.py:361
  23.9 5.1 %collective-permute-start.4 = (f32[96,128]{1,0:T(8,128)S(1)}, f32[96,128]{1,0:T(8,128)S(1)}, u32[]{:S(2)}, u32[]{:S(2)}) collective-permute-start(f32[96,128]{1,0:T(8,128)S(1)} %add.36.sample_ref.s0), channel_id=1, source_target_pairs={{0,2},{1,3},{2,0},{3,1},{4,6},{5,7},{6,4},{7,5},{8,10},{9,11},{10,... | collective-permute-start | bytes 147464 | tf_op jit(solution)/shard_map/ppermute | solution.py:361
  29.9 5.4 %collective-permute-start.7 = (f32[1056,128]{1,0:T(8,128)S(1)}, f32[1056,128]{1,0:T(8,128)S(1)}, u32[]{:S(2)}, u32[]{:S(2)}) collective-permute-start(f32[1056,128]{1,0:T(8,128)S(1)} %shard_map.46.sent_ref), channel_id=1, source_target_pairs={{0,8},{8,0},{16,24},{24,16},{32,40},{40,32},{48,56},{56,48},{64,72... | collective-permute-start | bytes 1622024 | tf_op jit(solution)/shard_map/ppermute | solution.py:365
  35.5 5.6 %collective-permute-start.10 = (f32[288,128]{1,0:T(8,128)S(1)}, f32[288,128]{1,0:T(8,128)S(1)}, u32[]{:S(2)}, u32[]{:S(2)}) collective-permute-start(f32[288,128]{1,0:T(8,128)S(1)} %concatenate.20), channel_id=1, source_target_pairs={{0,192},{8,56},{16,208},{24,40},{32,224},{40,24},{48,240},{56,8},{... | collective-permute-start | bytes 442376 | tf_op jit(solution)/shard_map/ppermute | solution.py:365
  38.3 4.4 %collective-permute-start.8 = (f32[288,128]{1,0:T(8,128)S(1)}, f32[288,128]{1,0:T(8,128)S(1)}, u32[]{:S(2)}, u32[]{:S(2)}) collective-permute-start(f32[288,128]{1,0:T(8,128)S(1)} %get-tuple-element.25), channel_id=1, source_target_pairs={{0,64},{8,24},{16,80},{24,8},{32,96},{40,56},{48,112},{56,40},{64,... | collective-permute-start | bytes 442376 | tf_op jit(solution)/shard_map/ppermute | solution.py:365
  38.4 5.9 %collective-permute-start.9 = (f32[288,128]{1,0:T(8,128)S(1)}, f32[288,128]{1,0:T(8,128)S(1)}, u32[]{:S(2)}, u32[]{:S(2)}) collective-permute-start(f32[288,128]{1,0:T(8,128)S(1)} %get-tuple-element.26), channel_id=1, source_target_pairs={{0,128},{8,40},{16,144},{24,56},{32,160},{40,8},{48,176},{56,24},{... | collective-permute-start | bytes 442376 | tf_op jit(solution)/shard_map/ppermute | solution.py:365
  44.3 6.2 %collective-permute-start.13 = (f32[288,128]{1,0:T(8,128)S(1)}, f32[288,128]{1,0:T(8,128)S(1)}, u32[]{:S(2)}, u32[]{:S(2)}) collective-permute-start(f32[288,128]{1,0:T(8,128)S(1)} %fusion.2), channel_id=1, source_target_pairs={{0,48},{8,200},{16,32},{24,216},{32,16},{40,232},{48,0},{56,248},{... | collective-permute-start | bytes 442376 | tf_op jit(solution)/shard_map/ppermute | solution.py:365
  46.9 5.5 %collective-permute-start.12 = (f32[288,128]{1,0:T(8,128)S(1)}, f32[288,128]{1,0:T(8,128)S(1)}, u32[]{:S(2)}, u32[]{:S(2)}) collective-permute-start(f32[288,128]{1,0:T(8,128)S(1)} %fusion.2), channel_id=1, source_target_pairs={{0,32},{8,136},{16,48},{24,152},{32,0},{40,168},{48,16},{56,184},{... | collective-permute-start | bytes 442376 | tf_op jit(solution)/shard_map/ppermute | solution.py:365
  47.1 5.3 %collective-permute-start.11 = (f32[288,128]{1,0:T(8,128)S(1)}, f32[288,128]{1,0:T(8,128)S(1)}, u32[]{:S(2)}, u32[]{:S(2)}) collective-permute-start(f32[288,128]{1,0:T(8,128)S(1)} %fusion.2), channel_id=1, source_target_pairs={{0,16},{8,72},{16,0},{24,88},{32,48},{40,104},{48,32},{56,120},{64... | collective-permute-start | bytes 442376 | tf_op jit(solution)/shard_map/ppermute | solution.py:365
  52.5 7.4 %collective-permute-start.16 = (f32[256,128]{1,0:T(8,128)S(1)}, f32[256,128]{1,0:T(8,128)S(1)}, u32[]{:S(2)}, u32[]{:S(2)}) collective-permute-start(f32[256,128]{1,0:T(8,128)S(1)} %slice.30), channel_id=1, source_target_pairs={{0,192},{8,56},{16,208},{24,40},{32,224},{40,24},{48,240},{56,8},{... | collective-permute-start | bytes 393224 | tf_op jit(solution)/shard_map/ppermute | solution.py:365
  55.2 5.3 %collective-permute-start.15 = (f32[256,128]{1,0:T(8,128)S(1)}, f32[256,128]{1,0:T(8,128)S(1)}, u32[]{:S(2)}, u32[]{:S(2)}) collective-permute-start(f32[256,128]{1,0:T(8,128)S(1)} %slice.30), channel_id=1, source_target_pairs={{0,128},{8,40},{16,144},{24,56},{32,160},{40,8},{48,176},{56,24},{... | collective-permute-start | bytes 393224 | tf_op jit(solution)/shard_map/ppermute | solution.py:365
  55.7 4.8 %collective-permute-start.14 = (f32[256,128]{1,0:T(8,128)S(1)}, f32[256,128]{1,0:T(8,128)S(1)}, u32[]{:S(2)}, u32[]{:S(2)}) collective-permute-start(f32[256,128]{1,0:T(8,128)S(1)} %slice.30), channel_id=1, source_target_pairs={{0,64},{8,24},{16,80},{24,8},{32,96},{40,56},{48,112},{56,40},{64,... | collective-permute-start | bytes 393224 | tf_op jit(solution)/shard_map/ppermute | solution.py:365
  60.6 5.7 %collective-permute-start.17 = (f32[1024,128]{1,0:T(8,128)S(1)}, f32[1024,128]{1,0:T(8,128)S(1)}, u32[]{:S(2)}, u32[]{:S(2)}) collective-permute-start(f32[1024,128]{1,0:T(8,128)S(1)} %pad_maximum_fusion.value_ref), channel_id=1, source_target_pairs={{0,8},{8,0},{16,24},{24,16},{32,40},{40,32},{48,56},{56,48},{64,72... | collective-permute-start | bytes 1572872 | tf_op jit(solution)/shard_map/ppermute | solution.py:365

commit v5 on v4

--- a/solution.py
+++ b/solution.py
@@ -382,7 +382,7 @@
     total = keep + along_row(send, CORE)
     size = PER_GROUP * K
     gram = total[4 * size :]
-    got = [along_row(jnp.concatenate([total[t * size : (t + 1) * size], gram]), FIRST[t]) for t in (1, 2, 3)]
+    got = [along_row(jnp.concatenate([total[t * size : (t + 1) * size], gram]), FIRST[t]) for t in (2, 1, 3)]
     total = jnp.concatenate([total[:size], gram]) + got[0] + got[1] + got[2]
     got = [along_row(total, SECOND[t]) for t in (1, 2, 3)]
     total = total + got[0] + got[1] + got[2]

time: 67.5 us -> 66.9 us (level)
  starting transfers between devices: 32.8 us -> 32.1 us
    ppermute x11, starting transfers between devices: 18.9 us -> 18.2 us  [along_row(): lax.ppermute(value, 'row', [(i, i ^ masks[i % 2]) for i in range(32)])]
  transfers between devices with their start and end apart: 18 -> 18, of which waited for: 11 -> 10; matrix products, arithmetic and copies ran while one was open for 0% -> 0% of each run, Pallas kernels for 17% -> 17%
where the time goes in v5:
time: 66.9 us
  starting transfers between devices  32.1 us (48%)
  Pallas kernels  18.8 us (28%)
  waiting for transfers between devices  14.7 us (22%)
  between operations  0.95 us (1%)
    ppermute x11, starting transfers between devices, along_row(): lax.ppermute(value, 'row', [(i, i ^ masks[i % 2]) for i in range(32)])  18.2 us
    ppermute x7, starting transfers between devices, along_col(): return lax.ppermute(value, 'col', [(i, i ^ mask) for i in range(8)])  13.9 us
    ppermute x11, waiting for transfers between devices, along_row(): lax.ppermute(value, 'row', [(i, i ^ masks[i % 2]) for i in range(32)])  11.5 us
    pallas_call x1, Pallas kernels, partial_samples(): pl.pallas_call(send_kernel, out_shape=[sample] * len(SENT) + [jax.ShapeDt...  5.71 us
    pallas_call x5, Pallas kernels, term_call(): pl.pallas_call(kernel, out_shape=jax.ShapeDtypeStruct(shape, F32), in_spe...  4.33 us
    ppermute x7, waiting for transfers between devices, along_col(): return lax.ppermute(value, 'col', [(i, i ^ mask) for i in range(8)])  3.22 us
    pallas_call x1, Pallas kernels, partial_samples(): pl.pallas_call(keep_kernel, out_shape=[sample, jax.ShapeDtypeStruct((2 *...  2.72 us
    pallas_call x1, Pallas kernels, inverse_of(): pl.pallas_call(inverse_kernel, out_shape=jax.ShapeDtypeStruct((K, K), F32...  2.67 us
  transfers between devices with their start and end apart: 18, of which 10 were waited for; matrix products, arithmetic and copies ran while one was open for 0% of the time, Pallas kernels for 17%

profile of v5, /device:TPU:1, one launch (start us, length us, event | category | flops | bytes accessed | tf_op | source)
XLA Modules:
  0.0 66.9 jit_solution(6463786366098239556)
XLA Ops:
  0.6 5.7 %shard_map.41 = (f32[96,128]{1,0:T(8,128)S(1)}, f32[96,128]{1,0:T(8,128)S(1)}, f32[96,128]{1,0:T(8,128)S(1)}, bf16[1152,4096]{1,0:T(8,128)(2,1)S(1)}, bf16[4096,128]{1,0:T(8,128)(2,1)S(1)}) custom-call(f32[768,4096]{1,0:T(8,128)} %data_ref.3, f32[64,4096]{1,0:T(8,128)} %bitcast.2), custom_call_target="tpu_custom_call" | custom-call | flops 1207959552 | bytes 9437184 | tf_op jit(solution)/shard_map/pallas_call | solution.py:120
  6.3 5.3 %collective-permute-start = (f32[96,128]{1,0:T(8,128)S(1)}, f32[96,128]{1,0:T(8,128)S(1)}, u32[]{:S(2)}, u32[]{:S(2)}) collective-permute-start(f32[96,128]{1,0:T(8,128)S(1)} %get-tuple-element.14), channel_id=1, source_target_pairs={{0,3},{1,2},{2,1},{3,0},{4,7},{5,6},{6,5},{7,4},{8,11},{9,10},{10,... | collective-permute-start | bytes 147464 | tf_op jit(solution)/shard_map/ppermute | solution.py:361
  11.6 0.0 collective-permute-start.1
  11.6 0.4 collective-permute-start.2
  12.0 2.7 %shard_map.42 = (f32[96,128]{1,0:T(8,128)S(1)}, bf16[384,4096]{1,0:T(8,128)(2,1)S(1)}) custom-call(f32[768,4096]{1,0:T(8,128)} %data_ref.3, bf16[4096,128]{1,0:T(8,128)(2,1)S(1)} %get-tuple-element.12.weights_ref), custom_call_target="tpu_custom_call" | custom-call | flops 402653184 | bytes 3145728 | tf_op jit(solution)/shard_map/pallas_call | solution.py:134
  14.7 0.0 collective-permute-done
  14.7 1.3 %collective-permute-done.1 = f32[96,128]{1,0:T(8,128)S(1)} collective-permute-done((f32[96,128]{1,0:T(8,128)S(1)}, f32[96,128]{1,0:T(8,128)S(1)}, u32[]{:S(2)}, u32[]{:S(2)}) %collective-permute-start.1) | collective-permute-done | bytes 49184 | tf_op jit(solution)/shard_map/ppermute | solution.py:361
  16.1 0.0 collective-permute-done.2
  16.1 4.6 %collective-permute-start.3 = (f32[96,128]{1,0:T(8,128)S(1)}, f32[96,128]{1,0:T(8,128)S(1)}, u32[]{:S(2)}, u32[]{:S(2)}) collective-permute-start(f32[96,128]{1,0:T(8,128)S(1)} %add_add_fusion.1), channel_id=1, source_target_pairs={{0,7},{1,6},{2,5},{3,4},{4,3},{5,2},{6,1},{7,0},{8,15},{9,14},{10,... | collective-permute-start | bytes 147464 | tf_op jit(solution)/shard_map/ppermute | solution.py:361
  20.7 1.5 %collective-permute-done.3 = f32[96,128]{1,0:T(8,128)S(1)} collective-permute-done((f32[96,128]{1,0:T(8,128)S(1)}, f32[96,128]{1,0:T(8,128)S(1)}, u32[]{:S(2)}, u32[]{:S(2)}) %collective-permute-start.3) | collective-permute-done | bytes 49184 | tf_op jit(solution)/shard_map/ppermute | solution.py:361
  22.2 1.7 %collective-permute-start.6 = (f32[96,128]{1,0:T(8,128)S(1)}, f32[96,128]{1,0:T(8,128)S(1)}, u32[]{:S(2)}, u32[]{:S(2)}) collective-permute-start(f32[96,128]{1,0:T(8,128)S(1)} %add.36.sample_ref.s0), channel_id=1, source_target_pairs={{0,3},{1,2},{2,1},{3,0},{4,7},{5,6},{6,5},{7,4},{8,11},{9,10},{10,... | collective-permute-start | bytes 147464 | tf_op jit(solution)/shard_map/ppermute | solution.py:361
  23.9 0.0 collective-permute-start.5
  23.9 1.9 %collective-permute-start.4 = (f32[96,128]{1,0:T(8,128)S(1)}, f32[96,128]{1,0:T(8,128)S(1)}, u32[]{:S(2)}, u32[]{:S(2)}) collective-permute-start(f32[96,128]{1,0:T(8,128)S(1)} %add.36.sample_ref.s0), channel_id=1, source_target_pairs={{0,2},{1,3},{2,0},{3,1},{4,6},{5,7},{6,4},{7,5},{8,10},{9,11},{10,... | collective-permute-start | bytes 147464 | tf_op jit(solution)/shard_map/ppermute | solution.py:361
  25.8 0.9 %shard_map.43.begun_ref = f32[64,4096]{1,0:T(8,128)S(1)} custom-call(f32[96,128]{1,0:T(8,128)S(1)} %add.36.sample_ref.s0, bf16[384,4096]{1,0:T(8,128)(2,1)S(1)} %get-tuple-element.18.terms_ref), custom_call_target="tpu_custom_call" | custom-call | flops 402653184 | bytes 3145728 | tf_op jit(solution)/shard_map/pallas_call | solution.py:202
  26.8 0.4 collective-permute-done.6.sample_ref.s3
  27.1 0.9 %shard_map.44.begun_ref = f32[64,4096]{1,0:T(8,128)S(1)} custom-call(f32[96,128]{1,0:T(8,128)S(1)} %collective-permute-done.6.sample_ref.s3, bf16[1152,4096]{1,0:T(8,128)(2,1)S(1)} %get-tuple-element.17.terms_ref, f32[64,4096]{1,0:T(8,128)S(1)} %shard_map.43.begun_ref), custom_call_target="tpu_custom_call" | custom-call | flops 402653184 | bytes 3145728 | tf_op jit(solution)/shard_map/pallas_call | solution.py:202
  28.1 0.0 collective-permute-done.5.sample_ref.s1
  28.1 0.9 %shard_map.45.begun_ref = f32[64,4096]{1,0:T(8,128)S(1)} custom-call(f32[96,128]{1,0:T(8,128)S(1)} %collective-permute-done.5.sample_ref.s1, bf16[1152,4096]{1,0:T(8,128)(2,1)S(1)} %get-tuple-element.17.terms_ref, f32[64,4096]{1,0:T(8,128)S(1)} %shard_map.44.begun_ref), custom_call_target="tpu_custom_call" | custom-call | flops 402653184 | bytes 3145728 | tf_op jit(solution)/shard_map/pallas_call | solution.py:202
  29.0 0.0 collective-permute-done.4.s2.sample_ref
  29.0 0.9 %shard_map.46.sent_ref = f32[1056,128]{1,0:T(8,128)S(1)} custom-call(f32[96,128]{1,0:T(8,128)S(1)} %add.36.sample_ref.s0, f32[96,128]{1,0:T(8,128)S(1)} %collective-permute-done.6.sample_ref.s3, f32[96,128]{1,0:T(8,128)S(1)} %collective-permute-done.4.s2.sample_ref, f32[96,128]{1,0:T(8,128)S(1)} %collective-permute-done.5.sample_ref.s1, ...), custom_call_target="tpu_custom_call" | custom-call | flops 201326592 | bytes 1572864 | tf_op jit(solution)/shard_map/pallas_call | solution.py:202
  29.9 3.9 %collective-permute-start.7 = (f32[1056,128]{1,0:T(8,128)S(1)}, f32[1056,128]{1,0:T(8,128)S(1)}, u32[]{:S(2)}, u32[]{:S(2)}) collective-permute-start(f32[1056,128]{1,0:T(8,128)S(1)} %shard_map.46.sent_ref), channel_id=1, source_target_pairs={{0,8},{8,0},{16,24},{24,16},{32,40},{40,32},{48,56},{56,48},{64,72... | collective-permute-start | bytes 1622024 | tf_op jit(solution)/shard_map/ppermute | solution.py:365
  33.8 0.7 %shard_map.47 = f32[1056,128]{1,0:T(8,128)S(1)} custom-call(f32[96,128]{1,0:T(8,128)S(1)} %collective-permute-done.4.s2.sample_ref, bf16[1152,4096]{1,0:T(8,128)(2,1)S(1)} %get-tuple-element.17.terms_ref, f32[64,4096]{1,0:T(8,128)S(1)} %shard_map.45.begun_ref, f32[1056,128]{1,0:T(8,128)S(1)} %shard_map.46.sent_ref), custom_call_target="tpu_custom_call" | custom-call | flops 201326592 | bytes 1572864 | tf_op jit(solution)/shard_map/pallas_call | solution.py:202
  34.5 0.9 %collective-permute-done.7 = f32[1056,128]{1,0:T(8,128)S(1)} collective-permute-done((f32[1056,128]{1,0:T(8,128)S(1)}, f32[1056,128]{1,0:T(8,128)S(1)}, u32[]{:S(2)}, u32[]{:S(2)}) %collective-permute-start.7) | collective-permute-done | bytes 540704 | tf_op jit(solution)/shard_map/ppermute | solution.py:365
  35.3 0.1 add.37
  35.5 2.8 %collective-permute-start.10 = (f32[288,128]{1,0:T(8,128)S(1)}, f32[288,128]{1,0:T(8,128)S(1)}, u32[]{:S(2)}, u32[]{:S(2)}) collective-permute-start(f32[288,128]{1,0:T(8,128)S(1)} %concatenate.20), channel_id=1, source_target_pairs={{0,192},{8,56},{16,208},{24,40},{32,224},{40,24},{48,240},{56,8},{... | collective-permute-start | bytes 442376 | tf_op jit(solution)/shard_map/ppermute | solution.py:365
  38.3 0.4 collective-permute-start.8
  38.8 0.2 collective-permute-start.9
  39.0 3.0 %collective-permute-done.10 = f32[288,128]{1,0:T(8,128)S(1)} collective-permute-done((f32[288,128]{1,0:T(8,128)S(1)}, f32[288,128]{1,0:T(8,128)S(1)}, u32[]{:S(2)}, u32[]{:S(2)}) %collective-permute-start.10) | collective-permute-done | bytes 147488 | tf_op jit(solution)/shard_map/ppermute | solution.py:365
  42.0 2.2 %collective-permute-done.8 = f32[288,128]{1,0:T(8,128)S(1)} collective-permute-done((f32[288,128]{1,0:T(8,128)S(1)}, f32[288,128]{1,0:T(8,128)S(1)}, u32[]{:S(2)}, u32[]{:S(2)}) %collective-permute-start.8) | collective-permute-done | bytes 147488 | tf_op jit(solution)/shard_map/ppermute | solution.py:365
  44.2 0.0 collective-permute-done.9
  44.2 2.3 %collective-permute-start.13 = (f32[288,128]{1,0:T(8,128)S(1)}, f32[288,128]{1,0:T(8,128)S(1)}, u32[]{:S(2)}, u32[]{:S(2)}) collective-permute-start(f32[288,128]{1,0:T(8,128)S(1)} %fusion.2), channel_id=1, source_target_pairs={{0,48},{8,200},{16,32},{24,216},{32,16},{40,232},{48,0},{56,248},{... | collective-permute-start | bytes 442376 | tf_op jit(solution)/shard_map/ppermute | solution.py:365
  46.5 0.5 collective-permute-start.12
  47.0 0.5 collective-permute-start.11
  47.6 2.6 %collective-permute-done.13 = f32[288,128]{1,0:T(8,128)S(1)} collective-permute-done((f32[288,128]{1,0:T(8,128)S(1)}, f32[288,128]{1,0:T(8,128)S(1)}, u32[]{:S(2)}, u32[]{:S(2)}) %collective-permute-start.13) | collective-permute-done | bytes 147488 | tf_op jit(solution)/shard_map/ppermute | solution.py:365
  50.2 1.8 %collective-permute-done.12 = f32[288,128]{1,0:T(8,128)S(1)} collective-permute-done((f32[288,128]{1,0:T(8,128)S(1)}, f32[288,128]{1,0:T(8,128)S(1)}, u32[]{:S(2)}, u32[]{:S(2)}) %collective-permute-start.12) | collective-permute-done | bytes 147488 | tf_op jit(solution)/shard_map/ppermute | solution.py:365
  52.0 0.0 collective-permute-done.11
  52.1 2.5 %collective-permute-start.16 = (f32[256,128]{1,0:T(8,128)S(1)}, f32[256,128]{1,0:T(8,128)S(1)}, u32[]{:S(2)}, u32[]{:S(2)}) collective-permute-start(f32[256,128]{1,0:T(8,128)S(1)} %slice.30), channel_id=1, source_target_pairs={{0,192},{8,56},{16,208},{24,40},{32,224},{40,24},{48,240},{56,8},{... | collective-permute-start | bytes 393224 | tf_op jit(solution)/shard_map/ppermute | solution.py:365
  54.6 0.1 collective-permute-start.15
  54.7 0.8 %collective-permute-start.14 = (f32[256,128]{1,0:T(8,128)S(1)}, f32[256,128]{1,0:T(8,128)S(1)}, u32[]{:S(2)}, u32[]{:S(2)}) collective-permute-start(f32[256,128]{1,0:T(8,128)S(1)} %slice.30), channel_id=1, source_target_pairs={{0,64},{8,24},{16,80},{24,8},{32,96},{40,56},{48,112},{56,40},{64,... | collective-permute-start | bytes 393224 | tf_op jit(solution)/shard_map/ppermute | solution.py:365
  55.4 2.7 %shard_map.48.inverse_ref = f32[64,64]{1,0:T(8,128)S(1)} custom-call(f32[32,128]{1,0:T(8,128)S(1)} %slice.31.gram_ref), custom_call_target="tpu_custom_call" | custom-call | flops 26214400 | bytes 32768 | tf_op jit(solution)/shard_map/pallas_call | solution.py:289
  58.1 1.3 %shard_map.49 = f32[64,768]{1,0:T(8,128)} custom-call(f32[64,64]{1,0:T(8,128)S(1)} %shard_map.48.inverse_ref, f32[96,128]{1,0:T(8,128)S(1)} %add.36.sample_ref.s0, f32[96,128]{1,0:T(8,128)S(1)} %collective-permute-done.6.sample_ref.s3, f32[96,128]{1,0:T(8,128)S(1)} %collective-permute-done.4.s2.sample_ref, f32[96,128]{1,0:T(8,128)S(1)} %collective-permute-done.5.sample_ref.s1), custom_call_target="tpu_custom_call" | custom-call | flops 37748736 | bytes 393216 | tf_op jit(solution)/shard_map/pallas_call | solution.py:316
  59.4 0.0 collective-permute-done.16
  59.4 0.5 collective-permute-done.15
  59.9 0.0 collective-permute-done.14
  60.0 4.2 %collective-permute-start.17 = (f32[1024,128]{1,0:T(8,128)S(1)}, f32[1024,128]{1,0:T(8,128)S(1)}, u32[]{:S(2)}, u32[]{:S(2)}) collective-permute-start(f32[1024,128]{1,0:T(8,128)S(1)} %pad_maximum_fusion.value_ref), channel_id=1, source_target_pairs={{0,8},{8,0},{16,24},{24,16},{32,40},{40,32},{48,56},{56,48},{64,72... | collective-permute-start | bytes 1572872 | tf_op jit(solution)/shard_map/ppermute | solution.py:365
  64.1 1.0 %shard_map.50.refs_0_ = f32[64,4096]{1,0:T(8,128)} custom-call(f32[64,64]{1,0:T(8,128)S(1)} %shard_map.48.inverse_ref, f32[1024,128]{1,0:T(8,128)S(1)} %pad_maximum_fusion.value_ref), custom_call_target="tpu_custom_call" | custom-call | flops 50331648 | bytes 1048576 | tf_op jit(solution)/shard_map/pallas_call | solution.py:348
  65.2 0.5 collective-permute-done.17.value_ref
  65.7 1.0 %shard_map.51 = f32[64,4096]{1,0:T(8,128)} custom-call(f32[64,64]{1,0:T(8,128)S(1)} %shard_map.48.inverse_ref, f32[1024,128]{1,0:T(8,128)S(1)} %collective-permute-done.17.value_ref, f32[64,4096]{1,0:T(8,128)} %shard_map.50.refs_0_), custom_call_target="tpu_custom_call", output_to_operand_aliasing={{}: (2, {})} | custom-call | flops 50331648 | bytes 1048576 | tf_op jit(solution)/shard_map/pallas_call | solution.py:348
  (11 shorter events, 0.2 us)
Async XLA Ops:
  6.3 8.4 %collective-permute-start = (f32[96,128]{1,0:T(8,128)S(1)}, f32[96,128]{1,0:T(8,128)S(1)}, u32[]{:S(2)}, u32[]{:S(2)}) collective-permute-start(f32[96,128]{1,0:T(8,128)S(1)} %get-tuple-element.14), channel_id=1, source_target_pairs={{0,3},{1,2},{2,1},{3,0},{4,7},{5,6},{6,5},{7,4},{8,11},{9,10},{10,... | collective-permute-start | bytes 147464 | tf_op jit(solution)/shard_map/ppermute | solution.py:361
  11.6 4.5 %collective-permute-start.1 = (f32[96,128]{1,0:T(8,128)S(1)}, f32[96,128]{1,0:T(8,128)S(1)}, u32[]{:S(2)}, u32[]{:S(2)}) collective-permute-start(f32[96,128]{1,0:T(8,128)S(1)} %get-tuple-element.15), channel_id=1, source_target_pairs={{0,2},{1,3},{2,0},{3,1},{4,6},{5,7},{6,4},{7,5},{8,10},{9,11},{10,... | collective-permute-start | bytes 147464 | tf_op jit(solution)/shard_map/ppermute | solution.py:361
  11.6 4.5 %collective-permute-start.2 = (f32[96,128]{1,0:T(8,128)S(1)}, f32[96,128]{1,0:T(8,128)S(1)}, u32[]{:S(2)}, u32[]{:S(2)}) collective-permute-start(f32[96,128]{1,0:T(8,128)S(1)} %get-tuple-element.16), channel_id=1, source_target_pairs={{0,1},{1,0},{2,3},{3,2},{4,5},{5,4},{6,7},{7,6},{8,9},{9,8},{10,11... | collective-permute-start | bytes 147464 | tf_op jit(solution)/shard_map/ppermute | solution.py:361
  16.1 6.1 %collective-permute-start.3 = (f32[96,128]{1,0:T(8,128)S(1)}, f32[96,128]{1,0:T(8,128)S(1)}, u32[]{:S(2)}, u32[]{:S(2)}) collective-permute-start(f32[96,128]{1,0:T(8,128)S(1)} %add_add_fusion.1), channel_id=1, source_target_pairs={{0,7},{1,6},{2,5},{3,4},{4,3},{5,2},{6,1},{7,0},{8,15},{9,14},{10,... | collective-permute-start | bytes 147464 | tf_op jit(solution)/shard_map/ppermute | solution.py:361
  22.2 4.9 %collective-permute-start.6 = (f32[96,128]{1,0:T(8,128)S(1)}, f32[96,128]{1,0:T(8,128)S(1)}, u32[]{:S(2)}, u32[]{:S(2)}) collective-permute-start(f32[96,128]{1,0:T(8,128)S(1)} %add.36.sample_ref.s0), channel_id=1, source_target_pairs={{0,3},{1,2},{2,1},{3,0},{4,7},{5,6},{6,5},{7,4},{8,11},{9,10},{10,... | collective-permute-start | bytes 147464 | tf_op jit(solution)/shard_map/ppermute | solution.py:361
  23.9 4.2 %collective-permute-start.5 = (f32[96,128]{1,0:T(8,128)S(1)}, f32[96,128]{1,0:T(8,128)S(1)}, u32[]{:S(2)}, u32[]{:S(2)}) collective-permute-start(f32[96,128]{1,0:T(8,128)S(1)} %add.36.sample_ref.s0), channel_id=1, source_target_pairs={{0,1},{1,0},{2,3},{3,2},{4,5},{5,4},{6,7},{7,6},{8,9},{9,8},{10,11... | collective-permute-start | bytes 147464 | tf_op jit(solution)/shard_map/ppermute | solution.py:361
  23.9 5.1 %collective-permute-start.4 = (f32[96,128]{1,0:T(8,128)S(1)}, f32[96,128]{1,0:T(8,128)S(1)}, u32[]{:S(2)}, u32[]{:S(2)}) collective-permute-start(f32[96,128]{1,0:T(8,128)S(1)} %add.36.sample_ref.s0), channel_id=1, source_target_pairs={{0,2},{1,3},{2,0},{3,1},{4,6},{5,7},{6,4},{7,5},{8,10},{9,11},{10,... | collective-permute-start | bytes 147464 | tf_op jit(solution)/shard_map/ppermute | solution.py:361
  29.9 5.4 %collective-permute-start.7 = (f32[1056,128]{1,0:T(8,128)S(1)}, f32[1056,128]{1,0:T(8,128)S(1)}, u32[]{:S(2)}, u32[]{:S(2)}) collective-permute-start(f32[1056,128]{1,0:T(8,128)S(1)} %shard_map.46.sent_ref), channel_id=1, source_target_pairs={{0,8},{8,0},{16,24},{24,16},{32,40},{40,32},{48,56},{56,48},{64,72... | collective-permute-start | bytes 1622024 | tf_op jit(solution)/shard_map/ppermute | solution.py:365
  35.5 6.5 %collective-permute-start.10 = (f32[288,128]{1,0:T(8,128)S(1)}, f32[288,128]{1,0:T(8,128)S(1)}, u32[]{:S(2)}, u32[]{:S(2)}) collective-permute-start(f32[288,128]{1,0:T(8,128)S(1)} %concatenate.20), channel_id=1, source_target_pairs={{0,192},{8,56},{16,208},{24,40},{32,224},{40,24},{48,240},{56,8},{... | collective-permute-start | bytes 442376 | tf_op jit(solution)/shard_map/ppermute | solution.py:365
  38.3 5.9 %collective-permute-start.8 = (f32[288,128]{1,0:T(8,128)S(1)}, f32[288,128]{1,0:T(8,128)S(1)}, u32[]{:S(2)}, u32[]{:S(2)}) collective-permute-start(f32[288,128]{1,0:T(8,128)S(1)} %get-tuple-element.25), channel_id=1, source_target_pairs={{0,128},{8,40},{16,144},{24,56},{32,160},{40,8},{48,176},{56,24},{... | collective-permute-start | bytes 442376 | tf_op jit(solution)/shard_map/ppermute | solution.py:365
  38.8 5.4 %collective-permute-start.9 = (f32[288,128]{1,0:T(8,128)S(1)}, f32[288,128]{1,0:T(8,128)S(1)}, u32[]{:S(2)}, u32[]{:S(2)}) collective-permute-start(f32[288,128]{1,0:T(8,128)S(1)} %get-tuple-element.26), channel_id=1, source_target_pairs={{0,64},{8,24},{16,80},{24,8},{32,96},{40,56},{48,112},{56,40},{64,... | collective-permute-start | bytes 442376 | tf_op jit(solution)/shard_map/ppermute | solution.py:365
  44.2 5.9 %collective-permute-start.13 = (f32[288,128]{1,0:T(8,128)S(1)}, f32[288,128]{1,0:T(8,128)S(1)}, u32[]{:S(2)}, u32[]{:S(2)}) collective-permute-start(f32[288,128]{1,0:T(8,128)S(1)} %fusion.2), channel_id=1, source_target_pairs={{0,48},{8,200},{16,32},{24,216},{32,16},{40,232},{48,0},{56,248},{... | collective-permute-start | bytes 442376 | tf_op jit(solution)/shard_map/ppermute | solution.py:365
  46.5 5.5 %collective-permute-start.12 = (f32[288,128]{1,0:T(8,128)S(1)}, f32[288,128]{1,0:T(8,128)S(1)}, u32[]{:S(2)}, u32[]{:S(2)}) collective-permute-start(f32[288,128]{1,0:T(8,128)S(1)} %fusion.2), channel_id=1, source_target_pairs={{0,32},{8,136},{16,48},{24,152},{32,0},{40,168},{48,16},{56,184},{... | collective-permute-start | bytes 442376 | tf_op jit(solution)/shard_map/ppermute | solution.py:365
  47.0 5.0 %collective-permute-start.11 = (f32[288,128]{1,0:T(8,128)S(1)}, f32[288,128]{1,0:T(8,128)S(1)}, u32[]{:S(2)}, u32[]{:S(2)}) collective-permute-start(f32[288,128]{1,0:T(8,128)S(1)} %fusion.2), channel_id=1, source_target_pairs={{0,16},{8,72},{16,0},{24,88},{32,48},{40,104},{48,32},{56,120},{64... | collective-permute-start | bytes 442376 | tf_op jit(solution)/shard_map/ppermute | solution.py:365
  52.1 7.4 %collective-permute-start.16 = (f32[256,128]{1,0:T(8,128)S(1)}, f32[256,128]{1,0:T(8,128)S(1)}, u32[]{:S(2)}, u32[]{:S(2)}) collective-permute-start(f32[256,128]{1,0:T(8,128)S(1)} %slice.30), channel_id=1, source_target_pairs={{0,192},{8,56},{16,208},{24,40},{32,224},{40,24},{48,240},{56,8},{... | collective-permute-start | bytes 393224 | tf_op jit(solution)/shard_map/ppermute | solution.py:365
  54.6 5.3 %collective-permute-start.15 = (f32[256,128]{1,0:T(8,128)S(1)}, f32[256,128]{1,0:T(8,128)S(1)}, u32[]{:S(2)}, u32[]{:S(2)}) collective-permute-start(f32[256,128]{1,0:T(8,128)S(1)} %slice.30), channel_id=1, source_target_pairs={{0,128},{8,40},{16,144},{24,56},{32,160},{40,8},{48,176},{56,24},{... | collective-permute-start | bytes 393224 | tf_op jit(solution)/shard_map/ppermute | solution.py:365
  54.7 5.3 %collective-permute-start.14 = (f32[256,128]{1,0:T(8,128)S(1)}, f32[256,128]{1,0:T(8,128)S(1)}, u32[]{:S(2)}, u32[]{:S(2)}) collective-permute-start(f32[256,128]{1,0:T(8,128)S(1)} %slice.30), channel_id=1, source_target_pairs={{0,64},{8,24},{16,80},{24,8},{32,96},{40,56},{48,112},{56,40},{64,... | collective-permute-start | bytes 393224 | tf_op jit(solution)/shard_map/ppermute | solution.py:365
  60.0 5.7 %collective-permute-start.17 = (f32[1024,128]{1,0:T(8,128)S(1)}, f32[1024,128]{1,0:T(8,128)S(1)}, u32[]{:S(2)}, u32[]{:S(2)}) collective-permute-start(f32[1024,128]{1,0:T(8,128)S(1)} %pad_maximum_fusion.value_ref), channel_id=1, source_target_pairs={{0,8},{8,0},{16,24},{24,16},{32,40},{40,32},{48,56},{56,48},{64,72... | collective-permute-start | bytes 1572872 | tf_op jit(solution)/shard_map/ppermute | solution.py:365

commit v6 on v5

--- a/solution.py
+++ b/solution.py
@@ -215,12 +215,12 @@
     whole = (K, columns)
     blocks = (BLOCKS // 2 * K + K // 2, LANES)
     begun = term_call(term_kernel, whole, (quarters[0], kept_terms), cost)
-    for index in (0, 2):
+    for index in (0, 1):
         kernel = functools.partial(next_term_kernel, index)
         begun = term_call(kernel, whole, (quarters[1 + index], sent_terms, begun), cost)
-    sent = term_call(functools.partial(sent_half_kernel, 1), blocks, (*quarters, sent_terms, begun), less)
-    kernel = functools.partial(kept_half_kernel, 1)
-    kept = term_call(kernel, blocks, (quarters[2], sent_terms, begun, sent), less)
+    sent = term_call(functools.partial(sent_half_kernel, 2), blocks, (*quarters, sent_terms, begun), less)
+    kernel = functools.partial(kept_half_kernel, 2)
+    kept = term_call(kernel, blocks, (quarters[3], sent_terms, begun, sent), less)
     return kept, sent
 
 

time: 66.9 us -> 66.4 us (level)
  starting transfers between devices: 32.1 us -> 31.3 us
    ppermute x11, starting transfers between devices: 18.2 us -> 17.4 us  [along_row(): lax.ppermute(value, 'row', [(i, i ^ masks[i % 2]) for i in range(32)])]
  transfers between devices with their start and end apart: 18 -> 18, of which waited for: 10 -> 11; matrix products, arithmetic and copies ran while one was open for 0% -> 0% of each run, Pallas kernels for 17% -> 17%
where the time goes in v6:
time: 66.4 us; the launch traced here: 66.3 us
  starting transfers between devices  31.3 us (47%)
  Pallas kernels  18.8 us (28%)
  waiting for transfers between devices  15 us (23%)
  between operations  0.94 us (1%)
    ppermute x11, starting transfers between devices, along_row(): lax.ppermute(value, 'row', [(i, i ^ masks[i % 2]) for i in range(32)])  17.4 us
    ppermute x7, starting transfers between devices, along_col(): return lax.ppermute(value, 'col', [(i, i ^ mask) for i in range(8)])  13.9 us
    ppermute x11, waiting for transfers between devices, along_row(): lax.ppermute(value, 'row', [(i, i ^ masks[i % 2]) for i in range(32)])  11.5 us
    pallas_call x1, Pallas kernels, partial_samples(): pl.pallas_call(send_kernel, out_shape=[sample] * len(SENT) + [jax.ShapeDt...  5.71 us
    pallas_call x5, Pallas kernels, term_call(): pl.pallas_call(kernel, out_shape=jax.ShapeDtypeStruct(shape, F32), in_spe...  4.3 us
    ppermute x7, waiting for transfers between devices, along_col(): return lax.ppermute(value, 'col', [(i, i ^ mask) for i in range(8)])  3.45 us
    pallas_call x1, Pallas kernels, partial_samples(): pl.pallas_call(keep_kernel, out_shape=[sample, jax.ShapeDtypeStruct((2 *...  2.72 us
    pallas_call x1, Pallas kernels, inverse_of(): pl.pallas_call(inverse_kernel, out_shape=jax.ShapeDtypeStruct((K, K), F32...  2.67 us
  transfers between devices with their start and end apart: 18, of which 11 were waited for; matrix products, arithmetic and copies ran while one was open for 0% of the time, Pallas kernels for 17%

profile of v6, /device:TPU:1, one launch (start us, length us, event | category | flops | bytes accessed | tf_op | source)
XLA Modules:
  0.0 66.3 jit_solution(1543625099982908197)
XLA Ops:
  0.6 5.7 %shard_map.41 = (f32[96,128]{1,0:T(8,128)S(1)}, f32[96,128]{1,0:T(8,128)S(1)}, f32[96,128]{1,0:T(8,128)S(1)}, bf16[1152,4096]{1,0:T(8,128)(2,1)S(1)}, bf16[4096,128]{1,0:T(8,128)(2,1)S(1)}) custom-call(f32[768,4096]{1,0:T(8,128)} %data_ref.3, f32[64,4096]{1,0:T(8,128)} %bitcast.2), custom_call_target="tpu_custom_call" | custom-call | flops 1207959552 | bytes 9437184 | tf_op jit(solution)/shard_map/pallas_call | solution.py:120
  6.3 5.3 %collective-permute-start = (f32[96,128]{1,0:T(8,128)S(1)}, f32[96,128]{1,0:T(8,128)S(1)}, u32[]{:S(2)}, u32[]{:S(2)}) collective-permute-start(f32[96,128]{1,0:T(8,128)S(1)} %get-tuple-element.14), channel_id=1, source_target_pairs={{0,3},{1,2},{2,1},{3,0},{4,7},{5,6},{6,5},{7,4},{8,11},{9,10},{10,... | collective-permute-start | bytes 147464 | tf_op jit(solution)/shard_map/ppermute | solution.py:361
  11.6 0.0 collective-permute-start.1
  11.6 0.4 collective-permute-start.2
  12.0 2.7 %shard_map.42 = (f32[96,128]{1,0:T(8,128)S(1)}, bf16[384,4096]{1,0:T(8,128)(2,1)S(1)}) custom-call(f32[768,4096]{1,0:T(8,128)} %data_ref.3, bf16[4096,128]{1,0:T(8,128)(2,1)S(1)} %get-tuple-element.12.weights_ref), custom_call_target="tpu_custom_call" | custom-call | flops 402653184 | bytes 3145728 | tf_op jit(solution)/shard_map/pallas_call | solution.py:134
  14.7 0.0 collective-permute-done
  14.7 1.3 %collective-permute-done.1 = f32[96,128]{1,0:T(8,128)S(1)} collective-permute-done((f32[96,128]{1,0:T(8,128)S(1)}, f32[96,128]{1,0:T(8,128)S(1)}, u32[]{:S(2)}, u32[]{:S(2)}) %collective-permute-start.1) | collective-permute-done | bytes 49184 | tf_op jit(solution)/shard_map/ppermute | solution.py:361
  16.1 0.0 collective-permute-done.2
  16.1 4.6 %collective-permute-start.3 = (f32[96,128]{1,0:T(8,128)S(1)}, f32[96,128]{1,0:T(8,128)S(1)}, u32[]{:S(2)}, u32[]{:S(2)}) collective-permute-start(f32[96,128]{1,0:T(8,128)S(1)} %add_add_fusion.1), channel_id=1, source_target_pairs={{0,7},{1,6},{2,5},{3,4},{4,3},{5,2},{6,1},{7,0},{8,15},{9,14},{10,... | collective-permute-start | bytes 147464 | tf_op jit(solution)/shard_map/ppermute | solution.py:361
  20.7 1.5 %collective-permute-done.3 = f32[96,128]{1,0:T(8,128)S(1)} collective-permute-done((f32[96,128]{1,0:T(8,128)S(1)}, f32[96,128]{1,0:T(8,128)S(1)}, u32[]{:S(2)}, u32[]{:S(2)}) %collective-permute-start.3) | collective-permute-done | bytes 49184 | tf_op jit(solution)/shard_map/ppermute | solution.py:361
  22.2 1.7 %collective-permute-start.6 = (f32[96,128]{1,0:T(8,128)S(1)}, f32[96,128]{1,0:T(8,128)S(1)}, u32[]{:S(2)}, u32[]{:S(2)}) collective-permute-start(f32[96,128]{1,0:T(8,128)S(1)} %add.36.sample_ref.s0), channel_id=1, source_target_pairs={{0,3},{1,2},{2,1},{3,0},{4,7},{5,6},{6,5},{7,4},{8,11},{9,10},{10,... | collective-permute-start | bytes 147464 | tf_op jit(solution)/shard_map/ppermute | solution.py:361
  23.9 0.0 collective-permute-start.5
  23.9 1.9 %collective-permute-start.4 = (f32[96,128]{1,0:T(8,128)S(1)}, f32[96,128]{1,0:T(8,128)S(1)}, u32[]{:S(2)}, u32[]{:S(2)}) collective-permute-start(f32[96,128]{1,0:T(8,128)S(1)} %add.36.sample_ref.s0), channel_id=1, source_target_pairs={{0,1},{1,0},{2,3},{3,2},{4,5},{5,4},{6,7},{7,6},{8,9},{9,8},{10,11... | collective-permute-start | bytes 147464 | tf_op jit(solution)/shard_map/ppermute | solution.py:361
  25.8 0.9 %shard_map.43.begun_ref = f32[64,4096]{1,0:T(8,128)S(1)} custom-call(f32[96,128]{1,0:T(8,128)S(1)} %add.36.sample_ref.s0, bf16[384,4096]{1,0:T(8,128)(2,1)S(1)} %get-tuple-element.18.terms_ref), custom_call_target="tpu_custom_call" | custom-call | flops 402653184 | bytes 3145728 | tf_op jit(solution)/shard_map/pallas_call | solution.py:202
  26.8 0.3 collective-permute-done.6.sample_ref.s3
  27.0 0.9 %shard_map.44.begun_ref = f32[64,4096]{1,0:T(8,128)S(1)} custom-call(f32[96,128]{1,0:T(8,128)S(1)} %collective-permute-done.6.sample_ref.s3, bf16[1152,4096]{1,0:T(8,128)(2,1)S(1)} %get-tuple-element.17.terms_ref, f32[64,4096]{1,0:T(8,128)S(1)} %shard_map.43.begun_ref), custom_call_target="tpu_custom_call" | custom-call | flops 402653184 | bytes 3145728 | tf_op jit(solution)/shard_map/pallas_call | solution.py:202
  28.0 0.3 collective-permute-done.5.sample_ref.s2
  28.3 0.9 %shard_map.45.begun_ref = f32[64,4096]{1,0:T(8,128)S(1)} custom-call(f32[96,128]{1,0:T(8,128)S(1)} %collective-permute-done.5.sample_ref.s2, bf16[1152,4096]{1,0:T(8,128)(2,1)S(1)} %get-tuple-element.17.terms_ref, f32[64,4096]{1,0:T(8,128)S(1)} %shard_map.44.begun_ref), custom_call_target="tpu_custom_call" | custom-call | flops 402653184 | bytes 3145728 | tf_op jit(solution)/shard_map/pallas_call | solution.py:202
  29.2 0.0 collective-permute-done.4.s1.sample_ref
  29.2 0.9 %shard_map.46.sent_ref = f32[1056,128]{1,0:T(8,128)S(1)} custom-call(f32[96,128]{1,0:T(8,128)S(1)} %add.36.sample_ref.s0, f32[96,128]{1,0:T(8,128)S(1)} %collective-permute-done.6.sample_ref.s3, f32[96,128]{1,0:T(8,128)S(1)} %collective-permute-done.5.sample_ref.s2, f32[96,128]{1,0:T(8,128)S(1)} %collective-permute-done.4.s1.sample_ref, ...), custom_call_target="tpu_custom_call" | custom-call | flops 201326592 | bytes 1572864 | tf_op jit(solution)/shard_map/pallas_call | solution.py:202
  30.1 3.1 %collective-permute-start.7 = (f32[1056,128]{1,0:T(8,128)S(1)}, f32[1056,128]{1,0:T(8,128)S(1)}, u32[]{:S(2)}, u32[]{:S(2)}) collective-permute-start(f32[1056,128]{1,0:T(8,128)S(1)} %shard_map.46.sent_ref), channel_id=1, source_target_pairs={{0,8},{8,0},{16,24},{24,16},{32,40},{40,32},{48,56},{56,48},{64,72... | collective-permute-start | bytes 1622024 | tf_op jit(solution)/shard_map/ppermute | solution.py:365
  33.2 0.7 %shard_map.47 = f32[1056,128]{1,0:T(8,128)S(1)} custom-call(f32[96,128]{1,0:T(8,128)S(1)} %collective-permute-done.4.s1.sample_ref, bf16[1152,4096]{1,0:T(8,128)(2,1)S(1)} %get-tuple-element.17.terms_ref, f32[64,4096]{1,0:T(8,128)S(1)} %shard_map.45.begun_ref, f32[1056,128]{1,0:T(8,128)S(1)} %shard_map.46.sent_ref), custom_call_target="tpu_custom_call" | custom-call | flops 201326592 | bytes 1572864 | tf_op jit(solution)/shard_map/pallas_call | solution.py:202
  33.9 0.9 %collective-permute-done.7 = f32[1056,128]{1,0:T(8,128)S(1)} collective-permute-done((f32[1056,128]{1,0:T(8,128)S(1)}, f32[1056,128]{1,0:T(8,128)S(1)}, u32[]{:S(2)}, u32[]{:S(2)}) %collective-permute-start.7) | collective-permute-done | bytes 540704 | tf_op jit(solution)/shard_map/ppermute | solution.py:365
  34.8 0.1 add.37
  34.9 2.8 %collective-permute-start.10 = (f32[288,128]{1,0:T(8,128)S(1)}, f32[288,128]{1,0:T(8,128)S(1)}, u32[]{:S(2)}, u32[]{:S(2)}) collective-permute-start(f32[288,128]{1,0:T(8,128)S(1)} %concatenate.20), channel_id=1, source_target_pairs={{0,192},{8,56},{16,208},{24,40},{32,224},{40,24},{48,240},{56,8},{... | collective-permute-start | bytes 442376 | tf_op jit(solution)/shard_map/ppermute | solution.py:365
  37.7 0.4 collective-permute-start.8
  38.2 0.2 collective-permute-start.9
  38.4 3.0 %collective-permute-done.10 = f32[288,128]{1,0:T(8,128)S(1)} collective-permute-done((f32[288,128]{1,0:T(8,128)S(1)}, f32[288,128]{1,0:T(8,128)S(1)}, u32[]{:S(2)}, u32[]{:S(2)}) %collective-permute-start.10) | collective-permute-done | bytes 147488 | tf_op jit(solution)/shard_map/ppermute | solution.py:365
  41.4 2.2 %collective-permute-done.8 = f32[288,128]{1,0:T(8,128)S(1)} collective-permute-done((f32[288,128]{1,0:T(8,128)S(1)}, f32[288,128]{1,0:T(8,128)S(1)}, u32[]{:S(2)}, u32[]{:S(2)}) %collective-permute-start.8) | collective-permute-done | bytes 147488 | tf_op jit(solution)/shard_map/ppermute | solution.py:365
  43.6 0.0 collective-permute-done.9
  43.7 2.3 %collective-permute-start.13 = (f32[288,128]{1,0:T(8,128)S(1)}, f32[288,128]{1,0:T(8,128)S(1)}, u32[]{:S(2)}, u32[]{:S(2)}) collective-permute-start(f32[288,128]{1,0:T(8,128)S(1)} %fusion.2), channel_id=1, source_target_pairs={{0,48},{8,200},{16,32},{24,216},{32,16},{40,232},{48,0},{56,248},{... | collective-permute-start | bytes 442376 | tf_op jit(solution)/shard_map/ppermute | solution.py:365
  45.9 0.5 collective-permute-start.12
  46.4 0.6 collective-permute-start.11
  47.0 2.6 %collective-permute-done.13 = f32[288,128]{1,0:T(8,128)S(1)} collective-permute-done((f32[288,128]{1,0:T(8,128)S(1)}, f32[288,128]{1,0:T(8,128)S(1)}, u32[]{:S(2)}, u32[]{:S(2)}) %collective-permute-start.13) | collective-permute-done | bytes 147488 | tf_op jit(solution)/shard_map/ppermute | solution.py:365
  49.6 1.8 %collective-permute-done.12 = f32[288,128]{1,0:T(8,128)S(1)} collective-permute-done((f32[288,128]{1,0:T(8,128)S(1)}, f32[288,128]{1,0:T(8,128)S(1)}, u32[]{:S(2)}, u32[]{:S(2)}) %collective-permute-start.12) | collective-permute-done | bytes 147488 | tf_op jit(solution)/shard_map/ppermute | solution.py:365
  51.4 0.0 collective-permute-done.11
  51.5 2.5 %collective-permute-start.16 = (f32[256,128]{1,0:T(8,128)S(1)}, f32[256,128]{1,0:T(8,128)S(1)}, u32[]{:S(2)}, u32[]{:S(2)}) collective-permute-start(f32[256,128]{1,0:T(8,128)S(1)} %slice.30), channel_id=1, source_target_pairs={{0,192},{8,56},{16,208},{24,40},{32,224},{40,24},{48,240},{56,8},{... | collective-permute-start | bytes 393224 | tf_op jit(solution)/shard_map/ppermute | solution.py:365
  54.0 0.1 collective-permute-start.15
  54.1 0.8 %collective-permute-start.14 = (f32[256,128]{1,0:T(8,128)S(1)}, f32[256,128]{1,0:T(8,128)S(1)}, u32[]{:S(2)}, u32[]{:S(2)}) collective-permute-start(f32[256,128]{1,0:T(8,128)S(1)} %slice.30), channel_id=1, source_target_pairs={{0,64},{8,24},{16,80},{24,8},{32,96},{40,56},{48,112},{56,40},{64,... | collective-permute-start | bytes 393224 | tf_op jit(solution)/shard_map/ppermute | solution.py:365
  54.8 2.7 %shard_map.48.inverse_ref = f32[64,64]{1,0:T(8,128)S(1)} custom-call(f32[32,128]{1,0:T(8,128)S(1)} %slice.31.gram_ref), custom_call_target="tpu_custom_call" | custom-call | flops 26214400 | bytes 32768 | tf_op jit(solution)/shard_map/pallas_call | solution.py:289
  57.5 1.3 %shard_map.49 = f32[64,768]{1,0:T(8,128)} custom-call(f32[64,64]{1,0:T(8,128)S(1)} %shard_map.48.inverse_ref, f32[96,128]{1,0:T(8,128)S(1)} %add.36.sample_ref.s0, f32[96,128]{1,0:T(8,128)S(1)} %collective-permute-done.6.sample_ref.s3, f32[96,128]{1,0:T(8,128)S(1)} %collective-permute-done.5.sample_ref.s2, f32[96,128]{1,0:T(8,128)S(1)} %collective-permute-done.4.s1.sample_ref), custom_call_target="tpu_custom_call" | custom-call | flops 37748736 | bytes 393216 | tf_op jit(solution)/shard_map/pallas_call | solution.py:316
  58.8 0.0 collective-permute-done.16
  58.9 0.5 collective-permute-done.15
  59.3 0.0 collective-permute-done.14
  59.4 4.2 %collective-permute-start.17 = (f32[1024,128]{1,0:T(8,128)S(1)}, f32[1024,128]{1,0:T(8,128)S(1)}, u32[]{:S(2)}, u32[]{:S(2)}) collective-permute-start(f32[1024,128]{1,0:T(8,128)S(1)} %pad_maximum_fusion.value_ref), channel_id=1, source_target_pairs={{0,8},{8,0},{16,24},{24,16},{32,40},{40,32},{48,56},{56,48},{64,72... | collective-permute-start | bytes 1572872 | tf_op jit(solution)/shard_map/ppermute | solution.py:365
  63.5 1.0 %shard_map.50.refs_0_ = f32[64,4096]{1,0:T(8,128)} custom-call(f32[64,64]{1,0:T(8,128)S(1)} %shard_map.48.inverse_ref, f32[1024,128]{1,0:T(8,128)S(1)} %pad_maximum_fusion.value_ref), custom_call_target="tpu_custom_call" | custom-call | flops 50331648 | bytes 1048576 | tf_op jit(solution)/shard_map/pallas_call | solution.py:348
  64.6 0.5 collective-permute-done.17.value_ref
  65.1 1.0 %shard_map.51 = f32[64,4096]{1,0:T(8,128)} custom-call(f32[64,64]{1,0:T(8,128)S(1)} %shard_map.48.inverse_ref, f32[1024,128]{1,0:T(8,128)S(1)} %collective-permute-done.17.value_ref, f32[64,4096]{1,0:T(8,128)} %shard_map.50.refs_0_), custom_call_target="tpu_custom_call", output_to_operand_aliasing={{}: (2, {})} | custom-call | flops 50331648 | bytes 1048576 | tf_op jit(solution)/shard_map/pallas_call | solution.py:348
  (11 shorter events, 0.2 us)
Async XLA Ops:
  6.3 8.4 %collective-permute-start = (f32[96,128]{1,0:T(8,128)S(1)}, f32[96,128]{1,0:T(8,128)S(1)}, u32[]{:S(2)}, u32[]{:S(2)}) collective-permute-start(f32[96,128]{1,0:T(8,128)S(1)} %get-tuple-element.14), channel_id=1, source_target_pairs={{0,3},{1,2},{2,1},{3,0},{4,7},{5,6},{6,5},{7,4},{8,11},{9,10},{10,... | collective-permute-start | bytes 147464 | tf_op jit(solution)/shard_map/ppermute | solution.py:361
  11.6 4.5 %collective-permute-start.1 = (f32[96,128]{1,0:T(8,128)S(1)}, f32[96,128]{1,0:T(8,128)S(1)}, u32[]{:S(2)}, u32[]{:S(2)}) collective-permute-start(f32[96,128]{1,0:T(8,128)S(1)} %get-tuple-element.15), channel_id=1, source_target_pairs={{0,2},{1,3},{2,0},{3,1},{4,6},{5,7},{6,4},{7,5},{8,10},{9,11},{10,... | collective-permute-start | bytes 147464 | tf_op jit(solution)/shard_map/ppermute | solution.py:361
  11.6 4.5 %collective-permute-start.2 = (f32[96,128]{1,0:T(8,128)S(1)}, f32[96,128]{1,0:T(8,128)S(1)}, u32[]{:S(2)}, u32[]{:S(2)}) collective-permute-start(f32[96,128]{1,0:T(8,128)S(1)} %get-tuple-element.16), channel_id=1, source_target_pairs={{0,1},{1,0},{2,3},{3,2},{4,5},{5,4},{6,7},{7,6},{8,9},{9,8},{10,11... | collective-permute-start | bytes 147464 | tf_op jit(solution)/shard_map/ppermute | solution.py:361
  16.1 6.1 %collective-permute-start.3 = (f32[96,128]{1,0:T(8,128)S(1)}, f32[96,128]{1,0:T(8,128)S(1)}, u32[]{:S(2)}, u32[]{:S(2)}) collective-permute-start(f32[96,128]{1,0:T(8,128)S(1)} %add_add_fusion.1), channel_id=1, source_target_pairs={{0,7},{1,6},{2,5},{3,4},{4,3},{5,2},{6,1},{7,0},{8,15},{9,14},{10,... | collective-permute-start | bytes 147464 | tf_op jit(solution)/shard_map/ppermute | solution.py:361
  22.2 4.8 %collective-permute-start.6 = (f32[96,128]{1,0:T(8,128)S(1)}, f32[96,128]{1,0:T(8,128)S(1)}, u32[]{:S(2)}, u32[]{:S(2)}) collective-permute-start(f32[96,128]{1,0:T(8,128)S(1)} %add.36.sample_ref.s0), channel_id=1, source_target_pairs={{0,3},{1,2},{2,1},{3,0},{4,7},{5,6},{6,5},{7,4},{8,11},{9,10},{10,... | collective-permute-start | bytes 147464 | tf_op jit(solution)/shard_map/ppermute | solution.py:361
  23.9 4.4 %collective-permute-start.5 = (f32[96,128]{1,0:T(8,128)S(1)}, f32[96,128]{1,0:T(8,128)S(1)}, u32[]{:S(2)}, u32[]{:S(2)}) collective-permute-start(f32[96,128]{1,0:T(8,128)S(1)} %add.36.sample_ref.s0), channel_id=1, source_target_pairs={{0,2},{1,3},{2,0},{3,1},{4,6},{5,7},{6,4},{7,5},{8,10},{9,11},{10,... | collective-permute-start | bytes 147464 | tf_op jit(solution)/shard_map/ppermute | solution.py:361
  23.9 5.3 %collective-permute-start.4 = (f32[96,128]{1,0:T(8,128)S(1)}, f32[96,128]{1,0:T(8,128)S(1)}, u32[]{:S(2)}, u32[]{:S(2)}) collective-permute-start(f32[96,128]{1,0:T(8,128)S(1)} %add.36.sample_ref.s0), channel_id=1, source_target_pairs={{0,1},{1,0},{2,3},{3,2},{4,5},{5,4},{6,7},{7,6},{8,9},{9,8},{10,11... | collective-permute-start | bytes 147464 | tf_op jit(solution)/shard_map/ppermute | solution.py:361
  30.1 4.6 %collective-permute-start.7 = (f32[1056,128]{1,0:T(8,128)S(1)}, f32[1056,128]{1,0:T(8,128)S(1)}, u32[]{:S(2)}, u32[]{:S(2)}) collective-permute-start(f32[1056,128]{1,0:T(8,128)S(1)} %shard_map.46.sent_ref), channel_id=1, source_target_pairs={{0,8},{8,0},{16,24},{24,16},{32,40},{40,32},{48,56},{56,48},{64,72... | collective-permute-start | bytes 1622024 | tf_op jit(solution)/shard_map/ppermute | solution.py:365
  34.9 6.5 %collective-permute-start.10 = (f32[288,128]{1,0:T(8,128)S(1)}, f32[288,128]{1,0:T(8,128)S(1)}, u32[]{:S(2)}, u32[]{:S(2)}) collective-permute-start(f32[288,128]{1,0:T(8,128)S(1)} %concatenate.20), channel_id=1, source_target_pairs={{0,192},{8,56},{16,208},{24,40},{32,224},{40,24},{48,240},{56,8},{... | collective-permute-start | bytes 442376 | tf_op jit(solution)/shard_map/ppermute | solution.py:365
  37.7 5.9 %collective-permute-start.8 = (f32[288,128]{1,0:T(8,128)S(1)}, f32[288,128]{1,0:T(8,128)S(1)}, u32[]{:S(2)}, u32[]{:S(2)}) collective-permute-start(f32[288,128]{1,0:T(8,128)S(1)} %get-tuple-element.25), channel_id=1, source_target_pairs={{0,128},{8,40},{16,144},{24,56},{32,160},{40,8},{48,176},{56,24},{... | collective-permute-start | bytes 442376 | tf_op jit(solution)/shard_map/ppermute | solution.py:365
  38.2 5.4 %collective-permute-start.9 = (f32[288,128]{1,0:T(8,128)S(1)}, f32[288,128]{1,0:T(8,128)S(1)}, u32[]{:S(2)}, u32[]{:S(2)}) collective-permute-start(f32[288,128]{1,0:T(8,128)S(1)} %get-tuple-element.26), channel_id=1, source_target_pairs={{0,64},{8,24},{16,80},{24,8},{32,96},{40,56},{48,112},{56,40},{64,... | collective-permute-start | bytes 442376 | tf_op jit(solution)/shard_map/ppermute | solution.py:365
  43.7 5.9 %collective-permute-start.13 = (f32[288,128]{1,0:T(8,128)S(1)}, f32[288,128]{1,0:T(8,128)S(1)}, u32[]{:S(2)}, u32[]{:S(2)}) collective-permute-start(f32[288,128]{1,0:T(8,128)S(1)} %fusion.2), channel_id=1, source_target_pairs={{0,48},{8,200},{16,32},{24,216},{32,16},{40,232},{48,0},{56,248},{... | collective-permute-start | bytes 442376 | tf_op jit(solution)/shard_map/ppermute | solution.py:365
  45.9 5.5 %collective-permute-start.12 = (f32[288,128]{1,0:T(8,128)S(1)}, f32[288,128]{1,0:T(8,128)S(1)}, u32[]{:S(2)}, u32[]{:S(2)}) collective-permute-start(f32[288,128]{1,0:T(8,128)S(1)} %fusion.2), channel_id=1, source_target_pairs={{0,32},{8,136},{16,48},{24,152},{32,0},{40,168},{48,16},{56,184},{... | collective-permute-start | bytes 442376 | tf_op jit(solution)/shard_map/ppermute | solution.py:365
  46.4 5.0 %collective-permute-start.11 = (f32[288,128]{1,0:T(8,128)S(1)}, f32[288,128]{1,0:T(8,128)S(1)}, u32[]{:S(2)}, u32[]{:S(2)}) collective-permute-start(f32[288,128]{1,0:T(8,128)S(1)} %fusion.2), channel_id=1, source_target_pairs={{0,16},{8,72},{16,0},{24,88},{32,48},{40,104},{48,32},{56,120},{64... | collective-permute-start | bytes 442376 | tf_op jit(solution)/shard_map/ppermute | solution.py:365
  51.5 7.4 %collective-permute-start.16 = (f32[256,128]{1,0:T(8,128)S(1)}, f32[256,128]{1,0:T(8,128)S(1)}, u32[]{:S(2)}, u32[]{:S(2)}) collective-permute-start(f32[256,128]{1,0:T(8,128)S(1)} %slice.30), channel_id=1, source_target_pairs={{0,192},{8,56},{16,208},{24,40},{32,224},{40,24},{48,240},{56,8},{... | collective-permute-start | bytes 393224 | tf_op jit(solution)/shard_map/ppermute | solution.py:365
  54.0 5.3 %collective-permute-start.15 = (f32[256,128]{1,0:T(8,128)S(1)}, f32[256,128]{1,0:T(8,128)S(1)}, u32[]{:S(2)}, u32[]{:S(2)}) collective-permute-start(f32[256,128]{1,0:T(8,128)S(1)} %slice.30), channel_id=1, source_target_pairs={{0,128},{8,40},{16,144},{24,56},{32,160},{40,8},{48,176},{56,24},{... | collective-permute-start | bytes 393224 | tf_op jit(solution)/shard_map/ppermute | solution.py:365
  54.1 5.3 %collective-permute-start.14 = (f32[256,128]{1,0:T(8,128)S(1)}, f32[256,128]{1,0:T(8,128)S(1)}, u32[]{:S(2)}, u32[]{:S(2)}) collective-permute-start(f32[256,128]{1,0:T(8,128)S(1)} %slice.30), channel_id=1, source_target_pairs={{0,64},{8,24},{16,80},{24,8},{32,96},{40,56},{48,112},{56,40},{64,... | collective-permute-start | bytes 393224 | tf_op jit(solution)/shard_map/ppermute | solution.py:365
  59.4 5.7 %collective-permute-start.17 = (f32[1024,128]{1,0:T(8,128)S(1)}, f32[1024,128]{1,0:T(8,128)S(1)}, u32[]{:S(2)}, u32[]{:S(2)}) collective-permute-start(f32[1024,128]{1,0:T(8,128)S(1)} %pad_maximum_fusion.value_ref), channel_id=1, source_target_pairs={{0,8},{8,0},{16,24},{24,16},{32,40},{40,32},{48,56},{56,48},{64,72... | collective-permute-start | bytes 1572872 | tf_op jit(solution)/shard_map/ppermute | solution.py:365

commit v7 on v6

--- a/solution.py
+++ b/solution.py
@@ -84,6 +84,7 @@
 
 
 SENT = (3, 2, 1)
+ORDER = (0, 1, 3, 2)
 
 
 def send_kernel(data_ref, sketch_ref, out3, out2, out1, terms_ref, weights_ref, data, sketch, sems):
@@ -171,12 +172,12 @@
     size = terms_ref.shape[0] // len(SENT)
     _, left = left_of(sample_ref[...])
     width = PER_GROUP * LANES
-    for g in range(PER_GROUP):
+    for place, g in enumerate(ORDER):
         at = pl.ds(pl.multiple_of(group_place(first_group + g) * width, width), width)
         total = jnp.dot(left, terms_ref[pl.ds(index * size, size), at], preferred_element_type=F32)
         total = total[:K] + total[K:] + begun_ref[:, at]
         for t in range(PER_GROUP):
-            out_ref[pl.ds((g * PER_GROUP + t) * K, K), :] = total[:, t * LANES : (t + 1) * LANES]
+            out_ref[pl.ds((place * PER_GROUP + t) * K, K), :] = total[:, t * LANES : (t + 1) * LANES]
 
 
 def sent_half_kernel(index, s0, s3, s2, s1, terms_ref, begun_ref, out_ref):
@@ -382,9 +383,10 @@
     total = keep + along_row(send, CORE)
     size = PER_GROUP * K
     gram = total[4 * size :]
-    got = [along_row(jnp.concatenate([total[t * size : (t + 1) * size], gram]), FIRST[t]) for t in (2, 1, 3)]
+    places = {t: ORDER.index(t) * size for t in (3, 1, 2)}
+    got = [along_row(jnp.concatenate([total[p : p + size], gram]), FIRST[t]) for t, p in places.items()]
     total = jnp.concatenate([total[:size], gram]) + got[0] + got[1] + got[2]
-    got = [along_row(total, SECOND[t]) for t in (1, 2, 3)]
+    got = [along_row(total, SECOND[t]) for t in (1, 3, 2)]
     total = total + got[0] + got[1] + got[2]
 
     inverse = inverse_of(total[size:])

time: 66.4 us -> 66.1 us (level)
  waiting for transfers between devices: 15 us -> 14 us
  starting transfers between devices: 31.3 us -> 32 us
    ppermute x11, waiting for transfers between devices: 11.5 us -> 10.6 us  [along_row(): lax.ppermute(value, 'row', [(i, i ^ masks[i % 2]) for i in range(32)])]
    ppermute x11, starting transfers between devices: 17.4 us -> 18.1 us  [along_row(): lax.ppermute(value, 'row', [(i, i ^ masks[i % 2]) for i in range(32)])]
where the time goes in v7:
time: 66.1 us; the launch traced here: 66 us
  starting transfers between devices  32 us (48%)
  Pallas kernels  18.8 us (28%)
  waiting for transfers between devices  14 us (21%)
  between operations  0.94 us (1%)
    ppermute x11, starting transfers between devices, along_row(): lax.ppermute(value, 'row', [(i, i ^ masks[i % 2]) for i in range(32)])  18.1 us
    ppermute x7, starting transfers between devices, along_col(): return lax.ppermute(value, 'col', [(i, i ^ mask) for i in range(8)])  13.9 us
    ppermute x11, waiting for transfers between devices, along_row(): lax.ppermute(value, 'row', [(i, i ^ masks[i % 2]) for i in range(32)])  10.6 us
    pallas_call x1, Pallas kernels, partial_samples(): pl.pallas_call(send_kernel, out_shape=[sample] * len(SENT) + [jax.ShapeDt...  5.71 us
    pallas_call x5, Pallas kernels, term_call(): pl.pallas_call(kernel, out_shape=jax.ShapeDtypeStruct(shape, F32), in_spe...  4.3 us
    ppermute x7, waiting for transfers between devices, along_col(): return lax.ppermute(value, 'col', [(i, i ^ mask) for i in range(8)])  3.45 us
    pallas_call x1, Pallas kernels, partial_samples(): pl.pallas_call(keep_kernel, out_shape=[sample, jax.ShapeDtypeStruct((2 *...  2.72 us
    pallas_call x1, Pallas kernels, inverse_of(): pl.pallas_call(inverse_kernel, out_shape=jax.ShapeDtypeStruct((K, K), F32...  2.67 us
  transfers between devices with their start and end apart: 18, of which 11 were waited for; matrix products, arithmetic and copies ran while one was open for 0% of the time, Pallas kernels for 17%

profile of v7, /device:TPU:1, one launch (start us, length us, event | category | flops | bytes accessed | tf_op | source)
XLA Modules:
  0.0 66.0 jit_solution(18211159555639044080)
XLA Ops:
  0.6 5.7 %shard_map.41 = (f32[96,128]{1,0:T(8,128)S(1)}, f32[96,128]{1,0:T(8,128)S(1)}, f32[96,128]{1,0:T(8,128)S(1)}, bf16[1152,4096]{1,0:T(8,128)(2,1)S(1)}, bf16[4096,128]{1,0:T(8,128)(2,1)S(1)}) custom-call(f32[768,4096]{1,0:T(8,128)} %data_ref.3, f32[64,4096]{1,0:T(8,128)} %bitcast.2), custom_call_target="tpu_custom_call" | custom-call | flops 1207959552 | bytes 9437184 | tf_op jit(solution)/shard_map/pallas_call | solution.py:121
  6.3 5.3 %collective-permute-start = (f32[96,128]{1,0:T(8,128)S(1)}, f32[96,128]{1,0:T(8,128)S(1)}, u32[]{:S(2)}, u32[]{:S(2)}) collective-permute-start(f32[96,128]{1,0:T(8,128)S(1)} %get-tuple-element.14), channel_id=1, source_target_pairs={{0,3},{1,2},{2,1},{3,0},{4,7},{5,6},{6,5},{7,4},{8,11},{9,10},{10,... | collective-permute-start | bytes 147464 | tf_op jit(solution)/shard_map/ppermute | solution.py:362
  11.6 0.0 collective-permute-start.1
  11.6 0.4 collective-permute-start.2
  12.0 2.7 %shard_map.42 = (f32[96,128]{1,0:T(8,128)S(1)}, bf16[384,4096]{1,0:T(8,128)(2,1)S(1)}) custom-call(f32[768,4096]{1,0:T(8,128)} %data_ref.3, bf16[4096,128]{1,0:T(8,128)(2,1)S(1)} %get-tuple-element.12.weights_ref), custom_call_target="tpu_custom_call" | custom-call | flops 402653184 | bytes 3145728 | tf_op jit(solution)/shard_map/pallas_call | solution.py:135
  14.7 0.0 collective-permute-done
  14.7 1.3 %collective-permute-done.1 = f32[96,128]{1,0:T(8,128)S(1)} collective-permute-done((f32[96,128]{1,0:T(8,128)S(1)}, f32[96,128]{1,0:T(8,128)S(1)}, u32[]{:S(2)}, u32[]{:S(2)}) %collective-permute-start.1) | collective-permute-done | bytes 49184 | tf_op jit(solution)/shard_map/ppermute | solution.py:362
  16.1 0.0 collective-permute-done.2
  16.1 4.6 %collective-permute-start.3 = (f32[96,128]{1,0:T(8,128)S(1)}, f32[96,128]{1,0:T(8,128)S(1)}, u32[]{:S(2)}, u32[]{:S(2)}) collective-permute-start(f32[96,128]{1,0:T(8,128)S(1)} %add_add_fusion.1), channel_id=1, source_target_pairs={{0,7},{1,6},{2,5},{3,4},{4,3},{5,2},{6,1},{7,0},{8,15},{9,14},{10,... | collective-permute-start | bytes 147464 | tf_op jit(solution)/shard_map/ppermute | solution.py:362
  20.7 1.5 %collective-permute-done.3 = f32[96,128]{1,0:T(8,128)S(1)} collective-permute-done((f32[96,128]{1,0:T(8,128)S(1)}, f32[96,128]{1,0:T(8,128)S(1)}, u32[]{:S(2)}, u32[]{:S(2)}) %collective-permute-start.3) | collective-permute-done | bytes 49184 | tf_op jit(solution)/shard_map/ppermute | solution.py:362
  22.2 1.7 %collective-permute-start.6 = (f32[96,128]{1,0:T(8,128)S(1)}, f32[96,128]{1,0:T(8,128)S(1)}, u32[]{:S(2)}, u32[]{:S(2)}) collective-permute-start(f32[96,128]{1,0:T(8,128)S(1)} %add.36.sample_ref.s0), channel_id=1, source_target_pairs={{0,3},{1,2},{2,1},{3,0},{4,7},{5,6},{6,5},{7,4},{8,11},{9,10},{10,... | collective-permute-start | bytes 147464 | tf_op jit(solution)/shard_map/ppermute | solution.py:362
  23.9 0.0 collective-permute-start.5
  23.9 1.9 %collective-permute-start.4 = (f32[96,128]{1,0:T(8,128)S(1)}, f32[96,128]{1,0:T(8,128)S(1)}, u32[]{:S(2)}, u32[]{:S(2)}) collective-permute-start(f32[96,128]{1,0:T(8,128)S(1)} %add.36.sample_ref.s0), channel_id=1, source_target_pairs={{0,1},{1,0},{2,3},{3,2},{4,5},{5,4},{6,7},{7,6},{8,9},{9,8},{10,11... | collective-permute-start | bytes 147464 | tf_op jit(solution)/shard_map/ppermute | solution.py:362
  25.8 0.9 %shard_map.43.begun_ref = f32[64,4096]{1,0:T(8,128)S(1)} custom-call(f32[96,128]{1,0:T(8,128)S(1)} %add.36.sample_ref.s0, bf16[384,4096]{1,0:T(8,128)(2,1)S(1)} %get-tuple-element.18.terms_ref), custom_call_target="tpu_custom_call" | custom-call | flops 402653184 | bytes 3145728 | tf_op jit(solution)/shard_map/pallas_call | solution.py:203
  26.8 0.3 collective-permute-done.6.sample_ref.s3
  27.0 0.9 %shard_map.44.begun_ref = f32[64,4096]{1,0:T(8,128)S(1)} custom-call(f32[96,128]{1,0:T(8,128)S(1)} %collective-permute-done.6.sample_ref.s3, bf16[1152,4096]{1,0:T(8,128)(2,1)S(1)} %get-tuple-element.17.terms_ref, f32[64,4096]{1,0:T(8,128)S(1)} %shard_map.43.begun_ref), custom_call_target="tpu_custom_call" | custom-call | flops 402653184 | bytes 3145728 | tf_op jit(solution)/shard_map/pallas_call | solution.py:203
  28.0 0.3 collective-permute-done.5.sample_ref.s2
  28.3 0.9 %shard_map.45.begun_ref = f32[64,4096]{1,0:T(8,128)S(1)} custom-call(f32[96,128]{1,0:T(8,128)S(1)} %collective-permute-done.5.sample_ref.s2, bf16[1152,4096]{1,0:T(8,128)(2,1)S(1)} %get-tuple-element.17.terms_ref, f32[64,4096]{1,0:T(8,128)S(1)} %shard_map.44.begun_ref), custom_call_target="tpu_custom_call" | custom-call | flops 402653184 | bytes 3145728 | tf_op jit(solution)/shard_map/pallas_call | solution.py:203
  29.2 0.0 collective-permute-done.4.s1.sample_ref
  29.2 0.9 %shard_map.46.sent_ref = f32[1056,128]{1,0:T(8,128)S(1)} custom-call(f32[96,128]{1,0:T(8,128)S(1)} %add.36.sample_ref.s0, f32[96,128]{1,0:T(8,128)S(1)} %collective-permute-done.6.sample_ref.s3, f32[96,128]{1,0:T(8,128)S(1)} %collective-permute-done.5.sample_ref.s2, f32[96,128]{1,0:T(8,128)S(1)} %collective-permute-done.4.s1.sample_ref, ...), custom_call_target="tpu_custom_call" | custom-call | flops 201326592 | bytes 1572864 | tf_op jit(solution)/shard_map/pallas_call | solution.py:203
  30.1 3.1 %collective-permute-start.7 = (f32[1056,128]{1,0:T(8,128)S(1)}, f32[1056,128]{1,0:T(8,128)S(1)}, u32[]{:S(2)}, u32[]{:S(2)}) collective-permute-start(f32[1056,128]{1,0:T(8,128)S(1)} %shard_map.46.sent_ref), channel_id=1, source_target_pairs={{0,8},{8,0},{16,24},{24,16},{32,40},{40,32},{48,56},{56,48},{64,72... | collective-permute-start | bytes 1622024 | tf_op jit(solution)/shard_map/ppermute | solution.py:366
  33.2 0.7 %shard_map.47 = f32[1056,128]{1,0:T(8,128)S(1)} custom-call(f32[96,128]{1,0:T(8,128)S(1)} %collective-permute-done.4.s1.sample_ref, bf16[1152,4096]{1,0:T(8,128)(2,1)S(1)} %get-tuple-element.17.terms_ref, f32[64,4096]{1,0:T(8,128)S(1)} %shard_map.45.begun_ref, f32[1056,128]{1,0:T(8,128)S(1)} %shard_map.46.sent_ref), custom_call_target="tpu_custom_call" | custom-call | flops 201326592 | bytes 1572864 | tf_op jit(solution)/shard_map/pallas_call | solution.py:203
  33.9 0.9 %collective-permute-done.7 = f32[1056,128]{1,0:T(8,128)S(1)} collective-permute-done((f32[1056,128]{1,0:T(8,128)S(1)}, f32[1056,128]{1,0:T(8,128)S(1)}, u32[]{:S(2)}, u32[]{:S(2)}) %collective-permute-start.7) | collective-permute-done | bytes 540704 | tf_op jit(solution)/shard_map/ppermute | solution.py:366
  34.8 0.1 add.37
  34.9 3.0 %collective-permute-start.10 = (f32[288,128]{1,0:T(8,128)S(1)}, f32[288,128]{1,0:T(8,128)S(1)}, u32[]{:S(2)}, u32[]{:S(2)}) collective-permute-start(f32[288,128]{1,0:T(8,128)S(1)} %concatenate.20), channel_id=1, source_target_pairs={{0,128},{8,40},{16,144},{24,56},{32,160},{40,8},{48,176},{56,24},{... | collective-permute-start | bytes 442376 | tf_op jit(solution)/shard_map/ppermute | solution.py:366
  37.9 0.9 %collective-permute-start.8 = (f32[288,128]{1,0:T(8,128)S(1)}, f32[288,128]{1,0:T(8,128)S(1)}, u32[]{:S(2)}, u32[]{:S(2)}) collective-permute-start(f32[288,128]{1,0:T(8,128)S(1)} %get-tuple-element.25), channel_id=1, source_target_pairs={{0,192},{8,56},{16,208},{24,40},{32,224},{40,24},{48,240},{56,8},{... | collective-permute-start | bytes 442376 | tf_op jit(solution)/shard_map/ppermute | solution.py:366
  38.8 0.0 collective-permute-start.9
  38.8 2.0 %collective-permute-done.10 = f32[288,128]{1,0:T(8,128)S(1)} collective-permute-done((f32[288,128]{1,0:T(8,128)S(1)}, f32[288,128]{1,0:T(8,128)S(1)}, u32[]{:S(2)}, u32[]{:S(2)}) %collective-permute-start.10) | collective-permute-done | bytes 147488 | tf_op jit(solution)/shard_map/ppermute | solution.py:366
  40.8 2.7 %collective-permute-done.8 = f32[288,128]{1,0:T(8,128)S(1)} collective-permute-done((f32[288,128]{1,0:T(8,128)S(1)}, f32[288,128]{1,0:T(8,128)S(1)}, u32[]{:S(2)}, u32[]{:S(2)}) %collective-permute-start.8) | collective-permute-done | bytes 147488 | tf_op jit(solution)/shard_map/ppermute | solution.py:366
  43.5 0.0 collective-permute-done.9
  43.5 2.5 %collective-permute-start.13 = (f32[288,128]{1,0:T(8,128)S(1)}, f32[288,128]{1,0:T(8,128)S(1)}, u32[]{:S(2)}, u32[]{:S(2)}) collective-permute-start(f32[288,128]{1,0:T(8,128)S(1)} %fusion.2), channel_id=1, source_target_pairs={{0,32},{8,136},{16,48},{24,152},{32,0},{40,168},{48,16},{56,184},{... | collective-permute-start | bytes 442376 | tf_op jit(solution)/shard_map/ppermute | solution.py:366
  46.1 0.8 %collective-permute-start.12 = (f32[288,128]{1,0:T(8,128)S(1)}, f32[288,128]{1,0:T(8,128)S(1)}, u32[]{:S(2)}, u32[]{:S(2)}) collective-permute-start(f32[288,128]{1,0:T(8,128)S(1)} %fusion.2), channel_id=1, source_target_pairs={{0,48},{8,200},{16,32},{24,216},{32,16},{40,232},{48,0},{56,248},{... | collective-permute-start | bytes 442376 | tf_op jit(solution)/shard_map/ppermute | solution.py:366
  46.9 0.0 collective-permute-start.11
  46.9 2.2 %collective-permute-done.13 = f32[288,128]{1,0:T(8,128)S(1)} collective-permute-done((f32[288,128]{1,0:T(8,128)S(1)}, f32[288,128]{1,0:T(8,128)S(1)}, u32[]{:S(2)}, u32[]{:S(2)}) %collective-permute-start.13) | collective-permute-done | bytes 147488 | tf_op jit(solution)/shard_map/ppermute | solution.py:366
  49.1 2.2 %collective-permute-done.12 = f32[288,128]{1,0:T(8,128)S(1)} collective-permute-done((f32[288,128]{1,0:T(8,128)S(1)}, f32[288,128]{1,0:T(8,128)S(1)}, u32[]{:S(2)}, u32[]{:S(2)}) %collective-permute-start.12) | collective-permute-done | bytes 147488 | tf_op jit(solution)/shard_map/ppermute | solution.py:366
  51.3 0.0 collective-permute-done.11
  51.4 2.1 %collective-permute-start.16 = (f32[256,128]{1,0:T(8,128)S(1)}, f32[256,128]{1,0:T(8,128)S(1)}, u32[]{:S(2)}, u32[]{:S(2)}) collective-permute-start(f32[256,128]{1,0:T(8,128)S(1)} %slice.30), channel_id=1, source_target_pairs={{0,192},{8,56},{16,208},{24,40},{32,224},{40,24},{48,240},{56,8},{... | collective-permute-start | bytes 393224 | tf_op jit(solution)/shard_map/ppermute | solution.py:366
  53.5 0.5 collective-permute-start.15
  54.0 0.7 %collective-permute-start.14 = (f32[256,128]{1,0:T(8,128)S(1)}, f32[256,128]{1,0:T(8,128)S(1)}, u32[]{:S(2)}, u32[]{:S(2)}) collective-permute-start(f32[256,128]{1,0:T(8,128)S(1)} %slice.30), channel_id=1, source_target_pairs={{0,64},{8,24},{16,80},{24,8},{32,96},{40,56},{48,112},{56,40},{64,... | collective-permute-start | bytes 393224 | tf_op jit(solution)/shard_map/ppermute | solution.py:366
  54.7 2.7 %shard_map.48.inverse_ref = f32[64,64]{1,0:T(8,128)S(1)} custom-call(f32[32,128]{1,0:T(8,128)S(1)} %slice.31.gram_ref), custom_call_target="tpu_custom_call" | custom-call | flops 26214400 | bytes 32768 | tf_op jit(solution)/shard_map/pallas_call | solution.py:290
  57.4 1.3 %shard_map.49 = f32[64,768]{1,0:T(8,128)} custom-call(f32[64,64]{1,0:T(8,128)S(1)} %shard_map.48.inverse_ref, f32[96,128]{1,0:T(8,128)S(1)} %add.36.sample_ref.s0, f32[96,128]{1,0:T(8,128)S(1)} %collective-permute-done.6.sample_ref.s3, f32[96,128]{1,0:T(8,128)S(1)} %collective-permute-done.5.sample_ref.s2, f32[96,128]{1,0:T(8,128)S(1)} %collective-permute-done.4.s1.sample_ref), custom_call_target="tpu_custom_call" | custom-call | flops 37748736 | bytes 393216 | tf_op jit(solution)/shard_map/pallas_call | solution.py:317
  58.7 0.0 collective-permute-done.16
  58.7 0.1 collective-permute-done.15
  58.8 0.0 collective-permute-done.14
  58.9 4.4 %collective-permute-start.17 = (f32[1024,128]{1,0:T(8,128)S(1)}, f32[1024,128]{1,0:T(8,128)S(1)}, u32[]{:S(2)}, u32[]{:S(2)}) collective-permute-start(f32[1024,128]{1,0:T(8,128)S(1)} %pad_maximum_fusion.value_ref), channel_id=1, source_target_pairs={{0,8},{8,0},{16,24},{24,16},{32,40},{40,32},{48,56},{56,48},{64,72... | collective-permute-start | bytes 1572872 | tf_op jit(solution)/shard_map/ppermute | solution.py:366
  63.3 1.0 %shard_map.50.refs_0_ = f32[64,4096]{1,0:T(8,128)} custom-call(f32[64,64]{1,0:T(8,128)S(1)} %shard_map.48.inverse_ref, f32[1024,128]{1,0:T(8,128)S(1)} %pad_maximum_fusion.value_ref), custom_call_target="tpu_custom_call" | custom-call | flops 50331648 | bytes 1048576 | tf_op jit(solution)/shard_map/pallas_call | solution.py:349
  64.3 0.5 collective-permute-done.17.value_ref
  64.8 1.0 %shard_map.51 = f32[64,4096]{1,0:T(8,128)} custom-call(f32[64,64]{1,0:T(8,128)S(1)} %shard_map.48.inverse_ref, f32[1024,128]{1,0:T(8,128)S(1)} %collective-permute-done.17.value_ref, f32[64,4096]{1,0:T(8,128)} %shard_map.50.refs_0_), custom_call_target="tpu_custom_call", output_to_operand_aliasing={{}: (2, {})} | custom-call | flops 50331648 | bytes 1048576 | tf_op jit(solution)/shard_map/pallas_call | solution.py:349
  (11 shorter events, 0.2 us)
Async XLA Ops:
  6.3 8.4 %collective-permute-start = (f32[96,128]{1,0:T(8,128)S(1)}, f32[96,128]{1,0:T(8,128)S(1)}, u32[]{:S(2)}, u32[]{:S(2)}) collective-permute-start(f32[96,128]{1,0:T(8,128)S(1)} %get-tuple-element.14), channel_id=1, source_target_pairs={{0,3},{1,2},{2,1},{3,0},{4,7},{5,6},{6,5},{7,4},{8,11},{9,10},{10,... | collective-permute-start | bytes 147464 | tf_op jit(solution)/shard_map/ppermute | solution.py:362
  11.6 4.5 %collective-permute-start.1 = (f32[96,128]{1,0:T(8,128)S(1)}, f32[96,128]{1,0:T(8,128)S(1)}, u32[]{:S(2)}, u32[]{:S(2)}) collective-permute-start(f32[96,128]{1,0:T(8,128)S(1)} %get-tuple-element.15), channel_id=1, source_target_pairs={{0,2},{1,3},{2,0},{3,1},{4,6},{5,7},{6,4},{7,5},{8,10},{9,11},{10,... | collective-permute-start | bytes 147464 | tf_op jit(solution)/shard_map/ppermute | solution.py:362
  11.6 4.5 %collective-permute-start.2 = (f32[96,128]{1,0:T(8,128)S(1)}, f32[96,128]{1,0:T(8,128)S(1)}, u32[]{:S(2)}, u32[]{:S(2)}) collective-permute-start(f32[96,128]{1,0:T(8,128)S(1)} %get-tuple-element.16), channel_id=1, source_target_pairs={{0,1},{1,0},{2,3},{3,2},{4,5},{5,4},{6,7},{7,6},{8,9},{9,8},{10,11... | collective-permute-start | bytes 147464 | tf_op jit(solution)/shard_map/ppermute | solution.py:362
  16.1 6.1 %collective-permute-start.3 = (f32[96,128]{1,0:T(8,128)S(1)}, f32[96,128]{1,0:T(8,128)S(1)}, u32[]{:S(2)}, u32[]{:S(2)}) collective-permute-start(f32[96,128]{1,0:T(8,128)S(1)} %add_add_fusion.1), channel_id=1, source_target_pairs={{0,7},{1,6},{2,5},{3,4},{4,3},{5,2},{6,1},{7,0},{8,15},{9,14},{10,... | collective-permute-start | bytes 147464 | tf_op jit(solution)/shard_map/ppermute | solution.py:362
  22.2 4.8 %collective-permute-start.6 = (f32[96,128]{1,0:T(8,128)S(1)}, f32[96,128]{1,0:T(8,128)S(1)}, u32[]{:S(2)}, u32[]{:S(2)}) collective-permute-start(f32[96,128]{1,0:T(8,128)S(1)} %add.36.sample_ref.s0), channel_id=1, source_target_pairs={{0,3},{1,2},{2,1},{3,0},{4,7},{5,6},{6,5},{7,4},{8,11},{9,10},{10,... | collective-permute-start | bytes 147464 | tf_op jit(solution)/shard_map/ppermute | solution.py:362
  23.9 4.4 %collective-permute-start.5 = (f32[96,128]{1,0:T(8,128)S(1)}, f32[96,128]{1,0:T(8,128)S(1)}, u32[]{:S(2)}, u32[]{:S(2)}) collective-permute-start(f32[96,128]{1,0:T(8,128)S(1)} %add.36.sample_ref.s0), channel_id=1, source_target_pairs={{0,2},{1,3},{2,0},{3,1},{4,6},{5,7},{6,4},{7,5},{8,10},{9,11},{10,... | collective-permute-start | bytes 147464 | tf_op jit(solution)/shard_map/ppermute | solution.py:362
  23.9 5.3 %collective-permute-start.4 = (f32[96,128]{1,0:T(8,128)S(1)}, f32[96,128]{1,0:T(8,128)S(1)}, u32[]{:S(2)}, u32[]{:S(2)}) collective-permute-start(f32[96,128]{1,0:T(8,128)S(1)} %add.36.sample_ref.s0), channel_id=1, source_target_pairs={{0,1},{1,0},{2,3},{3,2},{4,5},{5,4},{6,7},{7,6},{8,9},{9,8},{10,11... | collective-permute-start | bytes 147464 | tf_op jit(solution)/shard_map/ppermute | solution.py:362
  30.1 4.6 %collective-permute-start.7 = (f32[1056,128]{1,0:T(8,128)S(1)}, f32[1056,128]{1,0:T(8,128)S(1)}, u32[]{:S(2)}, u32[]{:S(2)}) collective-permute-start(f32[1056,128]{1,0:T(8,128)S(1)} %shard_map.46.sent_ref), channel_id=1, source_target_pairs={{0,8},{8,0},{16,24},{24,16},{32,40},{40,32},{48,56},{56,48},{64,72... | collective-permute-start | bytes 1622024 | tf_op jit(solution)/shard_map/ppermute | solution.py:366
  34.9 5.9 %collective-permute-start.10 = (f32[288,128]{1,0:T(8,128)S(1)}, f32[288,128]{1,0:T(8,128)S(1)}, u32[]{:S(2)}, u32[]{:S(2)}) collective-permute-start(f32[288,128]{1,0:T(8,128)S(1)} %concatenate.20), channel_id=1, source_target_pairs={{0,128},{8,40},{16,144},{24,56},{32,160},{40,8},{48,176},{56,24},{... | collective-permute-start | bytes 442376 | tf_op jit(solution)/shard_map/ppermute | solution.py:366
  37.9 5.6 %collective-permute-start.8 = (f32[288,128]{1,0:T(8,128)S(1)}, f32[288,128]{1,0:T(8,128)S(1)}, u32[]{:S(2)}, u32[]{:S(2)}) collective-permute-start(f32[288,128]{1,0:T(8,128)S(1)} %get-tuple-element.25), channel_id=1, source_target_pairs={{0,192},{8,56},{16,208},{24,40},{32,224},{40,24},{48,240},{56,8},{... | collective-permute-start | bytes 442376 | tf_op jit(solution)/shard_map/ppermute | solution.py:366
  38.8 4.7 %collective-permute-start.9 = (f32[288,128]{1,0:T(8,128)S(1)}, f32[288,128]{1,0:T(8,128)S(1)}, u32[]{:S(2)}, u32[]{:S(2)}) collective-permute-start(f32[288,128]{1,0:T(8,128)S(1)} %get-tuple-element.26), channel_id=1, source_target_pairs={{0,64},{8,24},{16,80},{24,8},{32,96},{40,56},{48,112},{56,40},{64,... | collective-permute-start | bytes 442376 | tf_op jit(solution)/shard_map/ppermute | solution.py:366
  43.5 5.6 %collective-permute-start.13 = (f32[288,128]{1,0:T(8,128)S(1)}, f32[288,128]{1,0:T(8,128)S(1)}, u32[]{:S(2)}, u32[]{:S(2)}) collective-permute-start(f32[288,128]{1,0:T(8,128)S(1)} %fusion.2), channel_id=1, source_target_pairs={{0,32},{8,136},{16,48},{24,152},{32,0},{40,168},{48,16},{56,184},{... | collective-permute-start | bytes 442376 | tf_op jit(solution)/shard_map/ppermute | solution.py:366
  46.1 5.2 %collective-permute-start.12 = (f32[288,128]{1,0:T(8,128)S(1)}, f32[288,128]{1,0:T(8,128)S(1)}, u32[]{:S(2)}, u32[]{:S(2)}) collective-permute-start(f32[288,128]{1,0:T(8,128)S(1)} %fusion.2), channel_id=1, source_target_pairs={{0,48},{8,200},{16,32},{24,216},{32,16},{40,232},{48,0},{56,248},{... | collective-permute-start | bytes 442376 | tf_op jit(solution)/shard_map/ppermute | solution.py:366
  46.9 4.4 %collective-permute-start.11 = (f32[288,128]{1,0:T(8,128)S(1)}, f32[288,128]{1,0:T(8,128)S(1)}, u32[]{:S(2)}, u32[]{:S(2)}) collective-permute-start(f32[288,128]{1,0:T(8,128)S(1)} %fusion.2), channel_id=1, source_target_pairs={{0,16},{8,72},{16,0},{24,88},{32,48},{40,104},{48,32},{56,120},{64... | collective-permute-start | bytes 442376 | tf_op jit(solution)/shard_map/ppermute | solution.py:366
  51.4 7.4 %collective-permute-start.16 = (f32[256,128]{1,0:T(8,128)S(1)}, f32[256,128]{1,0:T(8,128)S(1)}, u32[]{:S(2)}, u32[]{:S(2)}) collective-permute-start(f32[256,128]{1,0:T(8,128)S(1)} %slice.30), channel_id=1, source_target_pairs={{0,192},{8,56},{16,208},{24,40},{32,224},{40,24},{48,240},{56,8},{... | collective-permute-start | bytes 393224 | tf_op jit(solution)/shard_map/ppermute | solution.py:366
  53.5 5.3 %collective-permute-start.15 = (f32[256,128]{1,0:T(8,128)S(1)}, f32[256,128]{1,0:T(8,128)S(1)}, u32[]{:S(2)}, u32[]{:S(2)}) collective-permute-start(f32[256,128]{1,0:T(8,128)S(1)} %slice.30), channel_id=1, source_target_pairs={{0,128},{8,40},{16,144},{24,56},{32,160},{40,8},{48,176},{56,24},{... | collective-permute-start | bytes 393224 | tf_op jit(solution)/shard_map/ppermute | solution.py:366
  54.0 4.9 %collective-permute-start.14 = (f32[256,128]{1,0:T(8,128)S(1)}, f32[256,128]{1,0:T(8,128)S(1)}, u32[]{:S(2)}, u32[]{:S(2)}) collective-permute-start(f32[256,128]{1,0:T(8,128)S(1)} %slice.30), channel_id=1, source_target_pairs={{0,64},{8,24},{16,80},{24,8},{32,96},{40,56},{48,112},{56,40},{64,... | collective-permute-start | bytes 393224 | tf_op jit(solution)/shard_map/ppermute | solution.py:366
  58.9 6.0 %collective-permute-start.17 = (f32[1024,128]{1,0:T(8,128)S(1)}, f32[1024,128]{1,0:T(8,128)S(1)}, u32[]{:S(2)}, u32[]{:S(2)}) collective-permute-start(f32[1024,128]{1,0:T(8,128)S(1)} %pad_maximum_fusion.value_ref), channel_id=1, source_target_pairs={{0,8},{8,0},{16,24},{24,16},{32,40},{40,32},{48,56},{56,48},{64,72... | collective-permute-start | bytes 1572872 | tf_op jit(solution)/shard_map/ppermute | solution.py:366

commit v8 on v7

--- a/solution.py
+++ b/solution.py
@@ -237,6 +237,11 @@
         ],
         axis=0,
     )
+    lane = lax.broadcasted_iota(jnp.int32, (K, LANES), 1)
+    own = jnp.where(lane == lax.broadcasted_iota(jnp.int32, (K, LANES), 0), work, 0.0)
+    column = 1.0 / jnp.sqrt(jnp.sum(own, axis=1, keepdims=True))
+    line = jnp.where(lane[:1] < K, 1.0 / jnp.sqrt(jnp.sum(own, axis=0, keepdims=True)), 1.0)
+    work = work * column * line
     count = K // 8
     parts = [work[8 * i : 8 * i + 8] for i in range(count)]
     sub = lax.broadcasted_iota(jnp.int32, (8, LANES), 0)

time: 66.1 us -> 66.1 us (level)
  transfers between devices with their start and end apart: 18 -> 18, of which waited for: 11 -> 10; matrix products, arithmetic and copies ran while one was open for 0% -> 0% of each run, Pallas kernels for 17% -> 17%
where the time goes in v8:
time: 66.1 us; the launch traced here: 66 us
  starting transfers between devices  32 us (48%)
  Pallas kernels  18.9 us (29%)
  waiting for transfers between devices  13.9 us (21%)
  between operations  0.95 us (1%)
    ppermute x11, starting transfers between devices, along_row(): lax.ppermute(value, 'row', [(i, i ^ masks[i % 2]) for i in range(32)])  18.1 us
    ppermute x7, starting transfers between devices, along_col(): return lax.ppermute(value, 'col', [(i, i ^ mask) for i in range(8)])  13.9 us
    ppermute x11, waiting for transfers between devices, along_row(): lax.ppermute(value, 'row', [(i, i ^ masks[i % 2]) for i in range(32)])  10.5 us
    pallas_call x1, Pallas kernels, partial_samples(): pl.pallas_call(send_kernel, out_shape=[sample] * len(SENT) + [jax.ShapeDt...  5.71 us
    pallas_call x5, Pallas kernels, term_call(): pl.pallas_call(kernel, out_shape=jax.ShapeDtypeStruct(shape, F32), in_spe...  4.3 us
    ppermute x7, waiting for transfers between devices, along_col(): return lax.ppermute(value, 'col', [(i, i ^ mask) for i in range(8)])  3.45 us
    pallas_call x1, Pallas kernels, inverse_of(): pl.pallas_call(inverse_kernel, out_shape=jax.ShapeDtypeStruct((K, K), F32...  2.81 us
    pallas_call x1, Pallas kernels, partial_samples(): pl.pallas_call(keep_kernel, out_shape=[sample, jax.ShapeDtypeStruct((2 *...  2.72 us
  transfers between devices with their start and end apart: 18, of which 10 were waited for; matrix products, arithmetic and copies ran while one was open for 0% of the time, Pallas kernels for 17%

profile of v8, /device:TPU:1, one launch (start us, length us, event | category | flops | bytes accessed | tf_op | source)
XLA Modules:
  0.0 66.0 jit_solution(10789133500744960613)
XLA Ops:
  0.6 5.7 %shard_map.41 = (f32[96,128]{1,0:T(8,128)S(1)}, f32[96,128]{1,0:T(8,128)S(1)}, f32[96,128]{1,0:T(8,128)S(1)}, bf16[1152,4096]{1,0:T(8,128)(2,1)S(1)}, bf16[4096,128]{1,0:T(8,128)(2,1)S(1)}) custom-call(f32[768,4096]{1,0:T(8,128)} %data_ref.3, f32[64,4096]{1,0:T(8,128)} %bitcast.2), custom_call_target="tpu_custom_call" | custom-call | flops 1207959552 | bytes 9437184 | tf_op jit(solution)/shard_map/pallas_call | solution.py:121
  6.3 5.3 %collective-permute-start = (f32[96,128]{1,0:T(8,128)S(1)}, f32[96,128]{1,0:T(8,128)S(1)}, u32[]{:S(2)}, u32[]{:S(2)}) collective-permute-start(f32[96,128]{1,0:T(8,128)S(1)} %get-tuple-element.14), channel_id=1, source_target_pairs={{0,3},{1,2},{2,1},{3,0},{4,7},{5,6},{6,5},{7,4},{8,11},{9,10},{10,... | collective-permute-start | bytes 147464 | tf_op jit(solution)/shard_map/ppermute | solution.py:367
  11.6 0.0 collective-permute-start.1
  11.6 0.4 collective-permute-start.2
  12.0 2.7 %shard_map.42 = (f32[96,128]{1,0:T(8,128)S(1)}, bf16[384,4096]{1,0:T(8,128)(2,1)S(1)}) custom-call(f32[768,4096]{1,0:T(8,128)} %data_ref.3, bf16[4096,128]{1,0:T(8,128)(2,1)S(1)} %get-tuple-element.12.weights_ref), custom_call_target="tpu_custom_call" | custom-call | flops 402653184 | bytes 3145728 | tf_op jit(solution)/shard_map/pallas_call | solution.py:135
  14.7 0.0 collective-permute-done
  14.7 1.3 %collective-permute-done.1 = f32[96,128]{1,0:T(8,128)S(1)} collective-permute-done((f32[96,128]{1,0:T(8,128)S(1)}, f32[96,128]{1,0:T(8,128)S(1)}, u32[]{:S(2)}, u32[]{:S(2)}) %collective-permute-start.1) | collective-permute-done | bytes 49184 | tf_op jit(solution)/shard_map/ppermute | solution.py:367
  16.1 0.0 collective-permute-done.2
  16.1 4.6 %collective-permute-start.3 = (f32[96,128]{1,0:T(8,128)S(1)}, f32[96,128]{1,0:T(8,128)S(1)}, u32[]{:S(2)}, u32[]{:S(2)}) collective-permute-start(f32[96,128]{1,0:T(8,128)S(1)} %add_add_fusion.1), channel_id=1, source_target_pairs={{0,7},{1,6},{2,5},{3,4},{4,3},{5,2},{6,1},{7,0},{8,15},{9,14},{10,... | collective-permute-start | bytes 147464 | tf_op jit(solution)/shard_map/ppermute | solution.py:367
  20.7 1.5 %collective-permute-done.3 = f32[96,128]{1,0:T(8,128)S(1)} collective-permute-done((f32[96,128]{1,0:T(8,128)S(1)}, f32[96,128]{1,0:T(8,128)S(1)}, u32[]{:S(2)}, u32[]{:S(2)}) %collective-permute-start.3) | collective-permute-done | bytes 49184 | tf_op jit(solution)/shard_map/ppermute | solution.py:367
  22.2 1.7 %collective-permute-start.6 = (f32[96,128]{1,0:T(8,128)S(1)}, f32[96,128]{1,0:T(8,128)S(1)}, u32[]{:S(2)}, u32[]{:S(2)}) collective-permute-start(f32[96,128]{1,0:T(8,128)S(1)} %add.36.sample_ref.s0), channel_id=1, source_target_pairs={{0,3},{1,2},{2,1},{3,0},{4,7},{5,6},{6,5},{7,4},{8,11},{9,10},{10,... | collective-permute-start | bytes 147464 | tf_op jit(solution)/shard_map/ppermute | solution.py:367
  23.9 0.0 collective-permute-start.5
  23.9 1.9 %collective-permute-start.4 = (f32[96,128]{1,0:T(8,128)S(1)}, f32[96,128]{1,0:T(8,128)S(1)}, u32[]{:S(2)}, u32[]{:S(2)}) collective-permute-start(f32[96,128]{1,0:T(8,128)S(1)} %add.36.sample_ref.s0), channel_id=1, source_target_pairs={{0,1},{1,0},{2,3},{3,2},{4,5},{5,4},{6,7},{7,6},{8,9},{9,8},{10,11... | collective-permute-start | bytes 147464 | tf_op jit(solution)/shard_map/ppermute | solution.py:367
  25.8 0.9 %shard_map.43.begun_ref = f32[64,4096]{1,0:T(8,128)S(1)} custom-call(f32[96,128]{1,0:T(8,128)S(1)} %add.36.sample_ref.s0, bf16[384,4096]{1,0:T(8,128)(2,1)S(1)} %get-tuple-element.18.terms_ref), custom_call_target="tpu_custom_call" | custom-call | flops 402653184 | bytes 3145728 | tf_op jit(solution)/shard_map/pallas_call | solution.py:203
  26.8 0.3 collective-permute-done.6.sample_ref.s3
  27.0 0.9 %shard_map.44.begun_ref = f32[64,4096]{1,0:T(8,128)S(1)} custom-call(f32[96,128]{1,0:T(8,128)S(1)} %collective-permute-done.6.sample_ref.s3, bf16[1152,4096]{1,0:T(8,128)(2,1)S(1)} %get-tuple-element.17.terms_ref, f32[64,4096]{1,0:T(8,128)S(1)} %shard_map.43.begun_ref), custom_call_target="tpu_custom_call" | custom-call | flops 402653184 | bytes 3145728 | tf_op jit(solution)/shard_map/pallas_call | solution.py:203
  28.0 0.3 collective-permute-done.5.sample_ref.s2
  28.3 0.9 %shard_map.45.begun_ref = f32[64,4096]{1,0:T(8,128)S(1)} custom-call(f32[96,128]{1,0:T(8,128)S(1)} %collective-permute-done.5.sample_ref.s2, bf16[1152,4096]{1,0:T(8,128)(2,1)S(1)} %get-tuple-element.17.terms_ref, f32[64,4096]{1,0:T(8,128)S(1)} %shard_map.44.begun_ref), custom_call_target="tpu_custom_call" | custom-call | flops 402653184 | bytes 3145728 | tf_op jit(solution)/shard_map/pallas_call | solution.py:203
  29.2 0.0 collective-permute-done.4.s1.sample_ref
  29.2 0.9 %shard_map.46.sent_ref = f32[1056,128]{1,0:T(8,128)S(1)} custom-call(f32[96,128]{1,0:T(8,128)S(1)} %add.36.sample_ref.s0, f32[96,128]{1,0:T(8,128)S(1)} %collective-permute-done.6.sample_ref.s3, f32[96,128]{1,0:T(8,128)S(1)} %collective-permute-done.5.sample_ref.s2, f32[96,128]{1,0:T(8,128)S(1)} %collective-permute-done.4.s1.sample_ref, ...), custom_call_target="tpu_custom_call" | custom-call | flops 201326592 | bytes 1572864 | tf_op jit(solution)/shard_map/pallas_call | solution.py:203
  30.1 3.1 %collective-permute-start.7 = (f32[1056,128]{1,0:T(8,128)S(1)}, f32[1056,128]{1,0:T(8,128)S(1)}, u32[]{:S(2)}, u32[]{:S(2)}) collective-permute-start(f32[1056,128]{1,0:T(8,128)S(1)} %shard_map.46.sent_ref), channel_id=1, source_target_pairs={{0,8},{8,0},{16,24},{24,16},{32,40},{40,32},{48,56},{56,48},{64,72... | collective-permute-start | bytes 1622024 | tf_op jit(solution)/shard_map/ppermute | solution.py:371
  33.2 0.7 %shard_map.47 = f32[1056,128]{1,0:T(8,128)S(1)} custom-call(f32[96,128]{1,0:T(8,128)S(1)} %collective-permute-done.4.s1.sample_ref, bf16[1152,4096]{1,0:T(8,128)(2,1)S(1)} %get-tuple-element.17.terms_ref, f32[64,4096]{1,0:T(8,128)S(1)} %shard_map.45.begun_ref, f32[1056,128]{1,0:T(8,128)S(1)} %shard_map.46.sent_ref), custom_call_target="tpu_custom_call" | custom-call | flops 201326592 | bytes 1572864 | tf_op jit(solution)/shard_map/pallas_call | solution.py:203
  33.9 0.9 %collective-permute-done.7 = f32[1056,128]{1,0:T(8,128)S(1)} collective-permute-done((f32[1056,128]{1,0:T(8,128)S(1)}, f32[1056,128]{1,0:T(8,128)S(1)}, u32[]{:S(2)}, u32[]{:S(2)}) %collective-permute-start.7) | collective-permute-done | bytes 540704 | tf_op jit(solution)/shard_map/ppermute | solution.py:371
  34.8 0.1 add.37
  34.9 3.0 %collective-permute-start.10 = (f32[288,128]{1,0:T(8,128)S(1)}, f32[288,128]{1,0:T(8,128)S(1)}, u32[]{:S(2)}, u32[]{:S(2)}) collective-permute-start(f32[288,128]{1,0:T(8,128)S(1)} %concatenate.20), channel_id=1, source_target_pairs={{0,128},{8,40},{16,144},{24,56},{32,160},{40,8},{48,176},{56,24},{... | collective-permute-start | bytes 442376 | tf_op jit(solution)/shard_map/ppermute | solution.py:371
  37.9 0.9 %collective-permute-start.8 = (f32[288,128]{1,0:T(8,128)S(1)}, f32[288,128]{1,0:T(8,128)S(1)}, u32[]{:S(2)}, u32[]{:S(2)}) collective-permute-start(f32[288,128]{1,0:T(8,128)S(1)} %get-tuple-element.25), channel_id=1, source_target_pairs={{0,192},{8,56},{16,208},{24,40},{32,224},{40,24},{48,240},{56,8},{... | collective-permute-start | bytes 442376 | tf_op jit(solution)/shard_map/ppermute | solution.py:371
  38.8 0.0 collective-permute-start.9
  38.8 2.0 %collective-permute-done.10 = f32[288,128]{1,0:T(8,128)S(1)} collective-permute-done((f32[288,128]{1,0:T(8,128)S(1)}, f32[288,128]{1,0:T(8,128)S(1)}, u32[]{:S(2)}, u32[]{:S(2)}) %collective-permute-start.10) | collective-permute-done | bytes 147488 | tf_op jit(solution)/shard_map/ppermute | solution.py:371
  40.8 2.7 %collective-permute-done.8 = f32[288,128]{1,0:T(8,128)S(1)} collective-permute-done((f32[288,128]{1,0:T(8,128)S(1)}, f32[288,128]{1,0:T(8,128)S(1)}, u32[]{:S(2)}, u32[]{:S(2)}) %collective-permute-start.8) | collective-permute-done | bytes 147488 | tf_op jit(solution)/shard_map/ppermute | solution.py:371
  43.5 0.0 collective-permute-done.9
  43.5 2.5 %collective-permute-start.13 = (f32[288,128]{1,0:T(8,128)S(1)}, f32[288,128]{1,0:T(8,128)S(1)}, u32[]{:S(2)}, u32[]{:S(2)}) collective-permute-start(f32[288,128]{1,0:T(8,128)S(1)} %fusion.2), channel_id=1, source_target_pairs={{0,32},{8,136},{16,48},{24,152},{32,0},{40,168},{48,16},{56,184},{... | collective-permute-start | bytes 442376 | tf_op jit(solution)/shard_map/ppermute | solution.py:371
  46.1 0.8 %collective-permute-start.12 = (f32[288,128]{1,0:T(8,128)S(1)}, f32[288,128]{1,0:T(8,128)S(1)}, u32[]{:S(2)}, u32[]{:S(2)}) collective-permute-start(f32[288,128]{1,0:T(8,128)S(1)} %fusion.2), channel_id=1, source_target_pairs={{0,48},{8,200},{16,32},{24,216},{32,16},{40,232},{48,0},{56,248},{... | collective-permute-start | bytes 442376 | tf_op jit(solution)/shard_map/ppermute | solution.py:371
  46.9 0.0 collective-permute-start.11
  46.9 2.2 %collective-permute-done.13 = f32[288,128]{1,0:T(8,128)S(1)} collective-permute-done((f32[288,128]{1,0:T(8,128)S(1)}, f32[288,128]{1,0:T(8,128)S(1)}, u32[]{:S(2)}, u32[]{:S(2)}) %collective-permute-start.13) | collective-permute-done | bytes 147488 | tf_op jit(solution)/shard_map/ppermute | solution.py:371
  49.1 2.2 %collective-permute-done.12 = f32[288,128]{1,0:T(8,128)S(1)} collective-permute-done((f32[288,128]{1,0:T(8,128)S(1)}, f32[288,128]{1,0:T(8,128)S(1)}, u32[]{:S(2)}, u32[]{:S(2)}) %collective-permute-start.12) | collective-permute-done | bytes 147488 | tf_op jit(solution)/shard_map/ppermute | solution.py:371
  51.3 0.0 collective-permute-done.11
  51.4 2.1 %collective-permute-start.16 = (f32[256,128]{1,0:T(8,128)S(1)}, f32[256,128]{1,0:T(8,128)S(1)}, u32[]{:S(2)}, u32[]{:S(2)}) collective-permute-start(f32[256,128]{1,0:T(8,128)S(1)} %slice.30), channel_id=1, source_target_pairs={{0,192},{8,56},{16,208},{24,40},{32,224},{40,24},{48,240},{56,8},{... | collective-permute-start | bytes 393224 | tf_op jit(solution)/shard_map/ppermute | solution.py:371
  53.5 0.5 collective-permute-start.15
  54.0 0.7 %collective-permute-start.14 = (f32[256,128]{1,0:T(8,128)S(1)}, f32[256,128]{1,0:T(8,128)S(1)}, u32[]{:S(2)}, u32[]{:S(2)}) collective-permute-start(f32[256,128]{1,0:T(8,128)S(1)} %slice.30), channel_id=1, source_target_pairs={{0,64},{8,24},{16,80},{24,8},{32,96},{40,56},{48,112},{56,40},{64,... | collective-permute-start | bytes 393224 | tf_op jit(solution)/shard_map/ppermute | solution.py:371
  54.7 2.8 %shard_map.48.inverse_ref = f32[64,64]{1,0:T(8,128)S(1)} custom-call(f32[32,128]{1,0:T(8,128)S(1)} %slice.31.gram_ref), custom_call_target="tpu_custom_call" | custom-call | flops 26214400 | bytes 32768 | tf_op jit(solution)/shard_map/pallas_call | solution.py:295
  57.5 1.3 %shard_map.49 = f32[64,768]{1,0:T(8,128)} custom-call(f32[64,64]{1,0:T(8,128)S(1)} %shard_map.48.inverse_ref, f32[96,128]{1,0:T(8,128)S(1)} %add.36.sample_ref.s0, f32[96,128]{1,0:T(8,128)S(1)} %collective-permute-done.6.sample_ref.s3, f32[96,128]{1,0:T(8,128)S(1)} %collective-permute-done.5.sample_ref.s2, f32[96,128]{1,0:T(8,128)S(1)} %collective-permute-done.4.s1.sample_ref), custom_call_target="tpu_custom_call" | custom-call | flops 37748736 | bytes 393216 | tf_op jit(solution)/shard_map/pallas_call | solution.py:322
  58.8 0.0 collective-permute-done.16
  58.9 0.0 collective-permute-done.15
  58.9 0.0 collective-permute-done.14
  58.9 4.4 %collective-permute-start.17 = (f32[1024,128]{1,0:T(8,128)S(1)}, f32[1024,128]{1,0:T(8,128)S(1)}, u32[]{:S(2)}, u32[]{:S(2)}) collective-permute-start(f32[1024,128]{1,0:T(8,128)S(1)} %pad_maximum_fusion.value_ref), channel_id=1, source_target_pairs={{0,8},{8,0},{16,24},{24,16},{32,40},{40,32},{48,56},{56,48},{64,72... | collective-permute-start | bytes 1572872 | tf_op jit(solution)/shard_map/ppermute | solution.py:371
  63.3 1.0 %shard_map.50.refs_0_ = f32[64,4096]{1,0:T(8,128)} custom-call(f32[64,64]{1,0:T(8,128)S(1)} %shard_map.48.inverse_ref, f32[1024,128]{1,0:T(8,128)S(1)} %pad_maximum_fusion.value_ref), custom_call_target="tpu_custom_call" | custom-call | flops 50331648 | bytes 1048576 | tf_op jit(solution)/shard_map/pallas_call | solution.py:354
  64.3 0.5 collective-permute-done.17.value_ref
  64.8 1.0 %shard_map.51 = f32[64,4096]{1,0:T(8,128)} custom-call(f32[64,64]{1,0:T(8,128)S(1)} %shard_map.48.inverse_ref, f32[1024,128]{1,0:T(8,128)S(1)} %collective-permute-done.17.value_ref, f32[64,4096]{1,0:T(8,128)} %shard_map.50.refs_0_), custom_call_target="tpu_custom_call", output_to_operand_aliasing={{}: (2, {})} | custom-call | flops 50331648 | bytes 1048576 | tf_op jit(solution)/shard_map/pallas_call | solution.py:354
  (11 shorter events, 0.2 us)
Async XLA Ops:
  6.3 8.4 %collective-permute-start = (f32[96,128]{1,0:T(8,128)S(1)}, f32[96,128]{1,0:T(8,128)S(1)}, u32[]{:S(2)}, u32[]{:S(2)}) collective-permute-start(f32[96,128]{1,0:T(8,128)S(1)} %get-tuple-element.14), channel_id=1, source_target_pairs={{0,3},{1,2},{2,1},{3,0},{4,7},{5,6},{6,5},{7,4},{8,11},{9,10},{10,... | collective-permute-start | bytes 147464 | tf_op jit(solution)/shard_map/ppermute | solution.py:367
  11.6 4.5 %collective-permute-start.1 = (f32[96,128]{1,0:T(8,128)S(1)}, f32[96,128]{1,0:T(8,128)S(1)}, u32[]{:S(2)}, u32[]{:S(2)}) collective-permute-start(f32[96,128]{1,0:T(8,128)S(1)} %get-tuple-element.15), channel_id=1, source_target_pairs={{0,2},{1,3},{2,0},{3,1},{4,6},{5,7},{6,4},{7,5},{8,10},{9,11},{10,... | collective-permute-start | bytes 147464 | tf_op jit(solution)/shard_map/ppermute | solution.py:367
  11.6 4.5 %collective-permute-start.2 = (f32[96,128]{1,0:T(8,128)S(1)}, f32[96,128]{1,0:T(8,128)S(1)}, u32[]{:S(2)}, u32[]{:S(2)}) collective-permute-start(f32[96,128]{1,0:T(8,128)S(1)} %get-tuple-element.16), channel_id=1, source_target_pairs={{0,1},{1,0},{2,3},{3,2},{4,5},{5,4},{6,7},{7,6},{8,9},{9,8},{10,11... | collective-permute-start | bytes 147464 | tf_op jit(solution)/shard_map/ppermute | solution.py:367
  16.1 6.1 %collective-permute-start.3 = (f32[96,128]{1,0:T(8,128)S(1)}, f32[96,128]{1,0:T(8,128)S(1)}, u32[]{:S(2)}, u32[]{:S(2)}) collective-permute-start(f32[96,128]{1,0:T(8,128)S(1)} %add_add_fusion.1), channel_id=1, source_target_pairs={{0,7},{1,6},{2,5},{3,4},{4,3},{5,2},{6,1},{7,0},{8,15},{9,14},{10,... | collective-permute-start | bytes 147464 | tf_op jit(solution)/shard_map/ppermute | solution.py:367
  22.2 4.8 %collective-permute-start.6 = (f32[96,128]{1,0:T(8,128)S(1)}, f32[96,128]{1,0:T(8,128)S(1)}, u32[]{:S(2)}, u32[]{:S(2)}) collective-permute-start(f32[96,128]{1,0:T(8,128)S(1)} %add.36.sample_ref.s0), channel_id=1, source_target_pairs={{0,3},{1,2},{2,1},{3,0},{4,7},{5,6},{6,5},{7,4},{8,11},{9,10},{10,... | collective-permute-start | bytes 147464 | tf_op jit(solution)/shard_map/ppermute | solution.py:367
  23.9 4.4 %collective-permute-start.5 = (f32[96,128]{1,0:T(8,128)S(1)}, f32[96,128]{1,0:T(8,128)S(1)}, u32[]{:S(2)}, u32[]{:S(2)}) collective-permute-start(f32[96,128]{1,0:T(8,128)S(1)} %add.36.sample_ref.s0), channel_id=1, source_target_pairs={{0,2},{1,3},{2,0},{3,1},{4,6},{5,7},{6,4},{7,5},{8,10},{9,11},{10,... | collective-permute-start | bytes 147464 | tf_op jit(solution)/shard_map/ppermute | solution.py:367
  23.9 5.3 %collective-permute-start.4 = (f32[96,128]{1,0:T(8,128)S(1)}, f32[96,128]{1,0:T(8,128)S(1)}, u32[]{:S(2)}, u32[]{:S(2)}) collective-permute-start(f32[96,128]{1,0:T(8,128)S(1)} %add.36.sample_ref.s0), channel_id=1, source_target_pairs={{0,1},{1,0},{2,3},{3,2},{4,5},{5,4},{6,7},{7,6},{8,9},{9,8},{10,11... | collective-permute-start | bytes 147464 | tf_op jit(solution)/shard_map/ppermute | solution.py:367
  30.1 4.6 %collective-permute-start.7 = (f32[1056,128]{1,0:T(8,128)S(1)}, f32[1056,128]{1,0:T(8,128)S(1)}, u32[]{:S(2)}, u32[]{:S(2)}) collective-permute-start(f32[1056,128]{1,0:T(8,128)S(1)} %shard_map.46.sent_ref), channel_id=1, source_target_pairs={{0,8},{8,0},{16,24},{24,16},{32,40},{40,32},{48,56},{56,48},{64,72... | collective-permute-start | bytes 1622024 | tf_op jit(solution)/shard_map/ppermute | solution.py:371
  34.9 5.9 %collective-permute-start.10 = (f32[288,128]{1,0:T(8,128)S(1)}, f32[288,128]{1,0:T(8,128)S(1)}, u32[]{:S(2)}, u32[]{:S(2)}) collective-permute-start(f32[288,128]{1,0:T(8,128)S(1)} %concatenate.20), channel_id=1, source_target_pairs={{0,128},{8,40},{16,144},{24,56},{32,160},{40,8},{48,176},{56,24},{... | collective-permute-start | bytes 442376 | tf_op jit(solution)/shard_map/ppermute | solution.py:371
  37.9 5.6 %collective-permute-start.8 = (f32[288,128]{1,0:T(8,128)S(1)}, f32[288,128]{1,0:T(8,128)S(1)}, u32[]{:S(2)}, u32[]{:S(2)}) collective-permute-start(f32[288,128]{1,0:T(8,128)S(1)} %get-tuple-element.25), channel_id=1, source_target_pairs={{0,192},{8,56},{16,208},{24,40},{32,224},{40,24},{48,240},{56,8},{... | collective-permute-start | bytes 442376 | tf_op jit(solution)/shard_map/ppermute | solution.py:371
  38.8 4.7 %collective-permute-start.9 = (f32[288,128]{1,0:T(8,128)S(1)}, f32[288,128]{1,0:T(8,128)S(1)}, u32[]{:S(2)}, u32[]{:S(2)}) collective-permute-start(f32[288,128]{1,0:T(8,128)S(1)} %get-tuple-element.26), channel_id=1, source_target_pairs={{0,64},{8,24},{16,80},{24,8},{32,96},{40,56},{48,112},{56,40},{64,... | collective-permute-start | bytes 442376 | tf_op jit(solution)/shard_map/ppermute | solution.py:371
  43.5 5.6 %collective-permute-start.13 = (f32[288,128]{1,0:T(8,128)S(1)}, f32[288,128]{1,0:T(8,128)S(1)}, u32[]{:S(2)}, u32[]{:S(2)}) collective-permute-start(f32[288,128]{1,0:T(8,128)S(1)} %fusion.2), channel_id=1, source_target_pairs={{0,32},{8,136},{16,48},{24,152},{32,0},{40,168},{48,16},{56,184},{... | collective-permute-start | bytes 442376 | tf_op jit(solution)/shard_map/ppermute | solution.py:371
  46.1 5.2 %collective-permute-start.12 = (f32[288,128]{1,0:T(8,128)S(1)}, f32[288,128]{1,0:T(8,128)S(1)}, u32[]{:S(2)}, u32[]{:S(2)}) collective-permute-start(f32[288,128]{1,0:T(8,128)S(1)} %fusion.2), channel_id=1, source_target_pairs={{0,48},{8,200},{16,32},{24,216},{32,16},{40,232},{48,0},{56,248},{... | collective-permute-start | bytes 442376 | tf_op jit(solution)/shard_map/ppermute | solution.py:371
  46.9 4.4 %collective-permute-start.11 = (f32[288,128]{1,0:T(8,128)S(1)}, f32[288,128]{1,0:T(8,128)S(1)}, u32[]{:S(2)}, u32[]{:S(2)}) collective-permute-start(f32[288,128]{1,0:T(8,128)S(1)} %fusion.2), channel_id=1, source_target_pairs={{0,16},{8,72},{16,0},{24,88},{32,48},{40,104},{48,32},{56,120},{64... | collective-permute-start | bytes 442376 | tf_op jit(solution)/shard_map/ppermute | solution.py:371
  51.4 7.5 %collective-permute-start.16 = (f32[256,128]{1,0:T(8,128)S(1)}, f32[256,128]{1,0:T(8,128)S(1)}, u32[]{:S(2)}, u32[]{:S(2)}) collective-permute-start(f32[256,128]{1,0:T(8,128)S(1)} %slice.30), channel_id=1, source_target_pairs={{0,192},{8,56},{16,208},{24,40},{32,224},{40,24},{48,240},{56,8},{... | collective-permute-start | bytes 393224 | tf_op jit(solution)/shard_map/ppermute | solution.py:371
  53.5 5.4 %collective-permute-start.15 = (f32[256,128]{1,0:T(8,128)S(1)}, f32[256,128]{1,0:T(8,128)S(1)}, u32[]{:S(2)}, u32[]{:S(2)}) collective-permute-start(f32[256,128]{1,0:T(8,128)S(1)} %slice.30), channel_id=1, source_target_pairs={{0,128},{8,40},{16,144},{24,56},{32,160},{40,8},{48,176},{56,24},{... | collective-permute-start | bytes 393224 | tf_op jit(solution)/shard_map/ppermute | solution.py:371
  54.0 4.9 %collective-permute-start.14 = (f32[256,128]{1,0:T(8,128)S(1)}, f32[256,128]{1,0:T(8,128)S(1)}, u32[]{:S(2)}, u32[]{:S(2)}) collective-permute-start(f32[256,128]{1,0:T(8,128)S(1)} %slice.30), channel_id=1, source_target_pairs={{0,64},{8,24},{16,80},{24,8},{32,96},{40,56},{48,112},{56,40},{64,... | collective-permute-start | bytes 393224 | tf_op jit(solution)/shard_map/ppermute | solution.py:371
  58.9 5.9 %collective-permute-start.17 = (f32[1024,128]{1,0:T(8,128)S(1)}, f32[1024,128]{1,0:T(8,128)S(1)}, u32[]{:S(2)}, u32[]{:S(2)}) collective-permute-start(f32[1024,128]{1,0:T(8,128)S(1)} %pad_maximum_fusion.value_ref), channel_id=1, source_target_pairs={{0,8},{8,0},{16,24},{24,16},{32,40},{40,32},{48,56},{56,48},{64,72... | collective-permute-start | bytes 1572872 | tf_op jit(solution)/shard_map/ppermute | solution.py:371

commit v9 on v8

--- a/solution.py
+++ b/solution.py
@@ -181,12 +181,15 @@
 
 
 def sent_half_kernel(index, s0, s3, s2, s1, terms_ref, begun_ref, out_ref):
-    every = jnp.concatenate([left_of(ref[...])[0] for ref in (s0, s3, s2, s1)], axis=1)
-    gram = lax.dot_general(every, every, (((1,), (1,)), ((), ())), preferred_element_type=F32)
-    gram = gram[:K] + gram[K:]
-    gram = gram + pltpu.roll(gram, K, axis=1)
+    every = jnp.concatenate([ref[...] for ref in (s0, s3, s2, s1)], axis=0).T
+    both = jnp.concatenate(split(every), axis=0)
+    gram = lax.dot_general(both, both, (((1,), (1,)), ((), ())), preferred_element_type=F32)
+    gram = gram[:LANES] + gram[LANES:]
+    gram = gram[:, :LANES] + gram[:, LANES:]
+    gram = gram[:K] + pltpu.roll(gram[K:], K, axis=1)
     lane = lax.broadcasted_iota(jnp.int32, (K // 2, LANES), 1)
-    out_ref[BLOCKS // 2 * K :, :] = jnp.where(lane < K, gram[: K // 2], gram[K // 2 :])
+    turned = pltpu.roll(gram[K // 2 :], K, axis=1)
+    out_ref[BLOCKS // 2 * K :, :] = jnp.where(lane < K, gram[: K // 2], turned)
     half_blocks(PER_GROUP, index, (s3, s2, s1)[index], terms_ref, begun_ref, out_ref)
 
 

time: 66.1 us -> 66 us (level)
  no operation moved by 1% of the time
where the time goes in v9:
time: 66 us; the launch traced here: 65.9 us
  starting transfers between devices  32 us (48%)
  Pallas kernels  18.8 us (28%)
  waiting for transfers between devices  13.9 us (21%)
  between operations  0.95 us (1%)
    ppermute x11, starting transfers between devices, along_row(): lax.ppermute(value, 'row', [(i, i ^ masks[i % 2]) for i in range(32)])  18.1 us
    ppermute x7, starting transfers between devices, along_col(): return lax.ppermute(value, 'col', [(i, i ^ mask) for i in range(8)])  13.9 us
    ppermute x11, waiting for transfers between devices, along_row(): lax.ppermute(value, 'row', [(i, i ^ masks[i % 2]) for i in range(32)])  10.5 us
    pallas_call x1, Pallas kernels, partial_samples(): pl.pallas_call(send_kernel, out_shape=[sample] * len(SENT) + [jax.ShapeDt...  5.71 us
    pallas_call x5, Pallas kernels, term_call(): pl.pallas_call(kernel, out_shape=jax.ShapeDtypeStruct(shape, F32), in_spe...  4.19 us
    ppermute x7, waiting for transfers between devices, along_col(): return lax.ppermute(value, 'col', [(i, i ^ mask) for i in range(8)])  3.45 us
    pallas_call x1, Pallas kernels, inverse_of(): pl.pallas_call(inverse_kernel, out_shape=jax.ShapeDtypeStruct((K, K), F32...  2.81 us
    pallas_call x1, Pallas kernels, partial_samples(): pl.pallas_call(keep_kernel, out_shape=[sample, jax.ShapeDtypeStruct((2 *...  2.72 us
  transfers between devices with their start and end apart: 18, of which 10 were waited for; matrix products, arithmetic and copies ran while one was open for 0% of the time, Pallas kernels for 17%

profile of v9, /device:TPU:1, one launch (start us, length us, event | category | flops | bytes accessed | tf_op | source)
XLA Modules:
  0.0 65.9 jit_solution(16104280442247604474)
XLA Ops:
  0.6 5.7 %shard_map.41 = (f32[96,128]{1,0:T(8,128)S(1)}, f32[96,128]{1,0:T(8,128)S(1)}, f32[96,128]{1,0:T(8,128)S(1)}, bf16[1152,4096]{1,0:T(8,128)(2,1)S(1)}, bf16[4096,128]{1,0:T(8,128)(2,1)S(1)}) custom-call(f32[768,4096]{1,0:T(8,128)} %data_ref.3, f32[64,4096]{1,0:T(8,128)} %bitcast.2), custom_call_target="tpu_custom_call" | custom-call | flops 1207959552 | bytes 9437184 | tf_op jit(solution)/shard_map/pallas_call | solution.py:121
  6.3 5.3 %collective-permute-start = (f32[96,128]{1,0:T(8,128)S(1)}, f32[96,128]{1,0:T(8,128)S(1)}, u32[]{:S(2)}, u32[]{:S(2)}) collective-permute-start(f32[96,128]{1,0:T(8,128)S(1)} %get-tuple-element.14), channel_id=1, source_target_pairs={{0,3},{1,2},{2,1},{3,0},{4,7},{5,6},{6,5},{7,4},{8,11},{9,10},{10,... | collective-permute-start | bytes 147464 | tf_op jit(solution)/shard_map/ppermute | solution.py:370
  11.6 0.0 collective-permute-start.1
  11.6 0.4 collective-permute-start.2
  12.0 2.7 %shard_map.42 = (f32[96,128]{1,0:T(8,128)S(1)}, bf16[384,4096]{1,0:T(8,128)(2,1)S(1)}) custom-call(f32[768,4096]{1,0:T(8,128)} %data_ref.3, bf16[4096,128]{1,0:T(8,128)(2,1)S(1)} %get-tuple-element.12.weights_ref), custom_call_target="tpu_custom_call" | custom-call | flops 402653184 | bytes 3145728 | tf_op jit(solution)/shard_map/pallas_call | solution.py:135
  14.7 0.0 collective-permute-done
  14.7 1.3 %collective-permute-done.1 = f32[96,128]{1,0:T(8,128)S(1)} collective-permute-done((f32[96,128]{1,0:T(8,128)S(1)}, f32[96,128]{1,0:T(8,128)S(1)}, u32[]{:S(2)}, u32[]{:S(2)}) %collective-permute-start.1) | collective-permute-done | bytes 49184 | tf_op jit(solution)/shard_map/ppermute | solution.py:370
  16.1 0.0 collective-permute-done.2
  16.1 4.6 %collective-permute-start.3 = (f32[96,128]{1,0:T(8,128)S(1)}, f32[96,128]{1,0:T(8,128)S(1)}, u32[]{:S(2)}, u32[]{:S(2)}) collective-permute-start(f32[96,128]{1,0:T(8,128)S(1)} %add_add_fusion.1), channel_id=1, source_target_pairs={{0,7},{1,6},{2,5},{3,4},{4,3},{5,2},{6,1},{7,0},{8,15},{9,14},{10,... | collective-permute-start | bytes 147464 | tf_op jit(solution)/shard_map/ppermute | solution.py:370
  20.7 1.5 %collective-permute-done.3 = f32[96,128]{1,0:T(8,128)S(1)} collective-permute-done((f32[96,128]{1,0:T(8,128)S(1)}, f32[96,128]{1,0:T(8,128)S(1)}, u32[]{:S(2)}, u32[]{:S(2)}) %collective-permute-start.3) | collective-permute-done | bytes 49184 | tf_op jit(solution)/shard_map/ppermute | solution.py:370
  22.2 1.7 %collective-permute-start.6 = (f32[96,128]{1,0:T(8,128)S(1)}, f32[96,128]{1,0:T(8,128)S(1)}, u32[]{:S(2)}, u32[]{:S(2)}) collective-permute-start(f32[96,128]{1,0:T(8,128)S(1)} %add.36.sample_ref.s0), channel_id=1, source_target_pairs={{0,3},{1,2},{2,1},{3,0},{4,7},{5,6},{6,5},{7,4},{8,11},{9,10},{10,... | collective-permute-start | bytes 147464 | tf_op jit(solution)/shard_map/ppermute | solution.py:370
  23.9 0.0 collective-permute-start.5
  23.9 1.9 %collective-permute-start.4 = (f32[96,128]{1,0:T(8,128)S(1)}, f32[96,128]{1,0:T(8,128)S(1)}, u32[]{:S(2)}, u32[]{:S(2)}) collective-permute-start(f32[96,128]{1,0:T(8,128)S(1)} %add.36.sample_ref.s0), channel_id=1, source_target_pairs={{0,1},{1,0},{2,3},{3,2},{4,5},{5,4},{6,7},{7,6},{8,9},{9,8},{10,11... | collective-permute-start | bytes 147464 | tf_op jit(solution)/shard_map/ppermute | solution.py:370
  25.8 0.9 %shard_map.43.begun_ref = f32[64,4096]{1,0:T(8,128)S(1)} custom-call(f32[96,128]{1,0:T(8,128)S(1)} %add.36.sample_ref.s0, bf16[384,4096]{1,0:T(8,128)(2,1)S(1)} %get-tuple-element.18.terms_ref), custom_call_target="tpu_custom_call" | custom-call | flops 402653184 | bytes 3145728 | tf_op jit(solution)/shard_map/pallas_call | solution.py:206
  26.8 0.3 collective-permute-done.6.sample_ref.s3
  27.0 0.9 %shard_map.44.begun_ref = f32[64,4096]{1,0:T(8,128)S(1)} custom-call(f32[96,128]{1,0:T(8,128)S(1)} %collective-permute-done.6.sample_ref.s3, bf16[1152,4096]{1,0:T(8,128)(2,1)S(1)} %get-tuple-element.17.terms_ref, f32[64,4096]{1,0:T(8,128)S(1)} %shard_map.43.begun_ref), custom_call_target="tpu_custom_call" | custom-call | flops 402653184 | bytes 3145728 | tf_op jit(solution)/shard_map/pallas_call | solution.py:206
  28.0 0.3 collective-permute-done.5.sample_ref.s2
  28.3 0.9 %shard_map.45.begun_ref = f32[64,4096]{1,0:T(8,128)S(1)} custom-call(f32[96,128]{1,0:T(8,128)S(1)} %collective-permute-done.5.sample_ref.s2, bf16[1152,4096]{1,0:T(8,128)(2,1)S(1)} %get-tuple-element.17.terms_ref, f32[64,4096]{1,0:T(8,128)S(1)} %shard_map.44.begun_ref), custom_call_target="tpu_custom_call" | custom-call | flops 402653184 | bytes 3145728 | tf_op jit(solution)/shard_map/pallas_call | solution.py:206
  29.2 0.0 collective-permute-done.4.s1.sample_ref
  29.2 0.8 %shard_map.46.sent_ref = f32[1056,128]{1,0:T(8,128)S(1)} custom-call(f32[96,128]{1,0:T(8,128)S(1)} %add.36.sample_ref.s0, f32[96,128]{1,0:T(8,128)S(1)} %collective-permute-done.6.sample_ref.s3, f32[96,128]{1,0:T(8,128)S(1)} %collective-permute-done.5.sample_ref.s2, f32[96,128]{1,0:T(8,128)S(1)} %collective-permute-done.4.s1.sample_ref, ...), custom_call_target="tpu_custom_call" | custom-call | flops 201326592 | bytes 1572864 | tf_op jit(solution)/shard_map/pallas_call | solution.py:206
  30.0 3.1 %collective-permute-start.7 = (f32[1056,128]{1,0:T(8,128)S(1)}, f32[1056,128]{1,0:T(8,128)S(1)}, u32[]{:S(2)}, u32[]{:S(2)}) collective-permute-start(f32[1056,128]{1,0:T(8,128)S(1)} %shard_map.46.sent_ref), channel_id=1, source_target_pairs={{0,8},{8,0},{16,24},{24,16},{32,40},{40,32},{48,56},{56,48},{64,72... | collective-permute-start | bytes 1622024 | tf_op jit(solution)/shard_map/ppermute | solution.py:374
  33.1 0.7 %shard_map.47 = f32[1056,128]{1,0:T(8,128)S(1)} custom-call(f32[96,128]{1,0:T(8,128)S(1)} %collective-permute-done.4.s1.sample_ref, bf16[1152,4096]{1,0:T(8,128)(2,1)S(1)} %get-tuple-element.17.terms_ref, f32[64,4096]{1,0:T(8,128)S(1)} %shard_map.45.begun_ref, f32[1056,128]{1,0:T(8,128)S(1)} %shard_map.46.sent_ref), custom_call_target="tpu_custom_call" | custom-call | flops 201326592 | bytes 1572864 | tf_op jit(solution)/shard_map/pallas_call | solution.py:206
  33.8 0.9 %collective-permute-done.7 = f32[1056,128]{1,0:T(8,128)S(1)} collective-permute-done((f32[1056,128]{1,0:T(8,128)S(1)}, f32[1056,128]{1,0:T(8,128)S(1)}, u32[]{:S(2)}, u32[]{:S(2)}) %collective-permute-start.7) | collective-permute-done | bytes 540704 | tf_op jit(solution)/shard_map/ppermute | solution.py:374
  34.6 0.1 add.37
  34.8 3.0 %collective-permute-start.10 = (f32[288,128]{1,0:T(8,128)S(1)}, f32[288,128]{1,0:T(8,128)S(1)}, u32[]{:S(2)}, u32[]{:S(2)}) collective-permute-start(f32[288,128]{1,0:T(8,128)S(1)} %concatenate.20), channel_id=1, source_target_pairs={{0,128},{8,40},{16,144},{24,56},{32,160},{40,8},{48,176},{56,24},{... | collective-permute-start | bytes 442376 | tf_op jit(solution)/shard_map/ppermute | solution.py:374
  37.8 0.9 %collective-permute-start.8 = (f32[288,128]{1,0:T(8,128)S(1)}, f32[288,128]{1,0:T(8,128)S(1)}, u32[]{:S(2)}, u32[]{:S(2)}) collective-permute-start(f32[288,128]{1,0:T(8,128)S(1)} %get-tuple-element.25), channel_id=1, source_target_pairs={{0,192},{8,56},{16,208},{24,40},{32,224},{40,24},{48,240},{56,8},{... | collective-permute-start | bytes 442376 | tf_op jit(solution)/shard_map/ppermute | solution.py:374
  38.7 0.0 collective-permute-start.9
  38.7 2.0 %collective-permute-done.10 = f32[288,128]{1,0:T(8,128)S(1)} collective-permute-done((f32[288,128]{1,0:T(8,128)S(1)}, f32[288,128]{1,0:T(8,128)S(1)}, u32[]{:S(2)}, u32[]{:S(2)}) %collective-permute-start.10) | collective-permute-done | bytes 147488 | tf_op jit(solution)/shard_map/ppermute | solution.py:374
  40.7 2.7 %collective-permute-done.8 = f32[288,128]{1,0:T(8,128)S(1)} collective-permute-done((f32[288,128]{1,0:T(8,128)S(1)}, f32[288,128]{1,0:T(8,128)S(1)}, u32[]{:S(2)}, u32[]{:S(2)}) %collective-permute-start.8) | collective-permute-done | bytes 147488 | tf_op jit(solution)/shard_map/ppermute | solution.py:374
  43.4 0.0 collective-permute-done.9
  43.4 2.5 %collective-permute-start.13 = (f32[288,128]{1,0:T(8,128)S(1)}, f32[288,128]{1,0:T(8,128)S(1)}, u32[]{:S(2)}, u32[]{:S(2)}) collective-permute-start(f32[288,128]{1,0:T(8,128)S(1)} %fusion.2), channel_id=1, source_target_pairs={{0,32},{8,136},{16,48},{24,152},{32,0},{40,168},{48,16},{56,184},{... | collective-permute-start | bytes 442376 | tf_op jit(solution)/shard_map/ppermute | solution.py:374
  46.0 0.8 %collective-permute-start.12 = (f32[288,128]{1,0:T(8,128)S(1)}, f32[288,128]{1,0:T(8,128)S(1)}, u32[]{:S(2)}, u32[]{:S(2)}) collective-permute-start(f32[288,128]{1,0:T(8,128)S(1)} %fusion.2), channel_id=1, source_target_pairs={{0,48},{8,200},{16,32},{24,216},{32,16},{40,232},{48,0},{56,248},{... | collective-permute-start | bytes 442376 | tf_op jit(solution)/shard_map/ppermute | solution.py:374
  46.8 0.0 collective-permute-start.11
  46.8 2.2 %collective-permute-done.13 = f32[288,128]{1,0:T(8,128)S(1)} collective-permute-done((f32[288,128]{1,0:T(8,128)S(1)}, f32[288,128]{1,0:T(8,128)S(1)}, u32[]{:S(2)}, u32[]{:S(2)}) %collective-permute-start.13) | collective-permute-done | bytes 147488 | tf_op jit(solution)/shard_map/ppermute | solution.py:374
  49.0 2.2 %collective-permute-done.12 = f32[288,128]{1,0:T(8,128)S(1)} collective-permute-done((f32[288,128]{1,0:T(8,128)S(1)}, f32[288,128]{1,0:T(8,128)S(1)}, u32[]{:S(2)}, u32[]{:S(2)}) %collective-permute-start.12) | collective-permute-done | bytes 147488 | tf_op jit(solution)/shard_map/ppermute | solution.py:374
  51.2 0.0 collective-permute-done.11
  51.2 2.1 %collective-permute-start.16 = (f32[256,128]{1,0:T(8,128)S(1)}, f32[256,128]{1,0:T(8,128)S(1)}, u32[]{:S(2)}, u32[]{:S(2)}) collective-permute-start(f32[256,128]{1,0:T(8,128)S(1)} %slice.30), channel_id=1, source_target_pairs={{0,192},{8,56},{16,208},{24,40},{32,224},{40,24},{48,240},{56,8},{... | collective-permute-start | bytes 393224 | tf_op jit(solution)/shard_map/ppermute | solution.py:374
  53.4 0.5 collective-permute-start.15
  53.9 0.7 %collective-permute-start.14 = (f32[256,128]{1,0:T(8,128)S(1)}, f32[256,128]{1,0:T(8,128)S(1)}, u32[]{:S(2)}, u32[]{:S(2)}) collective-permute-start(f32[256,128]{1,0:T(8,128)S(1)} %slice.30), channel_id=1, source_target_pairs={{0,64},{8,24},{16,80},{24,8},{32,96},{40,56},{48,112},{56,40},{64,... | collective-permute-start | bytes 393224 | tf_op jit(solution)/shard_map/ppermute | solution.py:374
  54.6 2.8 %shard_map.48.inverse_ref = f32[64,64]{1,0:T(8,128)S(1)} custom-call(f32[32,128]{1,0:T(8,128)S(1)} %slice.31.gram_ref), custom_call_target="tpu_custom_call" | custom-call | flops 26214400 | bytes 32768 | tf_op jit(solution)/shard_map/pallas_call | solution.py:298
  57.4 1.3 %shard_map.49 = f32[64,768]{1,0:T(8,128)} custom-call(f32[64,64]{1,0:T(8,128)S(1)} %shard_map.48.inverse_ref, f32[96,128]{1,0:T(8,128)S(1)} %add.36.sample_ref.s0, f32[96,128]{1,0:T(8,128)S(1)} %collective-permute-done.6.sample_ref.s3, f32[96,128]{1,0:T(8,128)S(1)} %collective-permute-done.5.sample_ref.s2, f32[96,128]{1,0:T(8,128)S(1)} %collective-permute-done.4.s1.sample_ref), custom_call_target="tpu_custom_call" | custom-call | flops 37748736 | bytes 393216 | tf_op jit(solution)/shard_map/pallas_call | solution.py:325
  58.7 0.0 collective-permute-done.16
  58.7 0.0 collective-permute-done.15
  58.7 0.0 collective-permute-done.14
  58.8 4.4 %collective-permute-start.17 = (f32[1024,128]{1,0:T(8,128)S(1)}, f32[1024,128]{1,0:T(8,128)S(1)}, u32[]{:S(2)}, u32[]{:S(2)}) collective-permute-start(f32[1024,128]{1,0:T(8,128)S(1)} %pad_maximum_fusion.value_ref), channel_id=1, source_target_pairs={{0,8},{8,0},{16,24},{24,16},{32,40},{40,32},{48,56},{56,48},{64,72... | collective-permute-start | bytes 1572872 | tf_op jit(solution)/shard_map/ppermute | solution.py:374
  63.2 1.0 %shard_map.50.refs_0_ = f32[64,4096]{1,0:T(8,128)} custom-call(f32[64,64]{1,0:T(8,128)S(1)} %shard_map.48.inverse_ref, f32[1024,128]{1,0:T(8,128)S(1)} %pad_maximum_fusion.value_ref), custom_call_target="tpu_custom_call" | custom-call | flops 50331648 | bytes 1048576 | tf_op jit(solution)/shard_map/pallas_call | solution.py:357
  64.2 0.5 collective-permute-done.17.value_ref
  64.7 1.0 %shard_map.51 = f32[64,4096]{1,0:T(8,128)} custom-call(f32[64,64]{1,0:T(8,128)S(1)} %shard_map.48.inverse_ref, f32[1024,128]{1,0:T(8,128)S(1)} %collective-permute-done.17.value_ref, f32[64,4096]{1,0:T(8,128)} %shard_map.50.refs_0_), custom_call_target="tpu_custom_call", output_to_operand_aliasing={{}: (2, {})} | custom-call | flops 50331648 | bytes 1048576 | tf_op jit(solution)/shard_map/pallas_call | solution.py:357
  (11 shorter events, 0.2 us)
Async XLA Ops:
  6.3 8.4 %collective-permute-start = (f32[96,128]{1,0:T(8,128)S(1)}, f32[96,128]{1,0:T(8,128)S(1)}, u32[]{:S(2)}, u32[]{:S(2)}) collective-permute-start(f32[96,128]{1,0:T(8,128)S(1)} %get-tuple-element.14), channel_id=1, source_target_pairs={{0,3},{1,2},{2,1},{3,0},{4,7},{5,6},{6,5},{7,4},{8,11},{9,10},{10,... | collective-permute-start | bytes 147464 | tf_op jit(solution)/shard_map/ppermute | solution.py:370
  11.6 4.5 %collective-permute-start.1 = (f32[96,128]{1,0:T(8,128)S(1)}, f32[96,128]{1,0:T(8,128)S(1)}, u32[]{:S(2)}, u32[]{:S(2)}) collective-permute-start(f32[96,128]{1,0:T(8,128)S(1)} %get-tuple-element.15), channel_id=1, source_target_pairs={{0,2},{1,3},{2,0},{3,1},{4,6},{5,7},{6,4},{7,5},{8,10},{9,11},{10,... | collective-permute-start | bytes 147464 | tf_op jit(solution)/shard_map/ppermute | solution.py:370
  11.6 4.5 %collective-permute-start.2 = (f32[96,128]{1,0:T(8,128)S(1)}, f32[96,128]{1,0:T(8,128)S(1)}, u32[]{:S(2)}, u32[]{:S(2)}) collective-permute-start(f32[96,128]{1,0:T(8,128)S(1)} %get-tuple-element.16), channel_id=1, source_target_pairs={{0,1},{1,0},{2,3},{3,2},{4,5},{5,4},{6,7},{7,6},{8,9},{9,8},{10,11... | collective-permute-start | bytes 147464 | tf_op jit(solution)/shard_map/ppermute | solution.py:370
  16.1 6.1 %collective-permute-start.3 = (f32[96,128]{1,0:T(8,128)S(1)}, f32[96,128]{1,0:T(8,128)S(1)}, u32[]{:S(2)}, u32[]{:S(2)}) collective-permute-start(f32[96,128]{1,0:T(8,128)S(1)} %add_add_fusion.1), channel_id=1, source_target_pairs={{0,7},{1,6},{2,5},{3,4},{4,3},{5,2},{6,1},{7,0},{8,15},{9,14},{10,... | collective-permute-start | bytes 147464 | tf_op jit(solution)/shard_map/ppermute | solution.py:370
  22.2 4.8 %collective-permute-start.6 = (f32[96,128]{1,0:T(8,128)S(1)}, f32[96,128]{1,0:T(8,128)S(1)}, u32[]{:S(2)}, u32[]{:S(2)}) collective-permute-start(f32[96,128]{1,0:T(8,128)S(1)} %add.36.sample_ref.s0), channel_id=1, source_target_pairs={{0,3},{1,2},{2,1},{3,0},{4,7},{5,6},{6,5},{7,4},{8,11},{9,10},{10,... | collective-permute-start | bytes 147464 | tf_op jit(solution)/shard_map/ppermute | solution.py:370
  23.9 4.4 %collective-permute-start.5 = (f32[96,128]{1,0:T(8,128)S(1)}, f32[96,128]{1,0:T(8,128)S(1)}, u32[]{:S(2)}, u32[]{:S(2)}) collective-permute-start(f32[96,128]{1,0:T(8,128)S(1)} %add.36.sample_ref.s0), channel_id=1, source_target_pairs={{0,2},{1,3},{2,0},{3,1},{4,6},{5,7},{6,4},{7,5},{8,10},{9,11},{10,... | collective-permute-start | bytes 147464 | tf_op jit(solution)/shard_map/ppermute | solution.py:370
  23.9 5.3 %collective-permute-start.4 = (f32[96,128]{1,0:T(8,128)S(1)}, f32[96,128]{1,0:T(8,128)S(1)}, u32[]{:S(2)}, u32[]{:S(2)}) collective-permute-start(f32[96,128]{1,0:T(8,128)S(1)} %add.36.sample_ref.s0), channel_id=1, source_target_pairs={{0,1},{1,0},{2,3},{3,2},{4,5},{5,4},{6,7},{7,6},{8,9},{9,8},{10,11... | collective-permute-start | bytes 147464 | tf_op jit(solution)/shard_map/ppermute | solution.py:370
  30.0 4.6 %collective-permute-start.7 = (f32[1056,128]{1,0:T(8,128)S(1)}, f32[1056,128]{1,0:T(8,128)S(1)}, u32[]{:S(2)}, u32[]{:S(2)}) collective-permute-start(f32[1056,128]{1,0:T(8,128)S(1)} %shard_map.46.sent_ref), channel_id=1, source_target_pairs={{0,8},{8,0},{16,24},{24,16},{32,40},{40,32},{48,56},{56,48},{64,72... | collective-permute-start | bytes 1622024 | tf_op jit(solution)/shard_map/ppermute | solution.py:374
  34.8 5.9 %collective-permute-start.10 = (f32[288,128]{1,0:T(8,128)S(1)}, f32[288,128]{1,0:T(8,128)S(1)}, u32[]{:S(2)}, u32[]{:S(2)}) collective-permute-start(f32[288,128]{1,0:T(8,128)S(1)} %concatenate.20), channel_id=1, source_target_pairs={{0,128},{8,40},{16,144},{24,56},{32,160},{40,8},{48,176},{56,24},{... | collective-permute-start | bytes 442376 | tf_op jit(solution)/shard_map/ppermute | solution.py:374
  37.8 5.6 %collective-permute-start.8 = (f32[288,128]{1,0:T(8,128)S(1)}, f32[288,128]{1,0:T(8,128)S(1)}, u32[]{:S(2)}, u32[]{:S(2)}) collective-permute-start(f32[288,128]{1,0:T(8,128)S(1)} %get-tuple-element.25), channel_id=1, source_target_pairs={{0,192},{8,56},{16,208},{24,40},{32,224},{40,24},{48,240},{56,8},{... | collective-permute-start | bytes 442376 | tf_op jit(solution)/shard_map/ppermute | solution.py:374
  38.7 4.7 %collective-permute-start.9 = (f32[288,128]{1,0:T(8,128)S(1)}, f32[288,128]{1,0:T(8,128)S(1)}, u32[]{:S(2)}, u32[]{:S(2)}) collective-permute-start(f32[288,128]{1,0:T(8,128)S(1)} %get-tuple-element.26), channel_id=1, source_target_pairs={{0,64},{8,24},{16,80},{24,8},{32,96},{40,56},{48,112},{56,40},{64,... | collective-permute-start | bytes 442376 | tf_op jit(solution)/shard_map/ppermute | solution.py:374
  43.4 5.6 %collective-permute-start.13 = (f32[288,128]{1,0:T(8,128)S(1)}, f32[288,128]{1,0:T(8,128)S(1)}, u32[]{:S(2)}, u32[]{:S(2)}) collective-permute-start(f32[288,128]{1,0:T(8,128)S(1)} %fusion.2), channel_id=1, source_target_pairs={{0,32},{8,136},{16,48},{24,152},{32,0},{40,168},{48,16},{56,184},{... | collective-permute-start | bytes 442376 | tf_op jit(solution)/shard_map/ppermute | solution.py:374
  46.0 5.2 %collective-permute-start.12 = (f32[288,128]{1,0:T(8,128)S(1)}, f32[288,128]{1,0:T(8,128)S(1)}, u32[]{:S(2)}, u32[]{:S(2)}) collective-permute-start(f32[288,128]{1,0:T(8,128)S(1)} %fusion.2), channel_id=1, source_target_pairs={{0,48},{8,200},{16,32},{24,216},{32,16},{40,232},{48,0},{56,248},{... | collective-permute-start | bytes 442376 | tf_op jit(solution)/shard_map/ppermute | solution.py:374
  46.8 4.4 %collective-permute-start.11 = (f32[288,128]{1,0:T(8,128)S(1)}, f32[288,128]{1,0:T(8,128)S(1)}, u32[]{:S(2)}, u32[]{:S(2)}) collective-permute-start(f32[288,128]{1,0:T(8,128)S(1)} %fusion.2), channel_id=1, source_target_pairs={{0,16},{8,72},{16,0},{24,88},{32,48},{40,104},{48,32},{56,120},{64... | collective-permute-start | bytes 442376 | tf_op jit(solution)/shard_map/ppermute | solution.py:374
  51.2 7.5 %collective-permute-start.16 = (f32[256,128]{1,0:T(8,128)S(1)}, f32[256,128]{1,0:T(8,128)S(1)}, u32[]{:S(2)}, u32[]{:S(2)}) collective-permute-start(f32[256,128]{1,0:T(8,128)S(1)} %slice.30), channel_id=1, source_target_pairs={{0,192},{8,56},{16,208},{24,40},{32,224},{40,24},{48,240},{56,8},{... | collective-permute-start | bytes 393224 | tf_op jit(solution)/shard_map/ppermute | solution.py:374
  53.4 5.4 %collective-permute-start.15 = (f32[256,128]{1,0:T(8,128)S(1)}, f32[256,128]{1,0:T(8,128)S(1)}, u32[]{:S(2)}, u32[]{:S(2)}) collective-permute-start(f32[256,128]{1,0:T(8,128)S(1)} %slice.30), channel_id=1, source_target_pairs={{0,128},{8,40},{16,144},{24,56},{32,160},{40,8},{48,176},{56,24},{... | collective-permute-start | bytes 393224 | tf_op jit(solution)/shard_map/ppermute | solution.py:374
  53.9 4.9 %collective-permute-start.14 = (f32[256,128]{1,0:T(8,128)S(1)}, f32[256,128]{1,0:T(8,128)S(1)}, u32[]{:S(2)}, u32[]{:S(2)}) collective-permute-start(f32[256,128]{1,0:T(8,128)S(1)} %slice.30), channel_id=1, source_target_pairs={{0,64},{8,24},{16,80},{24,8},{32,96},{40,56},{48,112},{56,40},{64,... | collective-permute-start | bytes 393224 | tf_op jit(solution)/shard_map/ppermute | solution.py:374
  58.8 5.9 %collective-permute-start.17 = (f32[1024,128]{1,0:T(8,128)S(1)}, f32[1024,128]{1,0:T(8,128)S(1)}, u32[]{:S(2)}, u32[]{:S(2)}) collective-permute-start(f32[1024,128]{1,0:T(8,128)S(1)} %pad_maximum_fusion.value_ref), channel_id=1, source_target_pairs={{0,8},{8,0},{16,24},{24,16},{32,40},{40,32},{48,56},{56,48},{64,72... | collective-permute-start | bytes 1572872 | tf_op jit(solution)/shard_map/ppermute | solution.py:374
